TPU v7x, 32 devices: a whole 2x2x4 slice. The times are simulated.
32 devices in a mesh: kern: 4 (over y, x), tile: 8 (over z, core).
Axes of the slice: x: 2, y: 2, z: 4, core: 2. Of those that a mesh axis runs over, the one named last changes fastest.
Arguments:
- diag_tiles: float32 [4, 8, 512, 512], P('kern', 'tile'), may hold values from -0.25 to 0.25
- left_factors: float32 [4, 8, 8, 80, 512], P('kern', 'tile'), may hold values from -0.25 to 0.25
- right_factors: float32 [4, 8, 12, 80, 512], P('kern', 'tile'), may hold values from -0.25 to 0.25
- tile_offsets: int32 [4, 8, 8], P('kern', 'tile'), may hold values from -6 to 6, as said below
- tile_ranks: int32 [4, 8, 8], P('kern', 'tile'), may hold values from 32 to 80
- mixing: float32 [64, 4, 4], replicated, may hold values from -3 to 3
- block_index: int32 [4096], P('tile'), may hold values from 0 to 63
- rhs_field: float32 [4, 4096, 128], P('kern', 'tile'), may hold values from -6 to 6
Outputs:
- product: float32 [4, 4096, 128], P('kern', 'tile')
Inputs may be any that keep to these rules, and one draw needn't show every extreme that they name: `tile_offsets`: each row's 8 offsets are distinct and nonzero.
All inputs are finite; a program needn't handle non-finite values.
Results may differ from a plain program's by a relative error of at most 0.00007.
Values sent between devices are 32-bit elements; how exact they have to be, the bound alone decides.
No kernel may reach another device: no remote copies, remote signals or barrier semaphores. Data moves between devices by JAX's collectives and lax.ppermute only.
A program may use at most 64 MiB of HBM per device.

v0:
```python
import functools

import jax
import jax.numpy as jnp
from jax import lax
from jax.experimental import pallas as pl
from jax.experimental.pallas import tpu as pltpu
from jax.sharding import PartitionSpec as P

f32 = jnp.float32
bf16 = jnp.bfloat16
VMEM_BYTES = 24 * 1024 * 1024
in_vmem = pl.BlockSpec(memory_space=pltpu.VMEM)
in_smem = pl.BlockSpec(memory_space=pltpu.SMEM)
in_hbm = pl.BlockSpec(memory_space=pltpu.HBM)
in_any = pl.BlockSpec(memory_space=pl.ANY)


def to_hbm(value):
    return pltpu.with_memory_space_constraint(value, pltpu.HBM)


def struct(*shape, dtype=f32):
    return jax.ShapeDtypeStruct(shape, dtype)


def split(value):
    hi = value.astype(bf16)
    return hi, (value - hi.astype(f32)).astype(bf16)


def side_by_side(value):
    return jnp.concatenate(split(value), axis=1)


def dot(left, right):
    return jnp.dot(left, right, preferred_element_type=f32)


def fold(value):
    width = value.shape[1] // 2
    return value[:, :width] + value[:, width:]


def call(kernel, outs, out_specs, in_specs, scratch=(), flops=0, moved=0):
    return pl.pallas_call(
        kernel,
        out_shape=outs,
        in_specs=in_specs,
        out_specs=out_specs,
        scratch_shapes=list(scratch),
        compiler_params=pltpu.CompilerParams(vmem_limit_bytes=VMEM_BYTES),
        cost_estimate=pl.CostEstimate(flops=flops, bytes_accessed=moved, transcendentals=0),
    )


class Message:
    def __init__(self, pairs, slots, odd_slots=None):
        self.pairs = pairs
        self.slots = slots
        self.odd_slots = odd_slots
        self.width = len(slots)
        half = len(pairs) // 2
        self.across = self.width * sum((a < half) != (b < half) for a, b in pairs)


def messages_of(count, slots, per):
    reach = slots // 2
    groups = {}
    for slot in range(slots):
        offset = slot - reach if slot < reach else slot - reach + 1
        groups.setdefault(offset % count, []).append(slot)
    messages = []
    below, above = reach - 1, reach
    single = groups.get(1) == [above] and groups.get(count - 1) == [below]
    if single and count % 2 == 0 and below // per == above // per:
        del groups[1], groups[count - 1]
        for turn, (even, odd) in enumerate(((below, above), (above, below))):
            pairs = [(at, (at + (1, -1)[(at + turn) % 2]) % count) for at in range(count)]
            messages.append(Message(pairs, [even], [odd]))
    for ahead, group in groups.items():
        messages.append(Message([(at, (at - ahead) % count) for at in range(count)], group))
    return sorted(messages, key=lambda message: -message.across)


def store_coefficients(got, chunk, per, messages, rank, outs):
    size = per * rank
    got = got[:size] + got[size:]

    def piece(slot):
        row = (slot - chunk * per) * rank
        return got[row : row + rank]

    odd = jnp.full((rank, got.shape[1]), lax.axis_index("tile") & 1, jnp.int32) == 1
    for message, out in zip(messages, outs):
        for w, slot in enumerate(message.slots):
            if slot // per == chunk:
                value = piece(slot)
                if message.odd_slots is not None:
                    value = jnp.where(odd, piece(message.odd_slots[w]), value)
                out[w] = value


def first_coeff_kernel(messages, per, cols_ref, right_ref, *refs):
    outs, (split_ref, cols, right, sems) = refs[: len(messages)], refs[len(messages) :]
    slots, rank, size = right.shape
    chunks = slots // per
    cols_copy = pltpu.make_async_copy(cols_ref, cols, sems.at[chunks])
    cols_copy.start()
    copies = []
    for chunk in range(chunks):
        span = pl.ds(chunk * per, per)
        copies.append(pltpu.make_async_copy(right_ref.at[span], right.at[span], sems.at[chunk]))
        copies[-1].start()
    cols_copy.wait()
    both = side_by_side(cols[...])
    for chunk in range(chunks):
        copies[chunk].wait()
        hi, lo = split(right[pl.ds(chunk * per, per)].reshape(per * rank, size))
        base = 2 * chunk * per * rank
        split_ref[pl.ds(base, per * rank)] = hi
        split_ref[pl.ds(base + per * rank, per * rank)] = lo
        got = fold(dot(split_ref[pl.ds(base, 2 * per * rank)], both))
        store_coefficients(got, chunk, per, messages, rank, outs)


def first_coefficients(cols, right_tile, messages, per):
    slots, rank, size = right_tile.shape
    width = cols.shape[1]
    outs = [struct(message.width, rank, width) for message in messages]
    outs.append(struct(2 * slots * rank, size, dtype=bf16))
    got = call(
        functools.partial(first_coeff_kernel, messages, per),
        outs,
        [in_vmem] * len(outs),
        [in_hbm, in_hbm],
        [
            pltpu.VMEM(cols.shape, f32),
            pltpu.VMEM(right_tile.shape, f32),
            pltpu.SemaphoreType.DMA((slots // per + 1,)),
        ],
        flops=8 * slots * rank * size * width,
        moved=4 * slots * rank * (2 * size + width),
    )(to_hbm(cols), to_hbm(right_tile))
    return got[:-1], got[-1]


def halve_kernel(base, own_ref, got_ref, weights_ref, keep_ref, send_ref):
    own, got = own_ref[...], got_ref[...]
    keep_ref[...] = own * weights_ref[base] + got * weights_ref[base + 1]
    send_ref[...] = own * weights_ref[base + 2] + got * weights_ref[base + 3]


def halve(own, got, weights, half):
    part, width = own.shape
    return call(
        functools.partial(halve_kernel, 4 * half),
        [struct(part, width)] * 2,
        [in_vmem] * 2,
        [in_vmem] * 3,
        flops=6 * part * width,
        moved=32 * part * width,
    )(own, got, weights)


def mix(first, weights):
    groups = lax.axis_size("kern")
    if groups != 4:
        fields = [lax.all_gather(part, "kern") for part in first]
        mixed = jnp.sum(jnp.concatenate(fields, axis=1) * weights, axis=0)
        return [(mixed, jnp.zeros_like(mixed))]
    count = lax.axis_size("tile")
    steps = ([], [])
    for group in range(groups):
        for tile in range(count):
            for turn, pairs in enumerate(steps):
                dest = group ^ (1 + (turn + tile) % 2)
                pairs.append((group * count + tile, dest * count + tile))
    axes = ("kern", "tile")
    came = [lax.ppermute(part, axes, pairs) for part, pairs in zip(first, steps)]
    sums = [
        halve(part, got, weights, half)
        for half, (part, got) in enumerate(zip(first, came))
    ]
    return [
        (keep, lax.ppermute(send, axes, pairs)) for (keep, send), pairs in zip(sums, steps[::-1])
    ]


def mixed_coeff_kernel(messages, per, terms, *refs):
    fields, split_ref, outs, cols_ref = refs[:terms], refs[terms], refs[terms + 1 : -1], refs[-1]
    part = fields[0].shape[0]
    for at in range(0, terms, 2):
        total = fields[at][...] + fields[at + 1][...]
        cols_ref[pl.ds(at // 2 * part, part)] = total
    both = side_by_side(cols_ref[...])
    rank = outs[0].shape[1]
    got = fold(dot(split_ref[...], both))
    size = 2 * per * rank
    for chunk in range(split_ref.shape[0] // size):
        here = got[chunk * size : (chunk + 1) * size]
        store_coefficients(here, chunk, per, messages, rank, outs)


def mixed_coefficients(mixed, split_right, messages, per, rank):
    flat = [term for pair in mixed for term in pair]
    part, width = flat[0].shape
    size = part * len(mixed)
    total = split_right.shape[0]
    outs = [struct(message.width, rank, width) for message in messages]
    outs.append(struct(size, width))
    got = call(
        functools.partial(mixed_coeff_kernel, messages, per, len(flat)),
        outs,
        [in_vmem] * len(outs),
        [in_vmem] * (len(flat) + 1),
        flops=4 * total * size * width,
        moved=2 * total * (size + width),
    )(*flat, split_right)
    return got[:-1], got[-1]


def times_diag(diag_ref, cols_ref):
    both = side_by_side(cols_ref[...])
    hi, lo = split(diag_ref[...])
    return fold(dot(hi, both) + dot(lo, both))


def relay_kernel(count, *refs):
    for source, target in zip(refs[:count], refs[-count:]):
        target[...] = source[...]


def relay(values, after):
    return call(
        functools.partial(relay_kernel, len(values)),
        [struct(*value.shape) for value in values],
        [in_vmem] * len(values),
        [in_vmem] * len(values) + [in_any] * len(after),
        moved=8 * sum(value.size for value in values),
    )(*values, *after)


def diag_kernel(diag_ref, cols_ref, out_ref):
    out_ref[...] = times_diag(diag_ref, cols_ref)


def diagonal(diag_tile, cols):
    size, width = cols.shape
    return call(
        diag_kernel,
        struct(size, width),
        in_vmem,
        [in_vmem, in_vmem],
        flops=8 * size * size * width,
        moved=4 * size * (size + 2 * width),
    )(diag_tile, cols)


def weight_rows(size):
    groups = lax.axis_size("kern")
    me = lax.axis_index("kern")
    if groups != 4:
        return [(me * groups + b, slice(0, size)) for b in range(groups)]
    rows_of = []
    odd = lax.axis_index("tile") & 1
    one, two = me ^ (1 + odd), me ^ (2 - odd)
    for half, (first, second) in enumerate(((one, two), (two, one))):
        lanes = slice(half * (size // 2), (half + 1) * (size // 2))
        for a in (me, second):
            for b in (me, first):
                rows_of.append((a * groups + b, lanes))
    return rows_of


def prepare_kernel(
    halves, diag_hbm, cols_hbm, left_hbm, table_ref, index_ref,
    diag_out, left_out, weights_ref, diag_ref, cols_ref, left_ref, full_ref, sems,
):
    copies = []
    for at, (source, target) in enumerate(
        ((diag_hbm, diag_ref), (cols_hbm, cols_ref), (left_hbm, left_ref))
    ):
        copies.append(pltpu.make_async_copy(source, target, sems.at[at]))
        copies[-1].start()
    entries = table_ref.shape[1]
    size = index_ref.shape[1]
    hot = (lax.broadcasted_iota(jnp.int32, (entries, size), 0) == index_ref[...]).astype(f32)
    full_ref[...] = jnp.dot(
        table_ref[...], hot, precision=lax.Precision.HIGHEST, preferred_element_type=f32
    )
    width = weights_ref.shape[2]
    for at, (row, lanes) in enumerate(weight_rows(size)):
        piece = full_ref[pl.ds(row, 1), lanes]
        weights_ref[at] = jnp.broadcast_to(piece, (width, piece.shape[1])).T
    copies[0].wait()
    copies[1].wait()
    diag_out[...] = times_diag(diag_ref, cols_ref)
    copies[2].wait()
    total = left_ref.shape[0]
    step = 128 if total % 128 == 0 else total
    part = size // halves
    for at in range(0, total, step):
        span = slice(at, at + step)
        hi, lo = split(left_ref[span].T)
        for half in range(halves):
            base = 2 * half * part
            rows_of = slice(half * part, (half + 1) * part)
            left_out[base : base + part, span] = hi[rows_of]
            left_out[base + part : base + 2 * part, span] = lo[rows_of]


def prepare(diag_tile, cols, left_rows, table, index, halves):
    size, width = cols.shape
    total = left_rows.shape[0]
    weights = weight_rows(size)
    part = weights[0][1].stop
    return call(
        functools.partial(prepare_kernel, halves),
        [
            struct(size, width),
            struct(2 * size, total, dtype=bf16),
            struct(len(weights), part, width),
        ],
        [in_vmem] * 3,
        [in_hbm] * 3 + [in_vmem] * 2,
        [
            pltpu.VMEM(diag_tile.shape, f32),
            pltpu.VMEM(cols.shape, f32),
            pltpu.VMEM(left_rows.shape, f32),
            pltpu.VMEM((table.shape[0], size), f32),
            pltpu.SemaphoreType.DMA((3,)),
        ],
        flops=8 * size * size * width,
        moved=8 * total * size + 4 * size * (size + 2 * width),
    )(to_hbm(diag_tile), to_hbm(cols), to_hbm(left_rows), table, index)


def row_kernel(messages, halves, final, offs_ref, ranks_ref, *refs):
    gots = refs[: len(messages)]
    left_ref, diag_ref = refs[len(messages) : len(messages) + 2]
    outs = refs[len(messages) + 2 :]
    if final:
        outs, (picked, term_of, stage, sems) = outs[:-4], outs[-4:]
    else:
        outs, (picked, term_of) = outs[:-2], outs[-2:]
    terms = offs_ref.shape[1]
    rank, width = gots[0].shape[1:]
    slots = term_of.shape[0]
    reach = slots // 2
    for slot in range(slots):
        term_of[slot] = -1
    for k in range(terms):
        offset = offs_ref[0, k]
        term_of[jnp.where(offset < 0, offset + reach, offset + reach - 1)] = k
    line = lax.broadcasted_iota(jnp.int32, (rank, width), 0)

    def pick(got, w, term):
        @pl.when(term >= 0)
        def _():
            kept = jnp.where(line < ranks_ref[0, term], got[w], 0.0)
            picked[pl.ds(pl.multiple_of(term * rank, rank), rank)] = kept

    for got, message in zip(gots, messages):
        for w, slot in enumerate(message.slots):
            if message.odd_slots is not None:
                slot = jnp.where((lax.axis_index("tile") & 1) == 1, slot, message.odd_slots[w])
            pick(got, w, term_of[slot])
    both = side_by_side(picked[...])
    part = diag_ref.shape[0] // halves
    sent = []
    got = fold(dot(left_ref[...], both))
    for half in range(halves):
        rows_of = pl.ds(half * part, part)
        base = 2 * half * part
        total = got[base : base + part] + got[base + part : base + 2 * part] + diag_ref[rows_of]
        if final:
            stage[rows_of] = total
            sent.append(
                pltpu.make_async_copy(stage.at[rows_of], outs[0].at[rows_of], sems.at[half])
            )
            sent[-1].start()
        else:
            outs[half][...] = total
    for copy in sent:
        copy.wait()


def rows(offsets, ranks, gots, messages, left_split, diag_part, slots, halves, final):
    size, width = diag_part.shape
    total = left_split.shape[1]
    scratch = [pltpu.VMEM((total, width), f32), pltpu.SMEM((slots,), jnp.int32)]
    if final:
        scratch += [pltpu.VMEM((size, width), f32), pltpu.SemaphoreType.DMA((halves,))]
    return call(
        functools.partial(row_kernel, messages, halves, final),
        pltpu.HBM((size, width), f32) if final else [struct(size // halves, width)] * halves,
        in_hbm if final else [in_vmem] * halves,
        [in_smem, in_smem] + [in_vmem] * (len(messages) + 2),
        scratch,
        flops=8 * total * size * width,
        moved=4 * total * (size + width),
    )(offsets, ranks, *gots, left_split, diag_part)


def deliver(coeffs, messages, beside=None):
    gots = {}
    small = [at for at, message in enumerate(messages) if message.width < messages[0].width]
    if beside is None:
        small = []
    for at, message in enumerate(messages):
        if at not in small:
            gots[at] = lax.ppermute(coeffs[at], "tile", message.pairs)
    if small:
        values = relay([coeffs[at] for at in small], [gots[0], beside])
        for at, value in zip(small, values):
            gots[at] = lax.ppermute(value, "tile", messages[at].pairs)
    return [gots[at] for at in range(len(messages))]


def local(
    diag_tiles,
    left_factors,
    right_factors,
    tile_offsets,
    tile_ranks,
    mixing,
    block_index,
    rhs_field,
):
    diag_tile = diag_tiles[0, 0]
    right_tile = right_factors[0, 0]
    offsets = tile_offsets[0]
    ranks = tile_ranks[0]
    slots, rank, size = right_tile.shape
    halves = 2 if size % 32 == 0 else 1
    left_rows = left_factors.reshape(-1, size)
    groups = lax.axis_size("kern")
    table = mixing.reshape(mixing.shape[0], groups * groups).T
    index = block_index[None]
    cols = rhs_field[0]

    per = 4 if slots % 4 == 0 else slots
    messages = messages_of(lax.axis_size("tile"), slots, per)
    coeffs, split_right = first_coefficients(cols, right_tile, messages, per)
    gots = deliver(coeffs, messages)
    diag_part, left_split, weights = prepare(diag_tile, cols, left_rows, table, index, halves)
    first = rows(offsets, ranks, gots, messages, left_split, diag_part, slots, halves, False)
    mixed = mix(first, weights)
    coeffs, cols = mixed_coefficients(mixed, split_right, messages, per, rank)
    diag_part = diagonal(diag_tile, cols)
    gots = deliver(coeffs, messages, diag_part)
    return rows(offsets, ranks, gots, messages, left_split, diag_part, slots, halves, True)[None]


def solution(mesh):
    in_specs = (
        P("kern", "tile", None, None),
        P("kern", "tile", None, None, None),
        P("kern", "tile", None, None, None),
        P("kern", "tile", None),
        P("kern", "tile", None),
        P(),
        P("tile"),
        P("kern", "tile", None),
    )
    out_specs = P("kern", "tile", None)
    return jax.shard_map(local, mesh=mesh, in_specs=in_specs, out_specs=out_specs, check_vma=False)
```

profile of v0, /device:TPU:0, one launch (start us, length us, event | category | flops | bytes accessed | tf_op | source)
XLA Modules:
  0.0 52.3 jit_solution(8802480869020762089)
XLA Ops:
  0.0 2.6 %shard_map.82 = (f32[2,80,128]{2,1,0:T(8,128)S(1)}, f32[2,80,128]{2,1,0:T(8,128)S(1)}, f32[2,80,128]{2,1,0:T(8,128)S(1)}, f32[2,80,128]{2,1,0:T(8,128)S(1)}, f32...) custom-call(f32[512,128]{1,0:T(8,128)} %bitcast.21, ...), custom_call_target="tpu_custom_call" | custom-call | flops 503316480 | bytes 4423680 | tf_op jit(solution)/shard_map/pallas_call | solution.py:132
  2.6 4.6 %collective-permute-start.5 = (f32[1,80,128]{2,1,0:T(8,128)S(1)}, f32[1,80,128]{2,1,0:T(8,128)S(1)}, u32[]{:S(2)}, u32[]{:S(2)}) collective-permute-start(f32[1,80,128]{2,1,0:T(8,128)S(1)} %get-tuple-element.37), channel_id=1, source_target_pairs={{0,7},{1,2},{2,1},{3,4},{4,3},{5,6},{6,5},{7,0},{8,15},{9,10},{10,... | collective-permute-start | bytes 122888 | tf_op jit(solution)/shard_map/ppermute | solution.py:413
  7.2 1.2 %collective-permute-start = (f32[2,80,128]{2,1,0:T(8,128)S(1)}, f32[2,80,128]{2,1,0:T(8,128)S(1)}, u32[]{:S(2)}, u32[]{:S(2)}) collective-permute-start(f32[2,80,128]{2,1,0:T(8,128)S(1)} %get-tuple-element.32), channel_id=1, source_target_pairs={{0,4},{1,5},{2,6},{3,7},{4,0},{5,1},{6,2},{7,3},{8,12},{9,13},{10,... | collective-permute-start | bytes 245768 | tf_op jit(solution)/shard_map/ppermute | solution.py:413
  8.4 1.5 %collective-permute-start.1 = (f32[2,80,128]{2,1,0:T(8,128)S(1)}, f32[2,80,128]{2,1,0:T(8,128)S(1)}, u32[]{:S(2)}, u32[]{:S(2)}) collective-permute-start(f32[2,80,128]{2,1,0:T(8,128)S(1)} %get-tuple-element.33), channel_id=1, source_target_pairs={{0,5},{1,6},{2,7},{3,0},{4,1},{5,2},{6,3},{7,4},{8,13},{9,14},{10,... | collective-permute-start | bytes 245768 | tf_op jit(solution)/shard_map/ppermute | solution.py:413
  10.2 3.1 %collective-permute-start.3 = (f32[2,80,128]{2,1,0:T(8,128)S(1)}, f32[2,80,128]{2,1,0:T(8,128)S(1)}, u32[]{:S(2)}, u32[]{:S(2)}) collective-permute-start(f32[2,80,128]{2,1,0:T(8,128)S(1)} %get-tuple-element.35), channel_id=1, source_target_pairs={{0,6},{1,7},{2,0},{3,1},{4,2},{5,3},{6,4},{7,5},{8,14},{9,15},{10,... | collective-permute-start | bytes 245768 | tf_op jit(solution)/shard_map/ppermute | solution.py:413
  13.3 2.2 %shard_map.83 = (f32[512,128]{1,0:T(8,128)S(1)}, bf16[1024,640]{1,0:T(8,128)(2,1)S(1)}, f32[8,256,128]{2,1,0:T(8,128)S(1)}) custom-call(f32[512,512]{1,0:T(8,128)} %bitcast.11, f32[512,128]{1,0:T(8,128)} %bitcast.22, f32[640,512]{1,0:T(8,128)} %bitcast.20, f32[16,64]{1,0:T(8,128)S(1)} %bitcast.13, s32[1,512]{1,0:T(1,128)S(1)} %bitcast.14), custom_call_target="tpu_custom_call" | custom-call | flops 268435456 | bytes 4194304 | tf_op jit(solution)/shard_map/pallas_call | solution.py:318
  15.5 1.1 %collective-permute-done.refs_0_ = f32[2,80,128]{2,1,0:T(8,128)S(1)} collective-permute-done((f32[2,80,128]{2,1,0:T(8,128)S(1)}, f32[2,80,128]{2,1,0:T(8,128)S(1)}, u32[]{:S(2)}, u32[]{:S(2)}) %collective-permute-start) | collective-permute-done | bytes 81952 | tf_op jit(solution)/shard_map/ppermute | solution.py:413
  16.6 5.1 %collective-permute-done.2.refs_2_ = f32[2,80,128]{2,1,0:T(8,128)S(1)} collective-permute-done((f32[2,80,128]{2,1,0:T(8,128)S(1)}, f32[2,80,128]{2,1,0:T(8,128)S(1)}, u32[]{:S(2)}, u32[]{:S(2)}) %collective-permute-start.2) | collective-permute-done | bytes 81952 | tf_op jit(solution)/shard_map/ppermute | solution.py:413
  21.7 1.3 %shard_map.84 = (f32[256,128]{1,0:T(8,128)S(1)}, f32[256,128]{1,0:T(8,128)S(1)}) custom-call(s32[1,8]{1,0:T(1,128)S(1)} %bitcast.15, s32[1,8]{1,0:T(1,128)S(1)} %bitcast.17, f32[2,80,128]{2,1,0:T(8,128)S(1)} %collective-permute-done.refs_0_, f32[2,80,128]{2,1,0:T(8,128)S(1)} %collective-permute-done.1.refs_1_, ...), custom_call_target="tpu_custom_call" | custom-call | flops 335544320 | bytes 1638400 | tf_op jit(solution)/shard_map/pallas_call | solution.py:395
  23.0 1.6 %collective-permute-start.7 = (f32[256,128]{1,0:T(8,128)S(1)}, f32[256,128]{1,0:T(8,128)S(1)}, u32[]{:S(2)}, u32[]{:S(2)}) collective-permute-start(f32[256,128]{1,0:T(8,128)S(1)} %get-tuple-element.41.own_ref), channel_id=1, source_target_pairs={{0,8},{1,17},{2,10},{3,19},{4,12},{5,21},{6,14},{7,23},{8,0},{9,25... | collective-permute-start | bytes 393224 | tf_op jit(solution)/shard_map/ppermute | solution.py:180
  24.6 1.5 %collective-permute-start.9 = (f32[256,128]{1,0:T(8,128)S(1)}, f32[256,128]{1,0:T(8,128)S(1)}, u32[]{:S(2)}, u32[]{:S(2)}) collective-permute-start(f32[256,128]{1,0:T(8,128)S(1)} %get-tuple-element.45.own_ref), channel_id=1, source_target_pairs={{0,16},{1,9},{2,18},{3,11},{4,20},{5,13},{6,22},{7,15},{8,24},{9,1... | collective-permute-start | bytes 393224 | tf_op jit(solution)/shard_map/ppermute | solution.py:180
  26.1 2.2 %collective-permute-done.7.got_ref = f32[256,128]{1,0:T(8,128)S(1)} collective-permute-done((f32[256,128]{1,0:T(8,128)S(1)}, f32[256,128]{1,0:T(8,128)S(1)}, u32[]{:S(2)}, u32[]{:S(2)}) %collective-permute-start.7) | collective-permute-done | bytes 131104 | tf_op jit(solution)/shard_map/ppermute | solution.py:180
  28.4 1.3 %collective-permute-start.8 = (f32[256,128]{1,0:T(8,128)S(1)}, f32[256,128]{1,0:T(8,128)S(1)}, u32[]{:S(2)}, u32[]{:S(2)}) collective-permute-start(f32[256,128]{1,0:T(8,128)S(1)} %get-tuple-element.44), channel_id=1, source_target_pairs={{0,16},{1,9},{2,18},{3,11},{4,20},{5,13},{6,22},{7,15},{8,24},{9,1... | collective-permute-start | bytes 393224 | tf_op jit(solution)/shard_map/ppermute | solution.py:186
  29.7 1.5 %collective-permute-start.10 = (f32[256,128]{1,0:T(8,128)S(1)}, f32[256,128]{1,0:T(8,128)S(1)}, u32[]{:S(2)}, u32[]{:S(2)}) collective-permute-start(f32[256,128]{1,0:T(8,128)S(1)} %get-tuple-element.47), channel_id=1, source_target_pairs={{0,8},{1,17},{2,10},{3,19},{4,12},{5,21},{6,14},{7,23},{8,0},{9,25... | collective-permute-start | bytes 393224 | tf_op jit(solution)/shard_map/ppermute | solution.py:186
  31.3 2.1 %collective-permute-done.8.refs_1_ = f32[256,128]{1,0:T(8,128)S(1)} collective-permute-done((f32[256,128]{1,0:T(8,128)S(1)}, f32[256,128]{1,0:T(8,128)S(1)}, u32[]{:S(2)}, u32[]{:S(2)}) %collective-permute-start.8) | collective-permute-done | bytes 131104 | tf_op jit(solution)/shard_map/ppermute | solution.py:186
  33.4 1.4 %collective-permute-done.10.refs_3_ = f32[256,128]{1,0:T(8,128)S(1)} collective-permute-done((f32[256,128]{1,0:T(8,128)S(1)}, f32[256,128]{1,0:T(8,128)S(1)}, u32[]{:S(2)}, u32[]{:S(2)}) %collective-permute-start.10) | collective-permute-done | bytes 131104 | tf_op jit(solution)/shard_map/ppermute | solution.py:186
  34.8 0.7 %shard_map.87 = (f32[2,80,128]{2,1,0:T(8,128)S(1)}, f32[2,80,128]{2,1,0:T(8,128)S(1)}, f32[2,80,128]{2,1,0:T(8,128)S(1)}, f32[2,80,128]{2,1,0:T(8,128)S(1)}, f32...) custom-call(f32[256,128]{1,0:T(8,128)S(1)} %get-tuple-element.43.refs_0_, ...), custom_call_target="tpu_custom_call" | custom-call | flops 503316480 | bytes 2457600 | tf_op jit(solution)/shard_map/pallas_call | solution.py:212
  35.5 2.0 %collective-permute-start.11 = (f32[2,80,128]{2,1,0:T(8,128)S(1)}, f32[2,80,128]{2,1,0:T(8,128)S(1)}, u32[]{:S(2)}, u32[]{:S(2)}) collective-permute-start(f32[2,80,128]{2,1,0:T(8,128)S(1)} %get-tuple-element.49), channel_id=1, source_target_pairs={{0,4},{1,5},{2,6},{3,7},{4,0},{5,1},{6,2},{7,3},{8,12},{9,13},{10,... | collective-permute-start | bytes 245768 | tf_op jit(solution)/shard_map/ppermute | solution.py:413
  37.5 1.7 %collective-permute-start.13 = (f32[2,80,128]{2,1,0:T(8,128)S(1)}, f32[2,80,128]{2,1,0:T(8,128)S(1)}, u32[]{:S(2)}, u32[]{:S(2)}) collective-permute-start(f32[2,80,128]{2,1,0:T(8,128)S(1)} %get-tuple-element.51), channel_id=1, source_target_pairs={{0,3},{1,4},{2,5},{3,6},{4,7},{5,0},{6,1},{7,2},{8,11},{9,12},{10,... | collective-permute-start | bytes 245768 | tf_op jit(solution)/shard_map/ppermute | solution.py:413
  39.2 4.2 %collective-permute-start.14 = (f32[2,80,128]{2,1,0:T(8,128)S(1)}, f32[2,80,128]{2,1,0:T(8,128)S(1)}, u32[]{:S(2)}, u32[]{:S(2)}) collective-permute-start(f32[2,80,128]{2,1,0:T(8,128)S(1)} %get-tuple-element.52), channel_id=1, source_target_pairs={{0,6},{1,7},{2,0},{3,1},{4,2},{5,3},{6,4},{7,5},{8,14},{9,15},{10,... | collective-permute-start | bytes 245768 | tf_op jit(solution)/shard_map/ppermute | solution.py:413
  43.9 0.8 %collective-permute-done.11.refs_2_.refs_0_ = f32[2,80,128]{2,1,0:T(8,128)S(1)} collective-permute-done((f32[2,80,128]{2,1,0:T(8,128)S(1)}, f32[2,80,128]{2,1,0:T(8,128)S(1)}, u32[]{:S(2)}, u32[]{:S(2)}) %collective-permute-start.11) | collective-permute-done | bytes 81952 | tf_op jit(solution)/shard_map/ppermute | solution.py:413
  44.8 3.7 %collective-permute-start.17 = (f32[1,80,128]{2,1,0:T(8,128)S(1)}, f32[1,80,128]{2,1,0:T(8,128)S(1)}, u32[]{:S(2)}, u32[]{:S(2)}) collective-permute-start(f32[1,80,128]{2,1,0:T(8,128)S(1)} %get-tuple-element.58), channel_id=1, source_target_pairs={{0,1},{1,0},{2,3},{3,2},{4,5},{5,4},{6,7},{7,6},{8,9},{9,8},{10,11... | collective-permute-start | bytes 122888 | tf_op jit(solution)/shard_map/ppermute | solution.py:417
  48.5 1.6 %collective-permute-done.15.refs_4_ = f32[2,80,128]{2,1,0:T(8,128)S(1)} collective-permute-done((f32[2,80,128]{2,1,0:T(8,128)S(1)}, f32[2,80,128]{2,1,0:T(8,128)S(1)}, u32[]{:S(2)}, u32[]{:S(2)}) %collective-permute-start.15) | collective-permute-done | bytes 81952 | tf_op jit(solution)/shard_map/ppermute | solution.py:413
  50.4 2.0 %shard_map.90 = f32[512,128]{1,0:T(8,128)} custom-call(s32[1,8]{1,0:T(1,128)S(1)} %bitcast.16, s32[1,8]{1,0:T(1,128)S(1)} %bitcast.18, f32[2,80,128]{2,1,0:T(8,128)S(1)} %collective-permute-done.11.refs_2_.refs_0_, f32[2,80,128]{2,1,0:T(8,128)S(1)} %collective-permute-done.12.refs_1_, f32[2,80,128]{2,1,0:T(8,128)S(1)} %collective-permute-done.13.refs_2_, ...), custom_call_target="tpu_custom_call" | custom-call | flops 335544320 | bytes 1638400 | tf_op jit(solution)/shard_map/pallas_call | solution.py:395
  (31 shorter events, 1.3 us)
Async XLA Ops:
  0.0 13.3 %copy-start.2 = (s32[512]{0:T(512)S(1)}, s32[512]{0:T(512)}, u32[]{:S(2)}) copy-start(s32[512]{0:T(512)} %param.14) | copy-start | bytes 6148
  0.0 13.3 %copy-start.1 = (f32[64,4,4]{0,2,1:T(4,128)S(1)}, f32[64,4,4]{0,2,1:T(4,128)}, u32[]{:S(2)}) copy-start(f32[64,4,4]{0,2,1:T(4,128)} %param.13) | copy-start | bytes 12292
  0.0 21.7 %copy-start.3 = (s32[1,1,8]{2,1,0:T(1,128)S(1)}, s32[1,1,8]{2,1,0:T(1,128)}, u32[]{:S(2)}) copy-start(s32[1,1,8]{2,1,0:T(1,128)} %param.11) | copy-start | bytes 100
  0.0 21.7 %copy-start.4 = (s32[1,1,8]{2,1,0:T(1,128)S(1)}, s32[1,1,8]{2,1,0:T(1,128)}, u32[]{:S(2)}) copy-start(s32[1,1,8]{2,1,0:T(1,128)} %param.12) | copy-start | bytes 100
  2.6 7.6 %collective-permute-start.5 = (f32[1,80,128]{2,1,0:T(8,128)S(1)}, f32[1,80,128]{2,1,0:T(8,128)S(1)}, u32[]{:S(2)}, u32[]{:S(2)}) collective-permute-start(f32[1,80,128]{2,1,0:T(8,128)S(1)} %get-tuple-element.37), channel_id=1, source_target_pairs={{0,7},{1,2},{2,1},{3,4},{4,3},{5,6},{6,5},{7,0},{8,15},{9,10},{10,... | collective-permute-start | bytes 122888 | tf_op jit(solution)/shard_map/ppermute | solution.py:413
  7.2 6.1 %collective-permute-start.6 = (f32[1,80,128]{2,1,0:T(8,128)S(1)}, f32[1,80,128]{2,1,0:T(8,128)S(1)}, u32[]{:S(2)}, u32[]{:S(2)}) collective-permute-start(f32[1,80,128]{2,1,0:T(8,128)S(1)} %get-tuple-element.38), channel_id=1, source_target_pairs={{0,1},{1,0},{2,3},{3,2},{4,5},{5,4},{6,7},{7,6},{8,9},{9,8},{10,11... | collective-permute-start | bytes 122888 | tf_op jit(solution)/shard_map/ppermute | solution.py:413
  7.2 9.4 %collective-permute-start = (f32[2,80,128]{2,1,0:T(8,128)S(1)}, f32[2,80,128]{2,1,0:T(8,128)S(1)}, u32[]{:S(2)}, u32[]{:S(2)}) collective-permute-start(f32[2,80,128]{2,1,0:T(8,128)S(1)} %get-tuple-element.32), channel_id=1, source_target_pairs={{0,4},{1,5},{2,6},{3,7},{4,0},{5,1},{6,2},{7,3},{8,12},{9,13},{10,... | collective-permute-start | bytes 245768 | tf_op jit(solution)/shard_map/ppermute | solution.py:413
  8.4 8.2 %collective-permute-start.1 = (f32[2,80,128]{2,1,0:T(8,128)S(1)}, f32[2,80,128]{2,1,0:T(8,128)S(1)}, u32[]{:S(2)}, u32[]{:S(2)}) collective-permute-start(f32[2,80,128]{2,1,0:T(8,128)S(1)} %get-tuple-element.33), channel_id=1, source_target_pairs={{0,5},{1,6},{2,7},{3,0},{4,1},{5,2},{6,3},{7,4},{8,13},{9,14},{10,... | collective-permute-start | bytes 245768 | tf_op jit(solution)/shard_map/ppermute | solution.py:413
  9.9 11.8 %collective-permute-start.2 = (f32[2,80,128]{2,1,0:T(8,128)S(1)}, f32[2,80,128]{2,1,0:T(8,128)S(1)}, u32[]{:S(2)}, u32[]{:S(2)}) collective-permute-start(f32[2,80,128]{2,1,0:T(8,128)S(1)} %get-tuple-element.34), channel_id=1, source_target_pairs={{0,3},{1,4},{2,5},{3,6},{4,7},{5,0},{6,1},{7,2},{8,11},{9,12},{10,... | collective-permute-start | bytes 245768 | tf_op jit(solution)/shard_map/ppermute | solution.py:413
  10.2 11.5 %collective-permute-start.3 = (f32[2,80,128]{2,1,0:T(8,128)S(1)}, f32[2,80,128]{2,1,0:T(8,128)S(1)}, u32[]{:S(2)}, u32[]{:S(2)}) collective-permute-start(f32[2,80,128]{2,1,0:T(8,128)S(1)} %get-tuple-element.35), channel_id=1, source_target_pairs={{0,6},{1,7},{2,0},{3,1},{4,2},{5,3},{6,4},{7,5},{8,14},{9,15},{10,... | collective-permute-start | bytes 245768 | tf_op jit(solution)/shard_map/ppermute | solution.py:413
  13.3 8.4 %collective-permute-start.4 = (f32[2,80,128]{2,1,0:T(8,128)S(1)}, f32[2,80,128]{2,1,0:T(8,128)S(1)}, u32[]{:S(2)}, u32[]{:S(2)}) collective-permute-start(f32[2,80,128]{2,1,0:T(8,128)S(1)} %get-tuple-element.36), channel_id=1, source_target_pairs={{0,2},{1,3},{2,4},{3,5},{4,6},{5,7},{6,0},{7,1},{8,10},{9,11},{10,... | collective-permute-start | bytes 245768 | tf_op jit(solution)/shard_map/ppermute | solution.py:413
  23.0 5.3 %collective-permute-start.7 = (f32[256,128]{1,0:T(8,128)S(1)}, f32[256,128]{1,0:T(8,128)S(1)}, u32[]{:S(2)}, u32[]{:S(2)}) collective-permute-start(f32[256,128]{1,0:T(8,128)S(1)} %get-tuple-element.41.own_ref), channel_id=1, source_target_pairs={{0,8},{1,17},{2,10},{3,19},{4,12},{5,21},{6,14},{7,23},{8,0},{9,25... | collective-permute-start | bytes 393224 | tf_op jit(solution)/shard_map/ppermute | solution.py:180
  24.6 5.1 %collective-permute-start.9 = (f32[256,128]{1,0:T(8,128)S(1)}, f32[256,128]{1,0:T(8,128)S(1)}, u32[]{:S(2)}, u32[]{:S(2)}) collective-permute-start(f32[256,128]{1,0:T(8,128)S(1)} %get-tuple-element.45.own_ref), channel_id=1, source_target_pairs={{0,16},{1,9},{2,18},{3,11},{4,20},{5,13},{6,22},{7,15},{8,24},{9,1... | collective-permute-start | bytes 393224 | tf_op jit(solution)/shard_map/ppermute | solution.py:180
  28.4 15.1 %copy-start = (f32[1,1,512,512]{3,2,1,0:T(8,128)S(1)}, f32[1,1,512,512]{3,2,1,0:T(8,128)}, u32[]{:S(2)}) copy-start(f32[1,1,512,512]{3,2,1,0:T(8,128)} %param.8) | copy-start | bytes 3145732
  28.4 5.0 %collective-permute-start.8 = (f32[256,128]{1,0:T(8,128)S(1)}, f32[256,128]{1,0:T(8,128)S(1)}, u32[]{:S(2)}, u32[]{:S(2)}) collective-permute-start(f32[256,128]{1,0:T(8,128)S(1)} %get-tuple-element.44), channel_id=1, source_target_pairs={{0,16},{1,9},{2,18},{3,11},{4,20},{5,13},{6,22},{7,15},{8,24},{9,1... | collective-permute-start | bytes 393224 | tf_op jit(solution)/shard_map/ppermute | solution.py:186
  29.7 5.0 %collective-permute-start.10 = (f32[256,128]{1,0:T(8,128)S(1)}, f32[256,128]{1,0:T(8,128)S(1)}, u32[]{:S(2)}, u32[]{:S(2)}) collective-permute-start(f32[256,128]{1,0:T(8,128)S(1)} %get-tuple-element.47), channel_id=1, source_target_pairs={{0,8},{1,17},{2,10},{3,19},{4,12},{5,21},{6,14},{7,23},{8,0},{9,25... | collective-permute-start | bytes 393224 | tf_op jit(solution)/shard_map/ppermute | solution.py:186
  35.5 9.2 %collective-permute-start.11 = (f32[2,80,128]{2,1,0:T(8,128)S(1)}, f32[2,80,128]{2,1,0:T(8,128)S(1)}, u32[]{:S(2)}, u32[]{:S(2)}) collective-permute-start(f32[2,80,128]{2,1,0:T(8,128)S(1)} %get-tuple-element.49), channel_id=1, source_target_pairs={{0,4},{1,5},{2,6},{3,7},{4,0},{5,1},{6,2},{7,3},{8,12},{9,13},{10,... | collective-permute-start | bytes 245768 | tf_op jit(solution)/shard_map/ppermute | solution.py:413
  37.5 7.3 %collective-permute-start.12 = (f32[2,80,128]{2,1,0:T(8,128)S(1)}, f32[2,80,128]{2,1,0:T(8,128)S(1)}, u32[]{:S(2)}, u32[]{:S(2)}) collective-permute-start(f32[2,80,128]{2,1,0:T(8,128)S(1)} %get-tuple-element.50), channel_id=1, source_target_pairs={{0,5},{1,6},{2,7},{3,0},{4,1},{5,2},{6,3},{7,4},{8,13},{9,14},{10,... | collective-permute-start | bytes 245768 | tf_op jit(solution)/shard_map/ppermute | solution.py:413
  37.5 10.9 %collective-permute-start.13 = (f32[2,80,128]{2,1,0:T(8,128)S(1)}, f32[2,80,128]{2,1,0:T(8,128)S(1)}, u32[]{:S(2)}, u32[]{:S(2)}) collective-permute-start(f32[2,80,128]{2,1,0:T(8,128)S(1)} %get-tuple-element.51), channel_id=1, source_target_pairs={{0,3},{1,4},{2,5},{3,6},{4,7},{5,0},{6,1},{7,2},{8,11},{9,12},{10,... | collective-permute-start | bytes 245768 | tf_op jit(solution)/shard_map/ppermute | solution.py:413
  39.2 9.2 %collective-permute-start.14 = (f32[2,80,128]{2,1,0:T(8,128)S(1)}, f32[2,80,128]{2,1,0:T(8,128)S(1)}, u32[]{:S(2)}, u32[]{:S(2)}) collective-permute-start(f32[2,80,128]{2,1,0:T(8,128)S(1)} %get-tuple-element.52), channel_id=1, source_target_pairs={{0,6},{1,7},{2,0},{3,1},{4,2},{5,3},{6,4},{7,5},{8,14},{9,15},{10,... | collective-permute-start | bytes 245768 | tf_op jit(solution)/shard_map/ppermute | solution.py:413
  43.4 6.6 %collective-permute-start.15 = (f32[2,80,128]{2,1,0:T(8,128)S(1)}, f32[2,80,128]{2,1,0:T(8,128)S(1)}, u32[]{:S(2)}, u32[]{:S(2)}) collective-permute-start(f32[2,80,128]{2,1,0:T(8,128)S(1)} %get-tuple-element.53), channel_id=1, source_target_pairs={{0,2},{1,3},{2,4},{3,5},{4,6},{5,7},{6,0},{7,1},{8,10},{9,11},{10,... | collective-permute-start | bytes 245768 | tf_op jit(solution)/shard_map/ppermute | solution.py:413
  44.7 5.7 %collective-permute-start.16 = (f32[1,80,128]{2,1,0:T(8,128)S(1)}, f32[1,80,128]{2,1,0:T(8,128)S(1)}, u32[]{:S(2)}, u32[]{:S(2)}) collective-permute-start(f32[1,80,128]{2,1,0:T(8,128)S(1)} %get-tuple-element.57), channel_id=1, source_target_pairs={{0,7},{1,2},{2,1},{3,4},{4,3},{5,6},{6,5},{7,0},{8,15},{9,10},{10,... | collective-permute-start | bytes 122888 | tf_op jit(solution)/shard_map/ppermute | solution.py:417
  44.8 5.6 %collective-permute-start.17 = (f32[1,80,128]{2,1,0:T(8,128)S(1)}, f32[1,80,128]{2,1,0:T(8,128)S(1)}, u32[]{:S(2)}, u32[]{:S(2)}) collective-permute-start(f32[1,80,128]{2,1,0:T(8,128)S(1)} %get-tuple-element.58), channel_id=1, source_target_pairs={{0,1},{1,0},{2,3},{3,2},{4,5},{5,4},{6,7},{7,6},{8,9},{9,8},{10,11... | collective-permute-start | bytes 122888 | tf_op jit(solution)/shard_map/ppermute | solution.py:417
where the time goes:
time: 52.5 us; the launch traced here: 52.3 us
  starting transfers between devices  28.3 us (54%)
  waiting for transfers between devices  14.6 us (28%)
  Pallas kernels  9.28 us (18%)
    ppermute x12, starting transfers between devices, deliver(): gots[at] = lax.ppermute(coeffs[at], 'tile', message.pairs)  18.7 us
    ppermute x12, waiting for transfers between devices, deliver(): gots[at] = lax.ppermute(coeffs[at], 'tile', message.pairs)  8.5 us
    ppermute x2, starting transfers between devices, deliver(): gots[at] = lax.ppermute(value, 'tile', messages[at].pairs)  3.74 us
    ppermute x2, waiting for transfers between devices, mix(): lax.ppermute(send, axes, pairs)  3.49 us
    pallas_call x2, Pallas kernels, rows(): call(functools.partial(row_kernel, messages, halves, final), pltpu.HBM((s...  3.25 us
    ppermute x2, starting transfers between devices, mix(): lax.ppermute(part, axes, pairs)  3.06 us
    ppermute x2, starting transfers between devices, mix(): lax.ppermute(send, axes, pairs)  2.85 us
    pallas_call x1, Pallas kernels, first_coefficients(): call(functools.partial(first_coeff_kernel, messages, per), outs, [in_vmem...  2.59 us
  transfers between devices with their start and end apart: 18, of which 8 were waited for; matrix products, arithmetic and copies ran while one was open for 0% of the time, Pallas kernels for 5%

commit v1 on v0

--- a/solution.py
+++ b/solution.py
@@ -64,7 +64,7 @@
         self.across = self.width * sum((a < half) != (b < half) for a, b in pairs)
 
 
-def messages_of(count, slots, per):
+def message_sets_of(count, slots):
     reach = slots // 2
     groups = {}
     for slot in range(slots):
@@ -72,76 +72,128 @@
         groups.setdefault(offset % count, []).append(slot)
     messages = []
     below, above = reach - 1, reach
-    single = groups.get(1) == [above] and groups.get(count - 1) == [below]
-    if single and count % 2 == 0 and below // per == above // per:
+    if groups.get(1) == [above] and groups.get(count - 1) == [below] and count % 2 == 0:
         del groups[1], groups[count - 1]
         for turn, (even, odd) in enumerate(((below, above), (above, below))):
             pairs = [(at, (at + (1, -1)[(at + turn) % 2]) % count) for at in range(count)]
             messages.append(Message(pairs, [even], [odd]))
     for ahead, group in groups.items():
         messages.append(Message([(at, (at - ahead) % count) for at in range(count)], group))
-    return sorted(messages, key=lambda message: -message.across)
-
-
-def store_coefficients(got, chunk, per, messages, rank, outs):
-    size = per * rank
+    messages.sort(key=lambda message: -message.across)
+    return [messages[: len(messages) // 2], messages[len(messages) // 2 :]]
+
+
+def slots_of(messages):
+    return sorted({slot for m in messages for slot in m.slots + (m.odd_slots or [])})
+
+
+def copy_runs(slots, source, target, sems):
+    copies, at = [], 0
+    while at < len(slots):
+        count = 1
+        while at + count < len(slots) and slots[at + count] == slots[at] + count:
+            count += 1
+        copies.append(
+            pltpu.make_async_copy(
+                source.at[pl.ds(slots[at], count)], target.at[pl.ds(at, count)], sems.at[at]
+            )
+        )
+        copies[-1].start()
+        at += count
+    return copies
+
+
+def store_coefficients(split_ref, both, messages, rank, outs):
+    slots = slots_of(messages)
+    size = len(slots) * rank
+    got = fold(dot(split_ref[...], both))
     got = got[:size] + got[size:]
 
     def piece(slot):
-        row = (slot - chunk * per) * rank
+        row = slots.index(slot) * rank
         return got[row : row + rank]
 
     odd = jnp.full((rank, got.shape[1]), lax.axis_index("tile") & 1, jnp.int32) == 1
     for message, out in zip(messages, outs):
         for w, slot in enumerate(message.slots):
-            if slot // per == chunk:
-                value = piece(slot)
-                if message.odd_slots is not None:
-                    value = jnp.where(odd, piece(message.odd_slots[w]), value)
-                out[w] = value
-
-
-def first_coeff_kernel(messages, per, cols_ref, right_ref, *refs):
-    outs, (split_ref, cols, right, sems) = refs[: len(messages)], refs[len(messages) :]
-    slots, rank, size = right.shape
-    chunks = slots // per
-    cols_copy = pltpu.make_async_copy(cols_ref, cols, sems.at[chunks])
+            value = piece(slot)
+            if message.odd_slots is not None:
+                value = jnp.where(odd, piece(message.odd_slots[w]), value)
+            out[w] = value
+
+
+def split_rows(right, split_ref):
+    count, rank, size = right.shape
+    rows = count * rank
+    hi, lo = split(right[...].reshape(rows, size))
+    split_ref[:rows] = hi
+    split_ref[rows:] = lo
+
+
+def first_coeff_kernel(messages, others, cols_ref, right_ref, *refs):
+    outs, refs = refs[: len(messages)], refs[len(messages) :]
+    split_ref, both_ref, rest_ref, cols, right, cols_sem, sems, rest_sems = refs
+    cols_copy = pltpu.make_async_copy(cols_ref, cols, cols_sem)
     cols_copy.start()
-    copies = []
-    for chunk in range(chunks):
-        span = pl.ds(chunk * per, per)
-        copies.append(pltpu.make_async_copy(right_ref.at[span], right.at[span], sems.at[chunk]))
-        copies[-1].start()
+    copies = copy_runs(slots_of(messages), right_ref, right, sems)
+    rest = copy_runs(slots_of(others), right_ref, rest_ref, rest_sems)
     cols_copy.wait()
-    both = side_by_side(cols[...])
-    for chunk in range(chunks):
-        copies[chunk].wait()
-        hi, lo = split(right[pl.ds(chunk * per, per)].reshape(per * rank, size))
-        base = 2 * chunk * per * rank
-        split_ref[pl.ds(base, per * rank)] = hi
-        split_ref[pl.ds(base + per * rank, per * rank)] = lo
-        got = fold(dot(split_ref[pl.ds(base, 2 * per * rank)], both))
-        store_coefficients(got, chunk, per, messages, rank, outs)
-
-
-def first_coefficients(cols, right_tile, messages, per):
-    slots, rank, size = right_tile.shape
+    both_ref[...] = side_by_side(cols[...])
+    for copy in copies:
+        copy.wait()
+    split_rows(right, split_ref)
+    store_coefficients(split_ref, both_ref[...], messages, right.shape[1], outs)
+    for copy in rest:
+        copy.wait()
+
+
+def first_coefficients(cols, right_tile, messages, others):
+    _, rank, size = right_tile.shape
     width = cols.shape[1]
+    count, rest = len(slots_of(messages)), len(slots_of(others))
     outs = [struct(message.width, rank, width) for message in messages]
-    outs.append(struct(2 * slots * rank, size, dtype=bf16))
+    outs += [
+        struct(2 * count * rank, size, dtype=bf16),
+        struct(size, 2 * width, dtype=bf16),
+        struct(rest, rank, size),
+    ]
     got = call(
-        functools.partial(first_coeff_kernel, messages, per),
+        functools.partial(first_coeff_kernel, messages, others),
         outs,
         [in_vmem] * len(outs),
         [in_hbm, in_hbm],
         [
             pltpu.VMEM(cols.shape, f32),
-            pltpu.VMEM(right_tile.shape, f32),
-            pltpu.SemaphoreType.DMA((slots // per + 1,)),
+            pltpu.VMEM((count, rank, size), f32),
+            pltpu.SemaphoreType.DMA,
+            pltpu.SemaphoreType.DMA((count,)),
+            pltpu.SemaphoreType.DMA((rest,)),
         ],
-        flops=8 * slots * rank * size * width,
-        moved=4 * slots * rank * (2 * size + width),
+        flops=8 * count * rank * size * width,
+        moved=4 * (count + rest) * rank * size,
     )(to_hbm(cols), to_hbm(right_tile))
+    return got[:-3], got[-3], got[-2], got[-1]
+
+
+def rest_coeff_kernel(messages, both_ref, right_ref, *refs):
+    outs, split_ref = refs[:-1], refs[-1]
+    split_rows(right_ref, split_ref)
+    store_coefficients(split_ref, both_ref[...], messages, right_ref.shape[1], outs)
+
+
+def rest_coefficients(both, right, messages):
+    count, rank, size = right.shape
+    width = both.shape[1] // 2
+    outs = [struct(message.width, rank, width) for message in messages]
+    outs.append(struct(2 * count * rank, size, dtype=bf16))
+    got = call(
+        functools.partial(rest_coeff_kernel, messages),
+        outs,
+        [in_vmem] * len(outs),
+        [in_vmem] * 2,
+        flops=8 * count * rank * size * width,
+        moved=8 * count * rank * size,
+    )(both, right)
     return got[:-1], got[-1]
 
 
@@ -187,37 +239,51 @@
     ]
 
 
-def mixed_coeff_kernel(messages, per, terms, *refs):
-    fields, split_ref, outs, cols_ref = refs[:terms], refs[terms], refs[terms + 1 : -1], refs[-1]
+def mixed_coeff_kernel(messages, terms, *refs):
+    fields, split_ref = refs[:terms], refs[terms]
+    outs, cols_ref, both_ref = refs[terms + 1 : -2], refs[-2], refs[-1]
     part = fields[0].shape[0]
     for at in range(0, terms, 2):
+        rows_of = pl.ds(at // 2 * part, part)
         total = fields[at][...] + fields[at + 1][...]
-        cols_ref[pl.ds(at // 2 * part, part)] = total
-    both = side_by_side(cols_ref[...])
-    rank = outs[0].shape[1]
-    got = fold(dot(split_ref[...], both))
-    size = 2 * per * rank
-    for chunk in range(split_ref.shape[0] // size):
-        here = got[chunk * size : (chunk + 1) * size]
-        store_coefficients(here, chunk, per, messages, rank, outs)
-
-
-def mixed_coefficients(mixed, split_right, messages, per, rank):
+        cols_ref[rows_of] = total
+        both_ref[rows_of] = side_by_side(total)
+    store_coefficients(split_ref, both_ref[...], messages, outs[0].shape[1], outs)
+
+
+def mixed_coefficients(mixed, split_right, messages, rank):
     flat = [term for pair in mixed for term in pair]
     part, width = flat[0].shape
     size = part * len(mixed)
     total = split_right.shape[0]
     outs = [struct(message.width, rank, width) for message in messages]
-    outs.append(struct(size, width))
+    outs += [struct(size, width), struct(size, 2 * width, dtype=bf16)]
     got = call(
-        functools.partial(mixed_coeff_kernel, messages, per, len(flat)),
+        functools.partial(mixed_coeff_kernel, messages, len(flat)),
         outs,
         [in_vmem] * len(outs),
         [in_vmem] * (len(flat) + 1),
         flops=4 * total * size * width,
         moved=2 * total * (size + width),
     )(*flat, split_right)
-    return got[:-1], got[-1]
+    return got[:-2], got[-2], got[-1]
+
+
+def next_coeff_kernel(messages, both_ref, split_ref, *outs):
+    store_coefficients(split_ref, both_ref[...], messages, outs[0].shape[1], outs)
+
+
+def next_coefficients(both, split_right, messages, rank):
+    size, width = both.shape[0], both.shape[1] // 2
+    total = split_right.shape[0]
+    return call(
+        functools.partial(next_coeff_kernel, messages),
+        [struct(message.width, rank, width) for message in messages],
+        [in_vmem] * len(messages),
+        [in_vmem] * 2,
+        flops=4 * total * size * width,
+        moved=2 * total * (size + width),
+    )(both, split_right)
 
 
 def times_diag(diag_ref, cols_ref):
@@ -403,19 +469,17 @@
     )(offsets, ranks, *gots, left_split, diag_part)
 
 
-def deliver(coeffs, messages, beside=None):
-    gots = {}
-    small = [at for at, message in enumerate(messages) if message.width < messages[0].width]
-    if beside is None:
-        small = []
-    for at, message in enumerate(messages):
-        if at not in small:
-            gots[at] = lax.ppermute(coeffs[at], "tile", message.pairs)
-    if small:
-        values = relay([coeffs[at] for at in small], [gots[0], beside])
-        for at, value in zip(small, values):
-            gots[at] = lax.ppermute(value, "tile", messages[at].pairs)
-    return [gots[at] for at in range(len(messages))]
+def send(value, message):
+    return lax.ppermute(value, "tile", message.pairs)
+
+
+def send_near(coeffs, messages, after):
+    gots = []
+    for value, message in zip(coeffs, messages):
+        if message.odd_slots is not None and message.across:
+            value = relay([value], after)[0]
+        gots.append(send(value, message))
+    return gots
 
 
 def local(
@@ -440,16 +504,20 @@
     index = block_index[None]
     cols = rhs_field[0]
 
-    per = 4 if slots % 4 == 0 else slots
-    messages = messages_of(lax.axis_size("tile"), slots, per)
-    coeffs, split_right = first_coefficients(cols, right_tile, messages, per)
-    gots = deliver(coeffs, messages)
+    far, near = message_sets_of(lax.axis_size("tile"), slots)
+    messages = far + near
+    coeffs, split_far, both, rest = first_coefficients(cols, right_tile, far, near)
+    gots = [send(value, message) for value, message in zip(coeffs, far)]
+    coeffs, split_near = rest_coefficients(both, rest, near)
     diag_part, left_split, weights = prepare(diag_tile, cols, left_rows, table, index, halves)
+    gots += send_near(coeffs, near, [gots[0], diag_part])
     first = rows(offsets, ranks, gots, messages, left_split, diag_part, slots, halves, False)
     mixed = mix(first, weights)
-    coeffs, cols = mixed_coefficients(mixed, split_right, messages, per, rank)
+    coeffs, cols, both = mixed_coefficients(mixed, split_far, far, rank)
+    gots = [send(value, message) for value, message in zip(coeffs, far)]
+    coeffs = next_coefficients(both, split_near, near, rank)
     diag_part = diagonal(diag_tile, cols)
-    gots = deliver(coeffs, messages, diag_part)
+    gots += send_near(coeffs, near, [gots[0], diag_part])
     return rows(offsets, ranks, gots, messages, left_split, diag_part, slots, halves, True)[None]
 
 

time: 52.5 us -> 52.7 us (level)
    ppermute x14, waiting for transfers between devices: 8.86 us -> 7.88 us  [send(): return lax.ppermute(value, 'tile', message.pairs)]
    ppermute x2, waiting for transfers between devices: 2.25 us -> 3.03 us  [mix(): lax.ppermute(part, axes, pairs)]
    pallas_call x2 -> x4, Pallas kernels: 3.27 us -> 3.49 us  [the longest x1 2.16 us: first_coefficients(): call(functools.partial(first_coeff_kernel, messages, others), outs, [in_v...]
  transfers between devices with their start and end apart: 18 -> 18, of which waited for: 8 -> 7; matrix products, arithmetic and copies ran while one was open for 0% -> 0% of each run, Pallas kernels for 5% -> 7%
where the time goes in v1:
time: 52.7 us; the launch traced here: 52.4 us
  starting transfers between devices  28.3 us (54%)
  waiting for transfers between devices  14.4 us (27%)
  Pallas kernels  9.55 us (18%)
    ppermute x14, starting transfers between devices, send(): return lax.ppermute(value, 'tile', message.pairs)  22.2 us
    ppermute x14, waiting for transfers between devices, send(): return lax.ppermute(value, 'tile', message.pairs)  7.88 us
    ppermute x2, waiting for transfers between devices, mix(): lax.ppermute(send, axes, pairs)  3.49 us
    pallas_call x2, Pallas kernels, rows(): call(functools.partial(row_kernel, messages, halves, final), pltpu.HBM((s...  3.26 us
    ppermute x2, starting transfers between devices, mix(): lax.ppermute(send, axes, pairs)  3.1 us
    ppermute x2, starting transfers between devices, mix(): lax.ppermute(part, axes, pairs)  3.06 us
    ppermute x2, waiting for transfers between devices, mix(): lax.ppermute(part, axes, pairs)  3.03 us
    pallas_call x1, Pallas kernels, prepare(): call(functools.partial(prepare_kernel, halves), [struct(size, width), str...  2.22 us
  transfers between devices with their start and end apart: 18, of which 7 were waited for; matrix products, arithmetic and copies ran while one was open for 0% of the time, Pallas kernels for 7%

profile of v1, /device:TPU:0, one launch (start us, length us, event | category | flops | bytes accessed | tf_op | source)
XLA Modules:
  0.0 52.4 jit_solution(10242669434077933372)
XLA Ops:
  0.0 2.2 %shard_map.82 = (f32[2,80,128]{2,1,0:T(8,128)S(1)}, f32[2,80,128]{2,1,0:T(8,128)S(1)}, f32[2,80,128]{2,1,0:T(8,128)S(1)}, bf16[960,512]{1,0:T(8,128)(2,1)S(1)}, ...) custom-call(f32[512,128]{1,0:T(8,128)} %bitcast.21, f32[12,80,512]{2,1,0:T(8,128)} %bitcast.19), custom_call_target="tpu_custom_call" | custom-call | flops 251658240 | bytes 1966080 | tf_op jit(solution)/shard_map/pallas_call | solution.py:160
  2.2 4.1 %collective-permute-start = (f32[2,80,128]{2,1,0:T(8,128)S(1)}, f32[2,80,128]{2,1,0:T(8,128)S(1)}, u32[]{:S(2)}, u32[]{:S(2)}) collective-permute-start(f32[2,80,128]{2,1,0:T(8,128)S(1)} %get-tuple-element.34), channel_id=1, source_target_pairs={{0,4},{1,5},{2,6},{3,7},{4,0},{5,1},{6,2},{7,3},{8,12},{9,13},{10,... | collective-permute-start | bytes 245768 | tf_op jit(solution)/shard_map/ppermute | solution.py:473
  6.3 1.7 %collective-permute-start.2 = (f32[2,80,128]{2,1,0:T(8,128)S(1)}, f32[2,80,128]{2,1,0:T(8,128)S(1)}, u32[]{:S(2)}, u32[]{:S(2)}) collective-permute-start(f32[2,80,128]{2,1,0:T(8,128)S(1)} %get-tuple-element.36), channel_id=1, source_target_pairs={{0,3},{1,4},{2,5},{3,6},{4,7},{5,0},{6,1},{7,2},{8,11},{9,12},{10,... | collective-permute-start | bytes 245768 | tf_op jit(solution)/shard_map/ppermute | solution.py:473
  9.0 2.8 %collective-permute-start.3 = (f32[2,80,128]{2,1,0:T(8,128)S(1)}, f32[2,80,128]{2,1,0:T(8,128)S(1)}, u32[]{:S(2)}, u32[]{:S(2)}) collective-permute-start(f32[2,80,128]{2,1,0:T(8,128)S(1)} %get-tuple-element.39), channel_id=1, source_target_pairs={{0,6},{1,7},{2,0},{3,1},{4,2},{5,3},{6,4},{7,5},{8,14},{9,15},{10,... | collective-permute-start | bytes 245768 | tf_op jit(solution)/shard_map/ppermute | solution.py:473
  11.8 2.2 %collective-permute-start.4 = (f32[2,80,128]{2,1,0:T(8,128)S(1)}, f32[2,80,128]{2,1,0:T(8,128)S(1)}, u32[]{:S(2)}, u32[]{:S(2)}) collective-permute-start(f32[2,80,128]{2,1,0:T(8,128)S(1)} %get-tuple-element.40), channel_id=1, source_target_pairs={{0,2},{1,3},{2,4},{3,5},{4,6},{5,7},{6,0},{7,1},{8,10},{9,11},{10,... | collective-permute-start | bytes 245768 | tf_op jit(solution)/shard_map/ppermute | solution.py:473
  14.0 2.2 %shard_map.84 = (f32[512,128]{1,0:T(8,128)S(1)}, bf16[1024,640]{1,0:T(8,128)(2,1)S(1)}, f32[8,256,128]{2,1,0:T(8,128)S(1)}) custom-call(f32[512,512]{1,0:T(8,128)} %bitcast.11, f32[512,128]{1,0:T(8,128)} %bitcast.22, f32[640,512]{1,0:T(8,128)} %bitcast.20, f32[16,64]{1,0:T(8,128)S(1)} %bitcast.13, s32[1,512]{1,0:T(1,128)S(1)} %bitcast.14), custom_call_target="tpu_custom_call" | custom-call | flops 268435456 | bytes 4194304 | tf_op jit(solution)/shard_map/pallas_call | solution.py:384
  16.3 2.2 %collective-permute-start.5 = (f32[1,80,128]{2,1,0:T(8,128)S(1)}, f32[1,80,128]{2,1,0:T(8,128)S(1)}, u32[]{:S(2)}, u32[]{:S(2)}) collective-permute-start(f32[1,80,128]{2,1,0:T(8,128)S(1)} %shard_map.85), channel_id=1, source_target_pairs={{0,7},{1,2},{2,1},{3,4},{4,3},{5,6},{6,5},{7,0},{8,15},{9,10},{10,... | collective-permute-start | bytes 122888 | tf_op jit(solution)/shard_map/ppermute | solution.py:473
  18.5 2.4 %collective-permute-done.4.refs_4_ = f32[2,80,128]{2,1,0:T(8,128)S(1)} collective-permute-done((f32[2,80,128]{2,1,0:T(8,128)S(1)}, f32[2,80,128]{2,1,0:T(8,128)S(1)}, u32[]{:S(2)}, u32[]{:S(2)}) %collective-permute-start.4) | collective-permute-done | bytes 81952 | tf_op jit(solution)/shard_map/ppermute | solution.py:473
  21.6 1.3 %shard_map.86 = (f32[256,128]{1,0:T(8,128)S(1)}, f32[256,128]{1,0:T(8,128)S(1)}) custom-call(s32[1,8]{1,0:T(1,128)S(1)} %bitcast.15, s32[1,8]{1,0:T(1,128)S(1)} %bitcast.17, f32[2,80,128]{2,1,0:T(8,128)S(1)} %collective-permute-done.refs_1_.refs_0_, f32[2,80,128]{2,1,0:T(8,128)S(1)} %collective-permute-done.1.refs_1_, ...), custom_call_target="tpu_custom_call" | custom-call | flops 335544320 | bytes 1638400 | tf_op jit(solution)/shard_map/pallas_call | solution.py:461
  22.9 1.6 %collective-permute-start.7 = (f32[256,128]{1,0:T(8,128)S(1)}, f32[256,128]{1,0:T(8,128)S(1)}, u32[]{:S(2)}, u32[]{:S(2)}) collective-permute-start(f32[256,128]{1,0:T(8,128)S(1)} %get-tuple-element.45.own_ref), channel_id=1, source_target_pairs={{0,8},{1,17},{2,10},{3,19},{4,12},{5,21},{6,14},{7,23},{8,0},{9,25... | collective-permute-start | bytes 393224 | tf_op jit(solution)/shard_map/ppermute | solution.py:232
  24.4 1.5 %collective-permute-start.9 = (f32[256,128]{1,0:T(8,128)S(1)}, f32[256,128]{1,0:T(8,128)S(1)}, u32[]{:S(2)}, u32[]{:S(2)}) collective-permute-start(f32[256,128]{1,0:T(8,128)S(1)} %get-tuple-element.49.own_ref), channel_id=1, source_target_pairs={{0,16},{1,9},{2,18},{3,11},{4,20},{5,13},{6,22},{7,15},{8,24},{9,1... | collective-permute-start | bytes 393224 | tf_op jit(solution)/shard_map/ppermute | solution.py:232
  25.9 3.0 %collective-permute-done.7.got_ref = f32[256,128]{1,0:T(8,128)S(1)} collective-permute-done((f32[256,128]{1,0:T(8,128)S(1)}, f32[256,128]{1,0:T(8,128)S(1)}, u32[]{:S(2)}, u32[]{:S(2)}) %collective-permute-start.7) | collective-permute-done | bytes 131104 | tf_op jit(solution)/shard_map/ppermute | solution.py:232
  29.0 1.6 %collective-permute-start.8 = (f32[256,128]{1,0:T(8,128)S(1)}, f32[256,128]{1,0:T(8,128)S(1)}, u32[]{:S(2)}, u32[]{:S(2)}) collective-permute-start(f32[256,128]{1,0:T(8,128)S(1)} %get-tuple-element.48), channel_id=1, source_target_pairs={{0,16},{1,9},{2,18},{3,11},{4,20},{5,13},{6,22},{7,15},{8,24},{9,1... | collective-permute-start | bytes 393224 | tf_op jit(solution)/shard_map/ppermute | solution.py:238
  30.6 1.5 %collective-permute-start.10 = (f32[256,128]{1,0:T(8,128)S(1)}, f32[256,128]{1,0:T(8,128)S(1)}, u32[]{:S(2)}, u32[]{:S(2)}) collective-permute-start(f32[256,128]{1,0:T(8,128)S(1)} %get-tuple-element.51), channel_id=1, source_target_pairs={{0,8},{1,17},{2,10},{3,19},{4,12},{5,21},{6,14},{7,23},{8,0},{9,25... | collective-permute-start | bytes 393224 | tf_op jit(solution)/shard_map/ppermute | solution.py:238
  32.2 1.9 %collective-permute-done.8.refs_1_ = f32[256,128]{1,0:T(8,128)S(1)} collective-permute-done((f32[256,128]{1,0:T(8,128)S(1)}, f32[256,128]{1,0:T(8,128)S(1)}, u32[]{:S(2)}, u32[]{:S(2)}) %collective-permute-start.8) | collective-permute-done | bytes 131104 | tf_op jit(solution)/shard_map/ppermute | solution.py:238
  34.0 1.6 %collective-permute-done.10.refs_3_ = f32[256,128]{1,0:T(8,128)S(1)} collective-permute-done((f32[256,128]{1,0:T(8,128)S(1)}, f32[256,128]{1,0:T(8,128)S(1)}, u32[]{:S(2)}, u32[]{:S(2)}) %collective-permute-start.10) | collective-permute-done | bytes 131104 | tf_op jit(solution)/shard_map/ppermute | solution.py:238
  36.1 2.2 %collective-permute-start.11 = (f32[2,80,128]{2,1,0:T(8,128)S(1)}, f32[2,80,128]{2,1,0:T(8,128)S(1)}, u32[]{:S(2)}, u32[]{:S(2)}) collective-permute-start(f32[2,80,128]{2,1,0:T(8,128)S(1)} %get-tuple-element.53), channel_id=1, source_target_pairs={{0,4},{1,5},{2,6},{3,7},{4,0},{5,1},{6,2},{7,3},{8,12},{9,13},{10,... | collective-permute-start | bytes 245768 | tf_op jit(solution)/shard_map/ppermute | solution.py:473
  38.8 0.8 %collective-permute-start.12 = (f32[2,80,128]{2,1,0:T(8,128)S(1)}, f32[2,80,128]{2,1,0:T(8,128)S(1)}, u32[]{:S(2)}, u32[]{:S(2)}) collective-permute-start(f32[2,80,128]{2,1,0:T(8,128)S(1)} %get-tuple-element.54), channel_id=1, source_target_pairs={{0,5},{1,6},{2,7},{3,0},{4,1},{5,2},{6,3},{7,4},{8,13},{9,14},{10,... | collective-permute-start | bytes 245768 | tf_op jit(solution)/shard_map/ppermute | solution.py:473
  39.7 1.0 %collective-permute-start.13 = (f32[2,80,128]{2,1,0:T(8,128)S(1)}, f32[2,80,128]{2,1,0:T(8,128)S(1)}, u32[]{:S(2)}, u32[]{:S(2)}) collective-permute-start(f32[2,80,128]{2,1,0:T(8,128)S(1)} %get-tuple-element.55), channel_id=1, source_target_pairs={{0,3},{1,4},{2,5},{3,6},{4,7},{5,0},{6,1},{7,2},{8,11},{9,12},{10,... | collective-permute-start | bytes 245768 | tf_op jit(solution)/shard_map/ppermute | solution.py:473
  40.6 2.1 %collective-permute-start.14 = (f32[2,80,128]{2,1,0:T(8,128)S(1)}, f32[2,80,128]{2,1,0:T(8,128)S(1)}, u32[]{:S(2)}, u32[]{:S(2)}) collective-permute-start(f32[2,80,128]{2,1,0:T(8,128)S(1)} %get-tuple-element.58), channel_id=1, source_target_pairs={{0,6},{1,7},{2,0},{3,1},{4,2},{5,3},{6,4},{7,5},{8,14},{9,15},{10,... | collective-permute-start | bytes 245768 | tf_op jit(solution)/shard_map/ppermute | solution.py:473
  43.3 2.4 %collective-permute-start.16 = (f32[1,80,128]{2,1,0:T(8,128)S(1)}, f32[1,80,128]{2,1,0:T(8,128)S(1)}, u32[]{:S(2)}, u32[]{:S(2)}) collective-permute-start(f32[1,80,128]{2,1,0:T(8,128)S(1)} %shard_map.92), channel_id=1, source_target_pairs={{0,7},{1,2},{2,1},{3,4},{4,3},{5,6},{6,5},{7,0},{8,15},{9,10},{10,... | collective-permute-start | bytes 122888 | tf_op jit(solution)/shard_map/ppermute | solution.py:473
  45.7 4.0 %collective-permute-done.13.refs_2_ = f32[2,80,128]{2,1,0:T(8,128)S(1)} collective-permute-done((f32[2,80,128]{2,1,0:T(8,128)S(1)}, f32[2,80,128]{2,1,0:T(8,128)S(1)}, u32[]{:S(2)}, u32[]{:S(2)}) %collective-permute-start.13) | collective-permute-done | bytes 81952 | tf_op jit(solution)/shard_map/ppermute | solution.py:473
  49.6 0.8 %collective-permute-done.14.refs_3_ = f32[2,80,128]{2,1,0:T(8,128)S(1)} collective-permute-done((f32[2,80,128]{2,1,0:T(8,128)S(1)}, f32[2,80,128]{2,1,0:T(8,128)S(1)}, u32[]{:S(2)}, u32[]{:S(2)}) %collective-permute-start.14) | collective-permute-done | bytes 81952 | tf_op jit(solution)/shard_map/ppermute | solution.py:473
  50.5 2.0 %shard_map.93 = f32[512,128]{1,0:T(8,128)} custom-call(s32[1,8]{1,0:T(1,128)S(1)} %bitcast.16, s32[1,8]{1,0:T(1,128)S(1)} %bitcast.18, f32[2,80,128]{2,1,0:T(8,128)S(1)} %collective-permute-done.11.refs_1_.refs_0_, f32[2,80,128]{2,1,0:T(8,128)S(1)} %collective-permute-done.12.refs_1_, f32[2,80,128]{2,1,0:T(8,128)S(1)} %collective-permute-done.13.refs_2_, ...), custom_call_target="tpu_custom_call" | custom-call | flops 335544320 | bytes 1638400 | tf_op jit(solution)/shard_map/pallas_call | solution.py:461
  (34 shorter events, 3.2 us)
Async XLA Ops:
  0.0 14.0 %copy-start.1 = (f32[64,4,4]{0,2,1:T(4,128)S(1)}, f32[64,4,4]{0,2,1:T(4,128)}, u32[]{:S(2)}) copy-start(f32[64,4,4]{0,2,1:T(4,128)} %param.13) | copy-start | bytes 12292
  0.0 14.0 %copy-start.2 = (s32[512]{0:T(512)S(1)}, s32[512]{0:T(512)}, u32[]{:S(2)}) copy-start(s32[512]{0:T(512)} %param.14) | copy-start | bytes 6148
  2.2 9.6 %collective-permute-start = (f32[2,80,128]{2,1,0:T(8,128)S(1)}, f32[2,80,128]{2,1,0:T(8,128)S(1)}, u32[]{:S(2)}, u32[]{:S(2)}) collective-permute-start(f32[2,80,128]{2,1,0:T(8,128)S(1)} %get-tuple-element.34), channel_id=1, source_target_pairs={{0,4},{1,5},{2,6},{3,7},{4,0},{5,1},{6,2},{7,3},{8,12},{9,13},{10,... | collective-permute-start | bytes 245768 | tf_op jit(solution)/shard_map/ppermute | solution.py:473
  6.3 12.2 %collective-permute-start.1 = (f32[2,80,128]{2,1,0:T(8,128)S(1)}, f32[2,80,128]{2,1,0:T(8,128)S(1)}, u32[]{:S(2)}, u32[]{:S(2)}) collective-permute-start(f32[2,80,128]{2,1,0:T(8,128)S(1)} %get-tuple-element.35), channel_id=1, source_target_pairs={{0,5},{1,6},{2,7},{3,0},{4,1},{5,2},{6,3},{7,4},{8,13},{9,14},{10,... | collective-permute-start | bytes 245768 | tf_op jit(solution)/shard_map/ppermute | solution.py:473
  6.3 12.2 %collective-permute-start.2 = (f32[2,80,128]{2,1,0:T(8,128)S(1)}, f32[2,80,128]{2,1,0:T(8,128)S(1)}, u32[]{:S(2)}, u32[]{:S(2)}) collective-permute-start(f32[2,80,128]{2,1,0:T(8,128)S(1)} %get-tuple-element.36), channel_id=1, source_target_pairs={{0,3},{1,4},{2,5},{3,6},{4,7},{5,0},{6,1},{7,2},{8,11},{9,12},{10,... | collective-permute-start | bytes 245768 | tf_op jit(solution)/shard_map/ppermute | solution.py:473
  8.5 7.8 %collective-permute-start.6 = (f32[1,80,128]{2,1,0:T(8,128)S(1)}, f32[1,80,128]{2,1,0:T(8,128)S(1)}, u32[]{:S(2)}, u32[]{:S(2)}) collective-permute-start(f32[1,80,128]{2,1,0:T(8,128)S(1)} %get-tuple-element.43), channel_id=1, source_target_pairs={{0,1},{1,0},{2,3},{3,2},{4,5},{5,4},{6,7},{7,6},{8,9},{9,8},{10,11... | collective-permute-start | bytes 122888 | tf_op jit(solution)/shard_map/ppermute | solution.py:473
  9.0 9.4 %collective-permute-start.3 = (f32[2,80,128]{2,1,0:T(8,128)S(1)}, f32[2,80,128]{2,1,0:T(8,128)S(1)}, u32[]{:S(2)}, u32[]{:S(2)}) collective-permute-start(f32[2,80,128]{2,1,0:T(8,128)S(1)} %get-tuple-element.39), channel_id=1, source_target_pairs={{0,6},{1,7},{2,0},{3,1},{4,2},{5,3},{6,4},{7,5},{8,14},{9,15},{10,... | collective-permute-start | bytes 245768 | tf_op jit(solution)/shard_map/ppermute | solution.py:473
  11.8 9.1 %collective-permute-start.4 = (f32[2,80,128]{2,1,0:T(8,128)S(1)}, f32[2,80,128]{2,1,0:T(8,128)S(1)}, u32[]{:S(2)}, u32[]{:S(2)}) collective-permute-start(f32[2,80,128]{2,1,0:T(8,128)S(1)} %get-tuple-element.40), channel_id=1, source_target_pairs={{0,2},{1,3},{2,4},{3,5},{4,6},{5,7},{6,0},{7,1},{8,10},{9,11},{10,... | collective-permute-start | bytes 245768 | tf_op jit(solution)/shard_map/ppermute | solution.py:473
  14.0 7.6 %copy-start.3 = (s32[1,1,8]{2,1,0:T(1,128)S(1)}, s32[1,1,8]{2,1,0:T(1,128)}, u32[]{:S(2)}) copy-start(s32[1,1,8]{2,1,0:T(1,128)} %param.11) | copy-start | bytes 100
  14.0 7.6 %copy-start.4 = (s32[1,1,8]{2,1,0:T(1,128)S(1)}, s32[1,1,8]{2,1,0:T(1,128)}, u32[]{:S(2)}) copy-start(s32[1,1,8]{2,1,0:T(1,128)} %param.12) | copy-start | bytes 100
  16.3 5.3 %collective-permute-start.5 = (f32[1,80,128]{2,1,0:T(8,128)S(1)}, f32[1,80,128]{2,1,0:T(8,128)S(1)}, u32[]{:S(2)}, u32[]{:S(2)}) collective-permute-start(f32[1,80,128]{2,1,0:T(8,128)S(1)} %shard_map.85), channel_id=1, source_target_pairs={{0,7},{1,2},{2,1},{3,4},{4,3},{5,6},{6,5},{7,0},{8,15},{9,10},{10,... | collective-permute-start | bytes 122888 | tf_op jit(solution)/shard_map/ppermute | solution.py:473
  22.9 6.1 %collective-permute-start.7 = (f32[256,128]{1,0:T(8,128)S(1)}, f32[256,128]{1,0:T(8,128)S(1)}, u32[]{:S(2)}, u32[]{:S(2)}) collective-permute-start(f32[256,128]{1,0:T(8,128)S(1)} %get-tuple-element.45.own_ref), channel_id=1, source_target_pairs={{0,8},{1,17},{2,10},{3,19},{4,12},{5,21},{6,14},{7,23},{8,0},{9,25... | collective-permute-start | bytes 393224 | tf_op jit(solution)/shard_map/ppermute | solution.py:232
  24.4 6.2 %collective-permute-start.9 = (f32[256,128]{1,0:T(8,128)S(1)}, f32[256,128]{1,0:T(8,128)S(1)}, u32[]{:S(2)}, u32[]{:S(2)}) collective-permute-start(f32[256,128]{1,0:T(8,128)S(1)} %get-tuple-element.49.own_ref), channel_id=1, source_target_pairs={{0,16},{1,9},{2,18},{3,11},{4,20},{5,13},{6,22},{7,15},{8,24},{9,1... | collective-permute-start | bytes 393224 | tf_op jit(solution)/shard_map/ppermute | solution.py:232
  29.0 5.0 %collective-permute-start.8 = (f32[256,128]{1,0:T(8,128)S(1)}, f32[256,128]{1,0:T(8,128)S(1)}, u32[]{:S(2)}, u32[]{:S(2)}) collective-permute-start(f32[256,128]{1,0:T(8,128)S(1)} %get-tuple-element.48), channel_id=1, source_target_pairs={{0,16},{1,9},{2,18},{3,11},{4,20},{5,13},{6,22},{7,15},{8,24},{9,1... | collective-permute-start | bytes 393224 | tf_op jit(solution)/shard_map/ppermute | solution.py:238
  30.6 5.0 %collective-permute-start.10 = (f32[256,128]{1,0:T(8,128)S(1)}, f32[256,128]{1,0:T(8,128)S(1)}, u32[]{:S(2)}, u32[]{:S(2)}) collective-permute-start(f32[256,128]{1,0:T(8,128)S(1)} %get-tuple-element.51), channel_id=1, source_target_pairs={{0,8},{1,17},{2,10},{3,19},{4,12},{5,21},{6,14},{7,23},{8,0},{9,25... | collective-permute-start | bytes 393224 | tf_op jit(solution)/shard_map/ppermute | solution.py:238
  35.7 7.1 %copy-start = (f32[1,1,512,512]{3,2,1,0:T(8,128)S(1)}, f32[1,1,512,512]{3,2,1,0:T(8,128)}, u32[]{:S(2)}) copy-start(f32[1,1,512,512]{3,2,1,0:T(8,128)} %param.8) | copy-start | bytes 3145732
  36.1 6.7 %collective-permute-start.11 = (f32[2,80,128]{2,1,0:T(8,128)S(1)}, f32[2,80,128]{2,1,0:T(8,128)S(1)}, u32[]{:S(2)}, u32[]{:S(2)}) collective-permute-start(f32[2,80,128]{2,1,0:T(8,128)S(1)} %get-tuple-element.53), channel_id=1, source_target_pairs={{0,4},{1,5},{2,6},{3,7},{4,0},{5,1},{6,2},{7,3},{8,12},{9,13},{10,... | collective-permute-start | bytes 245768 | tf_op jit(solution)/shard_map/ppermute | solution.py:473
  38.8 4.5 %collective-permute-start.17 = (f32[1,80,128]{2,1,0:T(8,128)S(1)}, f32[1,80,128]{2,1,0:T(8,128)S(1)}, u32[]{:S(2)}, u32[]{:S(2)}) collective-permute-start(f32[1,80,128]{2,1,0:T(8,128)S(1)} %get-tuple-element.62), channel_id=1, source_target_pairs={{0,1},{1,0},{2,3},{3,2},{4,5},{5,4},{6,7},{7,6},{8,9},{9,8},{10,11... | collective-permute-start | bytes 122888 | tf_op jit(solution)/shard_map/ppermute | solution.py:473
  38.8 6.8 %collective-permute-start.12 = (f32[2,80,128]{2,1,0:T(8,128)S(1)}, f32[2,80,128]{2,1,0:T(8,128)S(1)}, u32[]{:S(2)}, u32[]{:S(2)}) collective-permute-start(f32[2,80,128]{2,1,0:T(8,128)S(1)} %get-tuple-element.54), channel_id=1, source_target_pairs={{0,5},{1,6},{2,7},{3,0},{4,1},{5,2},{6,3},{7,4},{8,13},{9,14},{10,... | collective-permute-start | bytes 245768 | tf_op jit(solution)/shard_map/ppermute | solution.py:473
  39.7 9.9 %collective-permute-start.13 = (f32[2,80,128]{2,1,0:T(8,128)S(1)}, f32[2,80,128]{2,1,0:T(8,128)S(1)}, u32[]{:S(2)}, u32[]{:S(2)}) collective-permute-start(f32[2,80,128]{2,1,0:T(8,128)S(1)} %get-tuple-element.55), channel_id=1, source_target_pairs={{0,3},{1,4},{2,5},{3,6},{4,7},{5,0},{6,1},{7,2},{8,11},{9,12},{10,... | collective-permute-start | bytes 245768 | tf_op jit(solution)/shard_map/ppermute | solution.py:473
  40.6 9.8 %collective-permute-start.14 = (f32[2,80,128]{2,1,0:T(8,128)S(1)}, f32[2,80,128]{2,1,0:T(8,128)S(1)}, u32[]{:S(2)}, u32[]{:S(2)}) collective-permute-start(f32[2,80,128]{2,1,0:T(8,128)S(1)} %get-tuple-element.58), channel_id=1, source_target_pairs={{0,6},{1,7},{2,0},{3,1},{4,2},{5,3},{6,4},{7,5},{8,14},{9,15},{10,... | collective-permute-start | bytes 245768 | tf_op jit(solution)/shard_map/ppermute | solution.py:473
  42.8 7.7 %collective-permute-start.15 = (f32[2,80,128]{2,1,0:T(8,128)S(1)}, f32[2,80,128]{2,1,0:T(8,128)S(1)}, u32[]{:S(2)}, u32[]{:S(2)}) collective-permute-start(f32[2,80,128]{2,1,0:T(8,128)S(1)} %get-tuple-element.59), channel_id=1, source_target_pairs={{0,2},{1,3},{2,4},{3,5},{4,6},{5,7},{6,0},{7,1},{8,10},{9,11},{10,... | collective-permute-start | bytes 245768 | tf_op jit(solution)/shard_map/ppermute | solution.py:473
  43.3 7.2 %collective-permute-start.16 = (f32[1,80,128]{2,1,0:T(8,128)S(1)}, f32[1,80,128]{2,1,0:T(8,128)S(1)}, u32[]{:S(2)}, u32[]{:S(2)}) collective-permute-start(f32[1,80,128]{2,1,0:T(8,128)S(1)} %shard_map.92), channel_id=1, source_target_pairs={{0,7},{1,2},{2,1},{3,4},{4,3},{5,6},{6,5},{7,0},{8,15},{9,10},{10,... | collective-permute-start | bytes 122888 | tf_op jit(solution)/shard_map/ppermute | solution.py:473

commit v2 on v1

--- a/solution.py
+++ b/solution.py
@@ -473,10 +473,10 @@
     return lax.ppermute(value, "tile", message.pairs)
 
 
-def send_near(coeffs, messages, after):
+def send_near(coeffs, messages, after=None):
     gots = []
     for value, message in zip(coeffs, messages):
-        if message.odd_slots is not None and message.across:
+        if after is not None and message.odd_slots is not None and message.across:
             value = relay([value], after)[0]
         gots.append(send(value, message))
     return gots
@@ -509,8 +509,8 @@
     coeffs, split_far, both, rest = first_coefficients(cols, right_tile, far, near)
     gots = [send(value, message) for value, message in zip(coeffs, far)]
     coeffs, split_near = rest_coefficients(both, rest, near)
+    gots += send_near(coeffs, near)
     diag_part, left_split, weights = prepare(diag_tile, cols, left_rows, table, index, halves)
-    gots += send_near(coeffs, near, [gots[0], diag_part])
     first = rows(offsets, ranks, gots, messages, left_split, diag_part, slots, halves, False)
     mixed = mix(first, weights)
     coeffs, cols, both = mixed_coefficients(mixed, split_far, far, rank)

time: 52.7 us -> 52.7 us (level)
  waiting for transfers between devices: 14.4 us -> 15.6 us
  starting transfers between devices: 28.3 us -> 27.2 us
    ppermute x14, waiting for transfers between devices: 7.88 us -> 9.92 us  [send(): return lax.ppermute(value, 'tile', message.pairs)]
    ppermute x14, starting transfers between devices: 22.2 us -> 21.3 us  [send(): return lax.ppermute(value, 'tile', message.pairs)]
    ppermute x2, waiting for transfers between devices: 3.03 us -> 2.23 us  [mix(): lax.ppermute(part, axes, pairs)]
  transfers between devices with their start and end apart: 18 -> 18, of which waited for: 7 -> 7; matrix products, arithmetic and copies ran while one was open for 0% -> 0% of each run, Pallas kernels for 7% -> 6%
where the time goes in v2:
time: 52.7 us; the launch traced here: 52.5 us
  starting transfers between devices  27.2 us (52%)
  waiting for transfers between devices  15.6 us (30%)
  Pallas kernels  9.52 us (18%)
    ppermute x14, starting transfers between devices, send(): return lax.ppermute(value, 'tile', message.pairs)  21.3 us
    ppermute x14, waiting for transfers between devices, send(): return lax.ppermute(value, 'tile', message.pairs)  9.92 us
    ppermute x2, waiting for transfers between devices, mix(): lax.ppermute(send, axes, pairs)  3.47 us
    pallas_call x2, Pallas kernels, rows(): call(functools.partial(row_kernel, messages, halves, final), pltpu.HBM((s...  3.26 us
    ppermute x2, starting transfers between devices, mix(): lax.ppermute(part, axes, pairs)  3.08 us
    ppermute x2, starting transfers between devices, mix(): lax.ppermute(send, axes, pairs)  2.87 us
    ppermute x2, waiting for transfers between devices, mix(): lax.ppermute(part, axes, pairs)  2.23 us
    pallas_call x1, Pallas kernels, prepare(): call(functools.partial(prepare_kernel, halves), [struct(size, width), str...  2.21 us
  transfers between devices with their start and end apart: 18, of which 7 were waited for; matrix products, arithmetic and copies ran while one was open for 0% of the time, Pallas kernels for 6%

profile of v2, /device:TPU:0, one launch (start us, length us, event | category | flops | bytes accessed | tf_op | source)
XLA Modules:
  0.0 52.5 jit_solution(7407181772410331086)
XLA Ops:
  0.0 2.2 %shard_map.82 = (f32[2,80,128]{2,1,0:T(8,128)S(1)}, f32[2,80,128]{2,1,0:T(8,128)S(1)}, f32[2,80,128]{2,1,0:T(8,128)S(1)}, bf16[960,512]{1,0:T(8,128)(2,1)S(1)}, ...) custom-call(f32[512,128]{1,0:T(8,128)} %bitcast.21, f32[12,80,512]{2,1,0:T(8,128)} %bitcast.19), custom_call_target="tpu_custom_call" | custom-call | flops 251658240 | bytes 1966080 | tf_op jit(solution)/shard_map/pallas_call | solution.py:160
  2.6 4.6 %collective-permute-start.5 = (f32[1,80,128]{2,1,0:T(8,128)S(1)}, f32[1,80,128]{2,1,0:T(8,128)S(1)}, u32[]{:S(2)}, u32[]{:S(2)}) collective-permute-start(f32[1,80,128]{2,1,0:T(8,128)S(1)} %get-tuple-element.41), channel_id=1, source_target_pairs={{0,7},{1,2},{2,1},{3,4},{4,3},{5,6},{6,5},{7,0},{8,15},{9,10},{10,... | collective-permute-start | bytes 122888 | tf_op jit(solution)/shard_map/ppermute | solution.py:473
  7.2 1.2 %collective-permute-start = (f32[2,80,128]{2,1,0:T(8,128)S(1)}, f32[2,80,128]{2,1,0:T(8,128)S(1)}, u32[]{:S(2)}, u32[]{:S(2)}) collective-permute-start(f32[2,80,128]{2,1,0:T(8,128)S(1)} %get-tuple-element.34), channel_id=1, source_target_pairs={{0,4},{1,5},{2,6},{3,7},{4,0},{5,1},{6,2},{7,3},{8,12},{9,13},{10,... | collective-permute-start | bytes 245768 | tf_op jit(solution)/shard_map/ppermute | solution.py:473
  8.4 1.5 %collective-permute-start.1 = (f32[2,80,128]{2,1,0:T(8,128)S(1)}, f32[2,80,128]{2,1,0:T(8,128)S(1)}, u32[]{:S(2)}, u32[]{:S(2)}) collective-permute-start(f32[2,80,128]{2,1,0:T(8,128)S(1)} %get-tuple-element.35), channel_id=1, source_target_pairs={{0,5},{1,6},{2,7},{3,0},{4,1},{5,2},{6,3},{7,4},{8,13},{9,14},{10,... | collective-permute-start | bytes 245768 | tf_op jit(solution)/shard_map/ppermute | solution.py:473
  10.2 3.1 %collective-permute-start.3 = (f32[2,80,128]{2,1,0:T(8,128)S(1)}, f32[2,80,128]{2,1,0:T(8,128)S(1)}, u32[]{:S(2)}, u32[]{:S(2)}) collective-permute-start(f32[2,80,128]{2,1,0:T(8,128)S(1)} %get-tuple-element.39), channel_id=1, source_target_pairs={{0,6},{1,7},{2,0},{3,1},{4,2},{5,3},{6,4},{7,5},{8,14},{9,15},{10,... | collective-permute-start | bytes 245768 | tf_op jit(solution)/shard_map/ppermute | solution.py:473
  13.4 2.2 %shard_map.84 = (f32[512,128]{1,0:T(8,128)S(1)}, bf16[1024,640]{1,0:T(8,128)(2,1)S(1)}, f32[8,256,128]{2,1,0:T(8,128)S(1)}) custom-call(f32[512,512]{1,0:T(8,128)} %bitcast.11, f32[512,128]{1,0:T(8,128)} %bitcast.22, f32[640,512]{1,0:T(8,128)} %bitcast.20, f32[16,64]{1,0:T(8,128)S(1)} %bitcast.13, s32[1,512]{1,0:T(1,128)S(1)} %bitcast.14), custom_call_target="tpu_custom_call" | custom-call | flops 268435456 | bytes 4194304 | tf_op jit(solution)/shard_map/pallas_call | solution.py:384
  15.6 1.0 %collective-permute-done.refs_0_ = f32[2,80,128]{2,1,0:T(8,128)S(1)} collective-permute-done((f32[2,80,128]{2,1,0:T(8,128)S(1)}, f32[2,80,128]{2,1,0:T(8,128)S(1)}, u32[]{:S(2)}, u32[]{:S(2)}) %collective-permute-start) | collective-permute-done | bytes 81952 | tf_op jit(solution)/shard_map/ppermute | solution.py:473
  16.6 5.1 %collective-permute-done.2.refs_2_ = f32[2,80,128]{2,1,0:T(8,128)S(1)} collective-permute-done((f32[2,80,128]{2,1,0:T(8,128)S(1)}, f32[2,80,128]{2,1,0:T(8,128)S(1)}, u32[]{:S(2)}, u32[]{:S(2)}) %collective-permute-start.2) | collective-permute-done | bytes 81952 | tf_op jit(solution)/shard_map/ppermute | solution.py:473
  21.7 1.3 %shard_map.85 = (f32[256,128]{1,0:T(8,128)S(1)}, f32[256,128]{1,0:T(8,128)S(1)}) custom-call(s32[1,8]{1,0:T(1,128)S(1)} %bitcast.15, s32[1,8]{1,0:T(1,128)S(1)} %bitcast.17, f32[2,80,128]{2,1,0:T(8,128)S(1)} %collective-permute-done.refs_0_, f32[2,80,128]{2,1,0:T(8,128)S(1)} %collective-permute-done.1.refs_1_, ...), custom_call_target="tpu_custom_call" | custom-call | flops 335544320 | bytes 1638400 | tf_op jit(solution)/shard_map/pallas_call | solution.py:461
  23.0 1.6 %collective-permute-start.7 = (f32[256,128]{1,0:T(8,128)S(1)}, f32[256,128]{1,0:T(8,128)S(1)}, u32[]{:S(2)}, u32[]{:S(2)}) collective-permute-start(f32[256,128]{1,0:T(8,128)S(1)} %get-tuple-element.45.own_ref), channel_id=1, source_target_pairs={{0,8},{1,17},{2,10},{3,19},{4,12},{5,21},{6,14},{7,23},{8,0},{9,25... | collective-permute-start | bytes 393224 | tf_op jit(solution)/shard_map/ppermute | solution.py:232
  24.6 1.5 %collective-permute-start.9 = (f32[256,128]{1,0:T(8,128)S(1)}, f32[256,128]{1,0:T(8,128)S(1)}, u32[]{:S(2)}, u32[]{:S(2)}) collective-permute-start(f32[256,128]{1,0:T(8,128)S(1)} %get-tuple-element.49.own_ref), channel_id=1, source_target_pairs={{0,16},{1,9},{2,18},{3,11},{4,20},{5,13},{6,22},{7,15},{8,24},{9,1... | collective-permute-start | bytes 393224 | tf_op jit(solution)/shard_map/ppermute | solution.py:232
  26.1 2.2 %collective-permute-done.7.got_ref = f32[256,128]{1,0:T(8,128)S(1)} collective-permute-done((f32[256,128]{1,0:T(8,128)S(1)}, f32[256,128]{1,0:T(8,128)S(1)}, u32[]{:S(2)}, u32[]{:S(2)}) %collective-permute-start.7) | collective-permute-done | bytes 131104 | tf_op jit(solution)/shard_map/ppermute | solution.py:232
  28.4 1.3 %collective-permute-start.8 = (f32[256,128]{1,0:T(8,128)S(1)}, f32[256,128]{1,0:T(8,128)S(1)}, u32[]{:S(2)}, u32[]{:S(2)}) collective-permute-start(f32[256,128]{1,0:T(8,128)S(1)} %get-tuple-element.48), channel_id=1, source_target_pairs={{0,16},{1,9},{2,18},{3,11},{4,20},{5,13},{6,22},{7,15},{8,24},{9,1... | collective-permute-start | bytes 393224 | tf_op jit(solution)/shard_map/ppermute | solution.py:238
  29.8 1.6 %collective-permute-start.10 = (f32[256,128]{1,0:T(8,128)S(1)}, f32[256,128]{1,0:T(8,128)S(1)}, u32[]{:S(2)}, u32[]{:S(2)}) collective-permute-start(f32[256,128]{1,0:T(8,128)S(1)} %get-tuple-element.51), channel_id=1, source_target_pairs={{0,8},{1,17},{2,10},{3,19},{4,12},{5,21},{6,14},{7,23},{8,0},{9,25... | collective-permute-start | bytes 393224 | tf_op jit(solution)/shard_map/ppermute | solution.py:238
  31.3 2.1 %collective-permute-done.8.refs_1_ = f32[256,128]{1,0:T(8,128)S(1)} collective-permute-done((f32[256,128]{1,0:T(8,128)S(1)}, f32[256,128]{1,0:T(8,128)S(1)}, u32[]{:S(2)}, u32[]{:S(2)}) %collective-permute-start.8) | collective-permute-done | bytes 131104 | tf_op jit(solution)/shard_map/ppermute | solution.py:238
  33.4 1.4 %collective-permute-done.10.refs_3_ = f32[256,128]{1,0:T(8,128)S(1)} collective-permute-done((f32[256,128]{1,0:T(8,128)S(1)}, f32[256,128]{1,0:T(8,128)S(1)}, u32[]{:S(2)}, u32[]{:S(2)}) %collective-permute-start.10) | collective-permute-done | bytes 131104 | tf_op jit(solution)/shard_map/ppermute | solution.py:238
  35.3 2.0 %collective-permute-start.11 = (f32[2,80,128]{2,1,0:T(8,128)S(1)}, f32[2,80,128]{2,1,0:T(8,128)S(1)}, u32[]{:S(2)}, u32[]{:S(2)}) collective-permute-start(f32[2,80,128]{2,1,0:T(8,128)S(1)} %get-tuple-element.53), channel_id=1, source_target_pairs={{0,4},{1,5},{2,6},{3,7},{4,0},{5,1},{6,2},{7,3},{8,12},{9,13},{10,... | collective-permute-start | bytes 245768 | tf_op jit(solution)/shard_map/ppermute | solution.py:473
  37.8 1.0 %collective-permute-start.12 = (f32[2,80,128]{2,1,0:T(8,128)S(1)}, f32[2,80,128]{2,1,0:T(8,128)S(1)}, u32[]{:S(2)}, u32[]{:S(2)}) collective-permute-start(f32[2,80,128]{2,1,0:T(8,128)S(1)} %get-tuple-element.54), channel_id=1, source_target_pairs={{0,5},{1,6},{2,7},{3,0},{4,1},{5,2},{6,3},{7,4},{8,13},{9,14},{10,... | collective-permute-start | bytes 245768 | tf_op jit(solution)/shard_map/ppermute | solution.py:473
  38.8 0.8 %collective-permute-start.13 = (f32[2,80,128]{2,1,0:T(8,128)S(1)}, f32[2,80,128]{2,1,0:T(8,128)S(1)}, u32[]{:S(2)}, u32[]{:S(2)}) collective-permute-start(f32[2,80,128]{2,1,0:T(8,128)S(1)} %get-tuple-element.55), channel_id=1, source_target_pairs={{0,3},{1,4},{2,5},{3,6},{4,7},{5,0},{6,1},{7,2},{8,11},{9,12},{10,... | collective-permute-start | bytes 245768 | tf_op jit(solution)/shard_map/ppermute | solution.py:473
  39.6 4.2 %collective-permute-start.14 = (f32[2,80,128]{2,1,0:T(8,128)S(1)}, f32[2,80,128]{2,1,0:T(8,128)S(1)}, u32[]{:S(2)}, u32[]{:S(2)}) collective-permute-start(f32[2,80,128]{2,1,0:T(8,128)S(1)} %get-tuple-element.58), channel_id=1, source_target_pairs={{0,6},{1,7},{2,0},{3,1},{4,2},{5,3},{6,4},{7,5},{8,14},{9,15},{10,... | collective-permute-start | bytes 245768 | tf_op jit(solution)/shard_map/ppermute | solution.py:473
  44.3 2.5 %collective-permute-start.16 = (f32[1,80,128]{2,1,0:T(8,128)S(1)}, f32[1,80,128]{2,1,0:T(8,128)S(1)}, u32[]{:S(2)}, u32[]{:S(2)}) collective-permute-start(f32[1,80,128]{2,1,0:T(8,128)S(1)} %shard_map.91), channel_id=1, source_target_pairs={{0,7},{1,2},{2,1},{3,4},{4,3},{5,6},{6,5},{7,0},{8,15},{9,10},{10,... | collective-permute-start | bytes 122888 | tf_op jit(solution)/shard_map/ppermute | solution.py:473
  46.8 1.0 %collective-permute-done.13.refs_2_ = f32[2,80,128]{2,1,0:T(8,128)S(1)} collective-permute-done((f32[2,80,128]{2,1,0:T(8,128)S(1)}, f32[2,80,128]{2,1,0:T(8,128)S(1)}, u32[]{:S(2)}, u32[]{:S(2)}) %collective-permute-start.13) | collective-permute-done | bytes 81952 | tf_op jit(solution)/shard_map/ppermute | solution.py:473
  47.7 2.8 %collective-permute-done.15.refs_4_ = f32[2,80,128]{2,1,0:T(8,128)S(1)} collective-permute-done((f32[2,80,128]{2,1,0:T(8,128)S(1)}, f32[2,80,128]{2,1,0:T(8,128)S(1)}, u32[]{:S(2)}, u32[]{:S(2)}) %collective-permute-start.15) | collective-permute-done | bytes 81952 | tf_op jit(solution)/shard_map/ppermute | solution.py:473
  50.6 2.0 %shard_map.92 = f32[512,128]{1,0:T(8,128)} custom-call(s32[1,8]{1,0:T(1,128)S(1)} %bitcast.16, s32[1,8]{1,0:T(1,128)S(1)} %bitcast.18, f32[2,80,128]{2,1,0:T(8,128)S(1)} %collective-permute-done.11.refs_1_.refs_0_, f32[2,80,128]{2,1,0:T(8,128)S(1)} %collective-permute-done.12.refs_1_, f32[2,80,128]{2,1,0:T(8,128)S(1)} %collective-permute-done.13.refs_2_, ...), custom_call_target="tpu_custom_call" | custom-call | flops 335544320 | bytes 1638400 | tf_op jit(solution)/shard_map/pallas_call | solution.py:461
  (33 shorter events, 2.3 us)
Async XLA Ops:
  0.0 13.3 %copy-start.1 = (f32[64,4,4]{0,2,1:T(4,128)S(1)}, f32[64,4,4]{0,2,1:T(4,128)}, u32[]{:S(2)}) copy-start(f32[64,4,4]{0,2,1:T(4,128)} %param.13) | copy-start | bytes 12292
  0.0 13.3 %copy-start.2 = (s32[512]{0:T(512)S(1)}, s32[512]{0:T(512)}, u32[]{:S(2)}) copy-start(s32[512]{0:T(512)} %param.14) | copy-start | bytes 6148
  2.6 7.5 %collective-permute-start.5 = (f32[1,80,128]{2,1,0:T(8,128)S(1)}, f32[1,80,128]{2,1,0:T(8,128)S(1)}, u32[]{:S(2)}, u32[]{:S(2)}) collective-permute-start(f32[1,80,128]{2,1,0:T(8,128)S(1)} %get-tuple-element.41), channel_id=1, source_target_pairs={{0,7},{1,2},{2,1},{3,4},{4,3},{5,6},{6,5},{7,0},{8,15},{9,10},{10,... | collective-permute-start | bytes 122888 | tf_op jit(solution)/shard_map/ppermute | solution.py:473
  7.2 6.1 %collective-permute-start.6 = (f32[1,80,128]{2,1,0:T(8,128)S(1)}, f32[1,80,128]{2,1,0:T(8,128)S(1)}, u32[]{:S(2)}, u32[]{:S(2)}) collective-permute-start(f32[1,80,128]{2,1,0:T(8,128)S(1)} %get-tuple-element.42), channel_id=1, source_target_pairs={{0,1},{1,0},{2,3},{3,2},{4,5},{5,4},{6,7},{7,6},{8,9},{9,8},{10,11... | collective-permute-start | bytes 122888 | tf_op jit(solution)/shard_map/ppermute | solution.py:473
  7.2 9.4 %collective-permute-start = (f32[2,80,128]{2,1,0:T(8,128)S(1)}, f32[2,80,128]{2,1,0:T(8,128)S(1)}, u32[]{:S(2)}, u32[]{:S(2)}) collective-permute-start(f32[2,80,128]{2,1,0:T(8,128)S(1)} %get-tuple-element.34), channel_id=1, source_target_pairs={{0,4},{1,5},{2,6},{3,7},{4,0},{5,1},{6,2},{7,3},{8,12},{9,13},{10,... | collective-permute-start | bytes 245768 | tf_op jit(solution)/shard_map/ppermute | solution.py:473
  8.4 8.2 %collective-permute-start.1 = (f32[2,80,128]{2,1,0:T(8,128)S(1)}, f32[2,80,128]{2,1,0:T(8,128)S(1)}, u32[]{:S(2)}, u32[]{:S(2)}) collective-permute-start(f32[2,80,128]{2,1,0:T(8,128)S(1)} %get-tuple-element.35), channel_id=1, source_target_pairs={{0,5},{1,6},{2,7},{3,0},{4,1},{5,2},{6,3},{7,4},{8,13},{9,14},{10,... | collective-permute-start | bytes 245768 | tf_op jit(solution)/shard_map/ppermute | solution.py:473
  10.0 11.7 %collective-permute-start.2 = (f32[2,80,128]{2,1,0:T(8,128)S(1)}, f32[2,80,128]{2,1,0:T(8,128)S(1)}, u32[]{:S(2)}, u32[]{:S(2)}) collective-permute-start(f32[2,80,128]{2,1,0:T(8,128)S(1)} %get-tuple-element.36), channel_id=1, source_target_pairs={{0,3},{1,4},{2,5},{3,6},{4,7},{5,0},{6,1},{7,2},{8,11},{9,12},{10,... | collective-permute-start | bytes 245768 | tf_op jit(solution)/shard_map/ppermute | solution.py:473
  10.2 11.5 %collective-permute-start.3 = (f32[2,80,128]{2,1,0:T(8,128)S(1)}, f32[2,80,128]{2,1,0:T(8,128)S(1)}, u32[]{:S(2)}, u32[]{:S(2)}) collective-permute-start(f32[2,80,128]{2,1,0:T(8,128)S(1)} %get-tuple-element.39), channel_id=1, source_target_pairs={{0,6},{1,7},{2,0},{3,1},{4,2},{5,3},{6,4},{7,5},{8,14},{9,15},{10,... | collective-permute-start | bytes 245768 | tf_op jit(solution)/shard_map/ppermute | solution.py:473
  13.3 8.4 %collective-permute-start.4 = (f32[2,80,128]{2,1,0:T(8,128)S(1)}, f32[2,80,128]{2,1,0:T(8,128)S(1)}, u32[]{:S(2)}, u32[]{:S(2)}) collective-permute-start(f32[2,80,128]{2,1,0:T(8,128)S(1)} %get-tuple-element.40), channel_id=1, source_target_pairs={{0,2},{1,3},{2,4},{3,5},{4,6},{5,7},{6,0},{7,1},{8,10},{9,11},{10,... | collective-permute-start | bytes 245768 | tf_op jit(solution)/shard_map/ppermute | solution.py:473
  13.4 8.4 %copy-start.3 = (s32[1,1,8]{2,1,0:T(1,128)S(1)}, s32[1,1,8]{2,1,0:T(1,128)}, u32[]{:S(2)}) copy-start(s32[1,1,8]{2,1,0:T(1,128)} %param.11) | copy-start | bytes 100
  13.4 8.4 %copy-start.4 = (s32[1,1,8]{2,1,0:T(1,128)S(1)}, s32[1,1,8]{2,1,0:T(1,128)}, u32[]{:S(2)}) copy-start(s32[1,1,8]{2,1,0:T(1,128)} %param.12) | copy-start | bytes 100
  23.0 5.3 %collective-permute-start.7 = (f32[256,128]{1,0:T(8,128)S(1)}, f32[256,128]{1,0:T(8,128)S(1)}, u32[]{:S(2)}, u32[]{:S(2)}) collective-permute-start(f32[256,128]{1,0:T(8,128)S(1)} %get-tuple-element.45.own_ref), channel_id=1, source_target_pairs={{0,8},{1,17},{2,10},{3,19},{4,12},{5,21},{6,14},{7,23},{8,0},{9,25... | collective-permute-start | bytes 393224 | tf_op jit(solution)/shard_map/ppermute | solution.py:232
  24.6 5.1 %collective-permute-start.9 = (f32[256,128]{1,0:T(8,128)S(1)}, f32[256,128]{1,0:T(8,128)S(1)}, u32[]{:S(2)}, u32[]{:S(2)}) collective-permute-start(f32[256,128]{1,0:T(8,128)S(1)} %get-tuple-element.49.own_ref), channel_id=1, source_target_pairs={{0,16},{1,9},{2,18},{3,11},{4,20},{5,13},{6,22},{7,15},{8,24},{9,1... | collective-permute-start | bytes 393224 | tf_op jit(solution)/shard_map/ppermute | solution.py:232
  28.4 5.0 %collective-permute-start.8 = (f32[256,128]{1,0:T(8,128)S(1)}, f32[256,128]{1,0:T(8,128)S(1)}, u32[]{:S(2)}, u32[]{:S(2)}) collective-permute-start(f32[256,128]{1,0:T(8,128)S(1)} %get-tuple-element.48), channel_id=1, source_target_pairs={{0,16},{1,9},{2,18},{3,11},{4,20},{5,13},{6,22},{7,15},{8,24},{9,1... | collective-permute-start | bytes 393224 | tf_op jit(solution)/shard_map/ppermute | solution.py:238
  29.8 5.0 %collective-permute-start.10 = (f32[256,128]{1,0:T(8,128)S(1)}, f32[256,128]{1,0:T(8,128)S(1)}, u32[]{:S(2)}, u32[]{:S(2)}) collective-permute-start(f32[256,128]{1,0:T(8,128)S(1)} %get-tuple-element.51), channel_id=1, source_target_pairs={{0,8},{1,17},{2,10},{3,19},{4,12},{5,21},{6,14},{7,23},{8,0},{9,25... | collective-permute-start | bytes 393224 | tf_op jit(solution)/shard_map/ppermute | solution.py:238
  34.8 9.0 %copy-start = (f32[1,1,512,512]{3,2,1,0:T(8,128)S(1)}, f32[1,1,512,512]{3,2,1,0:T(8,128)}, u32[]{:S(2)}) copy-start(f32[1,1,512,512]{3,2,1,0:T(8,128)} %param.8) | copy-start | bytes 3145732
  35.3 8.5 %collective-permute-start.11 = (f32[2,80,128]{2,1,0:T(8,128)S(1)}, f32[2,80,128]{2,1,0:T(8,128)S(1)}, u32[]{:S(2)}, u32[]{:S(2)}) collective-permute-start(f32[2,80,128]{2,1,0:T(8,128)S(1)} %get-tuple-element.53), channel_id=1, source_target_pairs={{0,4},{1,5},{2,6},{3,7},{4,0},{5,1},{6,2},{7,3},{8,12},{9,13},{10,... | collective-permute-start | bytes 245768 | tf_op jit(solution)/shard_map/ppermute | solution.py:473
  37.7 6.6 %collective-permute-start.17 = (f32[1,80,128]{2,1,0:T(8,128)S(1)}, f32[1,80,128]{2,1,0:T(8,128)S(1)}, u32[]{:S(2)}, u32[]{:S(2)}) collective-permute-start(f32[1,80,128]{2,1,0:T(8,128)S(1)} %get-tuple-element.62), channel_id=1, source_target_pairs={{0,1},{1,0},{2,3},{3,2},{4,5},{5,4},{6,7},{7,6},{8,9},{9,8},{10,11... | collective-permute-start | bytes 122888 | tf_op jit(solution)/shard_map/ppermute | solution.py:473
  37.8 9.0 %collective-permute-start.12 = (f32[2,80,128]{2,1,0:T(8,128)S(1)}, f32[2,80,128]{2,1,0:T(8,128)S(1)}, u32[]{:S(2)}, u32[]{:S(2)}) collective-permute-start(f32[2,80,128]{2,1,0:T(8,128)S(1)} %get-tuple-element.54), channel_id=1, source_target_pairs={{0,5},{1,6},{2,7},{3,0},{4,1},{5,2},{6,3},{7,4},{8,13},{9,14},{10,... | collective-permute-start | bytes 245768 | tf_op jit(solution)/shard_map/ppermute | solution.py:473
  38.8 8.9 %collective-permute-start.13 = (f32[2,80,128]{2,1,0:T(8,128)S(1)}, f32[2,80,128]{2,1,0:T(8,128)S(1)}, u32[]{:S(2)}, u32[]{:S(2)}) collective-permute-start(f32[2,80,128]{2,1,0:T(8,128)S(1)} %get-tuple-element.55), channel_id=1, source_target_pairs={{0,3},{1,4},{2,5},{3,6},{4,7},{5,0},{6,1},{7,2},{8,11},{9,12},{10,... | collective-permute-start | bytes 245768 | tf_op jit(solution)/shard_map/ppermute | solution.py:473
  39.6 8.1 %collective-permute-start.14 = (f32[2,80,128]{2,1,0:T(8,128)S(1)}, f32[2,80,128]{2,1,0:T(8,128)S(1)}, u32[]{:S(2)}, u32[]{:S(2)}) collective-permute-start(f32[2,80,128]{2,1,0:T(8,128)S(1)} %get-tuple-element.58), channel_id=1, source_target_pairs={{0,6},{1,7},{2,0},{3,1},{4,2},{5,3},{6,4},{7,5},{8,14},{9,15},{10,... | collective-permute-start | bytes 245768 | tf_op jit(solution)/shard_map/ppermute | solution.py:473
  43.8 6.8 %collective-permute-start.15 = (f32[2,80,128]{2,1,0:T(8,128)S(1)}, f32[2,80,128]{2,1,0:T(8,128)S(1)}, u32[]{:S(2)}, u32[]{:S(2)}) collective-permute-start(f32[2,80,128]{2,1,0:T(8,128)S(1)} %get-tuple-element.59), channel_id=1, source_target_pairs={{0,2},{1,3},{2,4},{3,5},{4,6},{5,7},{6,0},{7,1},{8,10},{9,11},{10,... | collective-permute-start | bytes 245768 | tf_op jit(solution)/shard_map/ppermute | solution.py:473
  44.3 6.3 %collective-permute-start.16 = (f32[1,80,128]{2,1,0:T(8,128)S(1)}, f32[1,80,128]{2,1,0:T(8,128)S(1)}, u32[]{:S(2)}, u32[]{:S(2)}) collective-permute-start(f32[1,80,128]{2,1,0:T(8,128)S(1)} %shard_map.91), channel_id=1, source_target_pairs={{0,7},{1,2},{2,1},{3,4},{4,3},{5,6},{6,5},{7,0},{8,15},{9,10},{10,... | collective-permute-start | bytes 122888 | tf_op jit(solution)/shard_map/ppermute | solution.py:473

commit v3 on v2

--- a/solution.py
+++ b/solution.py
@@ -80,7 +80,8 @@
     for ahead, group in groups.items():
         messages.append(Message([(at, (at - ahead) % count) for at in range(count)], group))
     messages.sort(key=lambda message: -message.across)
-    return [messages[: len(messages) // 2], messages[len(messages) // 2 :]]
+    first = messages[:1] + [m for m in messages[1:] if m.odd_slots is not None]
+    return [first, [message for message in messages if message not in first]]
 
 
 def slots_of(messages):
@@ -473,11 +474,11 @@
     return lax.ppermute(value, "tile", message.pairs)
 
 
-def send_near(coeffs, messages, after=None):
+def send_all(coeffs, messages, after=None):
     gots = []
     for value, message in zip(coeffs, messages):
         if after is not None and message.odd_slots is not None and message.across:
-            value = relay([value], after)[0]
+            value = relay([value], [gots[0], after])[0]
         gots.append(send(value, message))
     return gots
 
@@ -504,20 +505,19 @@
     index = block_index[None]
     cols = rhs_field[0]
 
-    far, near = message_sets_of(lax.axis_size("tile"), slots)
-    messages = far + near
-    coeffs, split_far, both, rest = first_coefficients(cols, right_tile, far, near)
-    gots = [send(value, message) for value, message in zip(coeffs, far)]
-    coeffs, split_near = rest_coefficients(both, rest, near)
-    gots += send_near(coeffs, near)
+    one, two = message_sets_of(lax.axis_size("tile"), slots)
+    messages = one + two
+    coeffs, split_one, both, rest = first_coefficients(cols, right_tile, one, two)
+    gots = send_all(coeffs, one)
+    coeffs, split_two = rest_coefficients(both, rest, two)
+    gots += send_all(coeffs, two)
     diag_part, left_split, weights = prepare(diag_tile, cols, left_rows, table, index, halves)
     first = rows(offsets, ranks, gots, messages, left_split, diag_part, slots, halves, False)
     mixed = mix(first, weights)
-    coeffs, cols, both = mixed_coefficients(mixed, split_far, far, rank)
-    gots = [send(value, message) for value, message in zip(coeffs, far)]
-    coeffs = next_coefficients(both, split_near, near, rank)
+    coeffs, cols, both = mixed_coefficients(mixed, split_one, one, rank)
     diag_part = diagonal(diag_tile, cols)
-    gots += send_near(coeffs, near, [gots[0], diag_part])
+    gots = send_all(coeffs, one, diag_part)
+    gots += send_all(next_coefficients(both, split_two, two, rank), two)
     return rows(offsets, ranks, gots, messages, left_split, diag_part, slots, halves, True)[None]
 
 

time: 52.7 us -> 51.9 us (0.985)
    ppermute x14, waiting for transfers between devices: 9.92 us -> 9.11 us  [send(): return lax.ppermute(value, 'tile', message.pairs)]
    ppermute x14, starting transfers between devices: 21.3 us -> 20.5 us  [send(): return lax.ppermute(value, 'tile', message.pairs)]
    ppermute x2, waiting for transfers between devices: 2.23 us -> 2.77 us  [mix(): lax.ppermute(part, axes, pairs)]
  transfers between devices with their start and end apart: 18 -> 18, of which waited for: 7 -> 6; matrix products, arithmetic and copies ran while one was open for 0% -> 0% of each run, Pallas kernels for 6% -> 7%
where the time goes in v3:
time: 51.9 us; the launch traced here: 51.7 us
  starting transfers between devices  26.7 us (51%)
  waiting for transfers between devices  15.4 us (30%)
  Pallas kernels  9.42 us (18%)
    ppermute x14, starting transfers between devices, send(): return lax.ppermute(value, 'tile', message.pairs)  20.5 us
    ppermute x14, waiting for transfers between devices, send(): return lax.ppermute(value, 'tile', message.pairs)  9.11 us
    ppermute x2, waiting for transfers between devices, mix(): lax.ppermute(send, axes, pairs)  3.49 us
    pallas_call x2, Pallas kernels, rows(): call(functools.partial(row_kernel, messages, halves, final), pltpu.HBM((s...  3.26 us
    ppermute x2, starting transfers between devices, mix(): lax.ppermute(send, axes, pairs)  3.13 us
    ppermute x2, starting transfers between devices, mix(): lax.ppermute(part, axes, pairs)  3.08 us
    ppermute x2, waiting for transfers between devices, mix(): lax.ppermute(part, axes, pairs)  2.77 us
    pallas_call x1, Pallas kernels, prepare(): call(functools.partial(prepare_kernel, halves), [struct(size, width), str...  2.21 us
  transfers between devices with their start and end apart: 18, of which 6 were waited for; matrix products, arithmetic and copies ran while one was open for 0% of the time, Pallas kernels for 7%

profile of v3, /device:TPU:0, one launch (start us, length us, event | category | flops | bytes accessed | tf_op | source)
XLA Modules:
  0.0 51.7 jit_solution(9626120149977718863)
XLA Ops:
  0.0 2.0 %shard_map.82 = (f32[2,80,128]{2,1,0:T(8,128)S(1)}, f32[1,80,128]{2,1,0:T(8,128)S(1)}, f32[1,80,128]{2,1,0:T(8,128)S(1)}, bf16[640,512]{1,0:T(8,128)(2,1)S(1)}, ...) custom-call(f32[512,128]{1,0:T(8,128)} %bitcast.21, f32[12,80,512]{2,1,0:T(8,128)} %bitcast.19), custom_call_target="tpu_custom_call" | custom-call | flops 167772160 | bytes 1966080 | tf_op jit(solution)/shard_map/pallas_call | solution.py:161
  2.0 4.6 %collective-permute-start.1 = (f32[1,80,128]{2,1,0:T(8,128)S(1)}, f32[1,80,128]{2,1,0:T(8,128)S(1)}, u32[]{:S(2)}, u32[]{:S(2)}) collective-permute-start(f32[1,80,128]{2,1,0:T(8,128)S(1)} %get-tuple-element.35), channel_id=1, source_target_pairs={{0,7},{1,2},{2,1},{3,4},{4,3},{5,6},{6,5},{7,0},{8,15},{9,10},{10,... | collective-permute-start | bytes 122888 | tf_op jit(solution)/shard_map/ppermute | solution.py:474
  6.5 1.2 %collective-permute-start = (f32[2,80,128]{2,1,0:T(8,128)S(1)}, f32[2,80,128]{2,1,0:T(8,128)S(1)}, u32[]{:S(2)}, u32[]{:S(2)}) collective-permute-start(f32[2,80,128]{2,1,0:T(8,128)S(1)} %get-tuple-element.34), channel_id=1, source_target_pairs={{0,4},{1,5},{2,6},{3,7},{4,0},{5,1},{6,2},{7,3},{8,12},{9,13},{10,... | collective-permute-start | bytes 245768 | tf_op jit(solution)/shard_map/ppermute | solution.py:474
  7.8 0.6 %shard_map.83 = (f32[2,80,128]{2,1,0:T(8,128)S(1)}, f32[2,80,128]{2,1,0:T(8,128)S(1)}, f32[2,80,128]{2,1,0:T(8,128)S(1)}, f32[2,80,128]{2,1,0:T(8,128)S(1)}, bf16[1280,512]{1,0:T(8,128)(2,1)S(1)}) custom-call(bf16[512,256]{1,0:T(8,128)(2,1)S(1)} %get-tuple-element.37.both_ref, f32[8,80,512]{2,1,0:T(8,128)S(1)} %get-tuple-element.38.right_ref), custom_call_target="tpu_custom_call" | custom-call | flops 335544320 | bytes 2621440 | tf_op jit(solution)/shard_map/pallas_call | solution.py:190
  8.4 1.6 %collective-permute-start.3 = (f32[2,80,128]{2,1,0:T(8,128)S(1)}, f32[2,80,128]{2,1,0:T(8,128)S(1)}, u32[]{:S(2)}, u32[]{:S(2)}) collective-permute-start(f32[2,80,128]{2,1,0:T(8,128)S(1)} %get-tuple-element.39), channel_id=1, source_target_pairs={{0,5},{1,6},{2,7},{3,0},{4,1},{5,2},{6,3},{7,4},{8,13},{9,14},{10,... | collective-permute-start | bytes 245768 | tf_op jit(solution)/shard_map/ppermute | solution.py:474
  10.2 3.1 %collective-permute-start.5 = (f32[2,80,128]{2,1,0:T(8,128)S(1)}, f32[2,80,128]{2,1,0:T(8,128)S(1)}, u32[]{:S(2)}, u32[]{:S(2)}) collective-permute-start(f32[2,80,128]{2,1,0:T(8,128)S(1)} %get-tuple-element.41), channel_id=1, source_target_pairs={{0,6},{1,7},{2,0},{3,1},{4,2},{5,3},{6,4},{7,5},{8,14},{9,15},{10,... | collective-permute-start | bytes 245768 | tf_op jit(solution)/shard_map/ppermute | solution.py:474
  13.4 2.2 %shard_map.84 = (f32[512,128]{1,0:T(8,128)S(1)}, bf16[1024,640]{1,0:T(8,128)(2,1)S(1)}, f32[8,256,128]{2,1,0:T(8,128)S(1)}) custom-call(f32[512,512]{1,0:T(8,128)} %bitcast.11, f32[512,128]{1,0:T(8,128)} %bitcast.22, f32[640,512]{1,0:T(8,128)} %bitcast.20, f32[16,64]{1,0:T(8,128)S(1)} %bitcast.13, s32[1,512]{1,0:T(1,128)S(1)} %bitcast.14), custom_call_target="tpu_custom_call" | custom-call | flops 268435456 | bytes 4194304 | tf_op jit(solution)/shard_map/pallas_call | solution.py:385
  15.6 5.4 %collective-permute-done.4.refs_4_ = f32[2,80,128]{2,1,0:T(8,128)S(1)} collective-permute-done((f32[2,80,128]{2,1,0:T(8,128)S(1)}, f32[2,80,128]{2,1,0:T(8,128)S(1)}, u32[]{:S(2)}, u32[]{:S(2)}) %collective-permute-start.4) | collective-permute-done | bytes 81952 | tf_op jit(solution)/shard_map/ppermute | solution.py:474
  21.0 1.3 %shard_map.85 = (f32[256,128]{1,0:T(8,128)S(1)}, f32[256,128]{1,0:T(8,128)S(1)}) custom-call(s32[1,8]{1,0:T(1,128)S(1)} %bitcast.15, s32[1,8]{1,0:T(1,128)S(1)} %bitcast.17, f32[2,80,128]{2,1,0:T(8,128)S(1)} %collective-permute-done.refs_0_, f32[1,80,128]{2,1,0:T(8,128)S(1)} %collective-permute-done.1.refs_1_, ...), custom_call_target="tpu_custom_call" | custom-call | flops 335544320 | bytes 1638400 | tf_op jit(solution)/shard_map/pallas_call | solution.py:462
  22.3 1.6 %collective-permute-start.7 = (f32[256,128]{1,0:T(8,128)S(1)}, f32[256,128]{1,0:T(8,128)S(1)}, u32[]{:S(2)}, u32[]{:S(2)}) collective-permute-start(f32[256,128]{1,0:T(8,128)S(1)} %get-tuple-element.45.own_ref), channel_id=1, source_target_pairs={{0,8},{1,17},{2,10},{3,19},{4,12},{5,21},{6,14},{7,23},{8,0},{9,25... | collective-permute-start | bytes 393224 | tf_op jit(solution)/shard_map/ppermute | solution.py:233
  23.9 1.5 %collective-permute-start.9 = (f32[256,128]{1,0:T(8,128)S(1)}, f32[256,128]{1,0:T(8,128)S(1)}, u32[]{:S(2)}, u32[]{:S(2)}) collective-permute-start(f32[256,128]{1,0:T(8,128)S(1)} %get-tuple-element.49.own_ref), channel_id=1, source_target_pairs={{0,16},{1,9},{2,18},{3,11},{4,20},{5,13},{6,22},{7,15},{8,24},{9,1... | collective-permute-start | bytes 393224 | tf_op jit(solution)/shard_map/ppermute | solution.py:233
  25.4 2.8 %collective-permute-done.7.got_ref = f32[256,128]{1,0:T(8,128)S(1)} collective-permute-done((f32[256,128]{1,0:T(8,128)S(1)}, f32[256,128]{1,0:T(8,128)S(1)}, u32[]{:S(2)}, u32[]{:S(2)}) %collective-permute-start.7) | collective-permute-done | bytes 131104 | tf_op jit(solution)/shard_map/ppermute | solution.py:233
  28.2 1.6 %collective-permute-start.8 = (f32[256,128]{1,0:T(8,128)S(1)}, f32[256,128]{1,0:T(8,128)S(1)}, u32[]{:S(2)}, u32[]{:S(2)}) collective-permute-start(f32[256,128]{1,0:T(8,128)S(1)} %get-tuple-element.48), channel_id=1, source_target_pairs={{0,16},{1,9},{2,18},{3,11},{4,20},{5,13},{6,22},{7,15},{8,24},{9,1... | collective-permute-start | bytes 393224 | tf_op jit(solution)/shard_map/ppermute | solution.py:239
  29.9 1.5 %collective-permute-start.10 = (f32[256,128]{1,0:T(8,128)S(1)}, f32[256,128]{1,0:T(8,128)S(1)}, u32[]{:S(2)}, u32[]{:S(2)}) collective-permute-start(f32[256,128]{1,0:T(8,128)S(1)} %get-tuple-element.51), channel_id=1, source_target_pairs={{0,8},{1,17},{2,10},{3,19},{4,12},{5,21},{6,14},{7,23},{8,0},{9,25... | collective-permute-start | bytes 393224 | tf_op jit(solution)/shard_map/ppermute | solution.py:239
  31.4 1.8 %collective-permute-done.8.refs_1_ = f32[256,128]{1,0:T(8,128)S(1)} collective-permute-done((f32[256,128]{1,0:T(8,128)S(1)}, f32[256,128]{1,0:T(8,128)S(1)}, u32[]{:S(2)}, u32[]{:S(2)}) %collective-permute-start.8) | collective-permute-done | bytes 131104 | tf_op jit(solution)/shard_map/ppermute | solution.py:239
  33.2 1.7 %collective-permute-done.10.refs_3_ = f32[256,128]{1,0:T(8,128)S(1)} collective-permute-done((f32[256,128]{1,0:T(8,128)S(1)}, f32[256,128]{1,0:T(8,128)S(1)}, u32[]{:S(2)}, u32[]{:S(2)}) %collective-permute-start.10) | collective-permute-done | bytes 131104 | tf_op jit(solution)/shard_map/ppermute | solution.py:239
  35.3 1.3 %collective-permute-start.11 = (f32[2,80,128]{2,1,0:T(8,128)S(1)}, f32[2,80,128]{2,1,0:T(8,128)S(1)}, u32[]{:S(2)}, u32[]{:S(2)}) collective-permute-start(f32[2,80,128]{2,1,0:T(8,128)S(1)} %get-tuple-element.53), channel_id=1, source_target_pairs={{0,4},{1,5},{2,6},{3,7},{4,0},{5,1},{6,2},{7,3},{8,12},{9,13},{10,... | collective-permute-start | bytes 245768 | tf_op jit(solution)/shard_map/ppermute | solution.py:474
  36.5 0.5 shard_map.91
  37.1 1.9 %collective-permute-start.14 = (f32[2,80,128]{2,1,0:T(8,128)S(1)}, f32[2,80,128]{2,1,0:T(8,128)S(1)}, u32[]{:S(2)}, u32[]{:S(2)}) collective-permute-start(f32[2,80,128]{2,1,0:T(8,128)S(1)} %get-tuple-element.59), channel_id=1, source_target_pairs={{0,5},{1,6},{2,7},{3,0},{4,1},{5,2},{6,3},{7,4},{8,13},{9,14},{10,... | collective-permute-start | bytes 245768 | tf_op jit(solution)/shard_map/ppermute | solution.py:474
  38.9 4.1 %collective-permute-start.16 = (f32[2,80,128]{2,1,0:T(8,128)S(1)}, f32[2,80,128]{2,1,0:T(8,128)S(1)}, u32[]{:S(2)}, u32[]{:S(2)}) collective-permute-start(f32[2,80,128]{2,1,0:T(8,128)S(1)} %get-tuple-element.61), channel_id=1, source_target_pairs={{0,6},{1,7},{2,0},{3,1},{4,2},{5,3},{6,4},{7,5},{8,14},{9,15},{10,... | collective-permute-start | bytes 245768 | tf_op jit(solution)/shard_map/ppermute | solution.py:474
  43.5 2.5 %collective-permute-start.12 = (f32[1,80,128]{2,1,0:T(8,128)S(1)}, f32[1,80,128]{2,1,0:T(8,128)S(1)}, u32[]{:S(2)}, u32[]{:S(2)}) collective-permute-start(f32[1,80,128]{2,1,0:T(8,128)S(1)} %shard_map.90), channel_id=1, source_target_pairs={{0,7},{1,2},{2,1},{3,4},{4,3},{5,6},{6,5},{7,0},{8,15},{9,10},{10,... | collective-permute-start | bytes 122888 | tf_op jit(solution)/shard_map/ppermute | solution.py:474
  46.0 2.1 %collective-permute-done.15.refs_4_ = f32[2,80,128]{2,1,0:T(8,128)S(1)} collective-permute-done((f32[2,80,128]{2,1,0:T(8,128)S(1)}, f32[2,80,128]{2,1,0:T(8,128)S(1)}, u32[]{:S(2)}, u32[]{:S(2)}) %collective-permute-start.15) | collective-permute-done | bytes 81952 | tf_op jit(solution)/shard_map/ppermute | solution.py:474
  48.1 1.6 %collective-permute-done.17.refs_6_ = f32[2,80,128]{2,1,0:T(8,128)S(1)} collective-permute-done((f32[2,80,128]{2,1,0:T(8,128)S(1)}, f32[2,80,128]{2,1,0:T(8,128)S(1)}, u32[]{:S(2)}, u32[]{:S(2)}) %collective-permute-start.17) | collective-permute-done | bytes 81952 | tf_op jit(solution)/shard_map/ppermute | solution.py:474
  49.7 2.0 %shard_map.92 = f32[512,128]{1,0:T(8,128)} custom-call(s32[1,8]{1,0:T(1,128)S(1)} %bitcast.16, s32[1,8]{1,0:T(1,128)S(1)} %bitcast.18, f32[2,80,128]{2,1,0:T(8,128)S(1)} %collective-permute-done.11.refs_1_.refs_0_, f32[1,80,128]{2,1,0:T(8,128)S(1)} %collective-permute-done.12.refs_1_, f32[1,80,128]{2,1,0:T(8,128)S(1)} %collective-permute-done.13.refs_2_, ...), custom_call_target="tpu_custom_call" | custom-call | flops 335544320 | bytes 1638400 | tf_op jit(solution)/shard_map/pallas_call | solution.py:462
  (33 shorter events, 1.2 us)
Async XLA Ops:
  2.0 11.4 %copy-start.1 = (f32[64,4,4]{0,2,1:T(4,128)S(1)}, f32[64,4,4]{0,2,1:T(4,128)}, u32[]{:S(2)}) copy-start(f32[64,4,4]{0,2,1:T(4,128)} %param.13) | copy-start | bytes 12292
  2.0 11.4 %copy-start.2 = (s32[512]{0:T(512)S(1)}, s32[512]{0:T(512)}, u32[]{:S(2)}) copy-start(s32[512]{0:T(512)} %param.14) | copy-start | bytes 6148
  2.0 8.2 %collective-permute-start.1 = (f32[1,80,128]{2,1,0:T(8,128)S(1)}, f32[1,80,128]{2,1,0:T(8,128)S(1)}, u32[]{:S(2)}, u32[]{:S(2)}) collective-permute-start(f32[1,80,128]{2,1,0:T(8,128)S(1)} %get-tuple-element.35), channel_id=1, source_target_pairs={{0,7},{1,2},{2,1},{3,4},{4,3},{5,6},{6,5},{7,0},{8,15},{9,10},{10,... | collective-permute-start | bytes 122888 | tf_op jit(solution)/shard_map/ppermute | solution.py:474
  6.5 6.8 %collective-permute-start.2 = (f32[1,80,128]{2,1,0:T(8,128)S(1)}, f32[1,80,128]{2,1,0:T(8,128)S(1)}, u32[]{:S(2)}, u32[]{:S(2)}) collective-permute-start(f32[1,80,128]{2,1,0:T(8,128)S(1)} %get-tuple-element.36), channel_id=1, source_target_pairs={{0,1},{1,0},{2,3},{3,2},{4,5},{5,4},{6,7},{7,6},{8,9},{9,8},{10,11... | collective-permute-start | bytes 122888 | tf_op jit(solution)/shard_map/ppermute | solution.py:474
  6.5 9.0 %collective-permute-start = (f32[2,80,128]{2,1,0:T(8,128)S(1)}, f32[2,80,128]{2,1,0:T(8,128)S(1)}, u32[]{:S(2)}, u32[]{:S(2)}) collective-permute-start(f32[2,80,128]{2,1,0:T(8,128)S(1)} %get-tuple-element.34), channel_id=1, source_target_pairs={{0,4},{1,5},{2,6},{3,7},{4,0},{5,1},{6,2},{7,3},{8,12},{9,13},{10,... | collective-permute-start | bytes 245768 | tf_op jit(solution)/shard_map/ppermute | solution.py:474
  8.4 7.2 %collective-permute-start.3 = (f32[2,80,128]{2,1,0:T(8,128)S(1)}, f32[2,80,128]{2,1,0:T(8,128)S(1)}, u32[]{:S(2)}, u32[]{:S(2)}) collective-permute-start(f32[2,80,128]{2,1,0:T(8,128)S(1)} %get-tuple-element.39), channel_id=1, source_target_pairs={{0,5},{1,6},{2,7},{3,0},{4,1},{5,2},{6,3},{7,4},{8,13},{9,14},{10,... | collective-permute-start | bytes 245768 | tf_op jit(solution)/shard_map/ppermute | solution.py:474
  9.9 11.1 %collective-permute-start.4 = (f32[2,80,128]{2,1,0:T(8,128)S(1)}, f32[2,80,128]{2,1,0:T(8,128)S(1)}, u32[]{:S(2)}, u32[]{:S(2)}) collective-permute-start(f32[2,80,128]{2,1,0:T(8,128)S(1)} %get-tuple-element.40), channel_id=1, source_target_pairs={{0,3},{1,4},{2,5},{3,6},{4,7},{5,0},{6,1},{7,2},{8,11},{9,12},{10,... | collective-permute-start | bytes 245768 | tf_op jit(solution)/shard_map/ppermute | solution.py:474
  10.2 10.8 %collective-permute-start.5 = (f32[2,80,128]{2,1,0:T(8,128)S(1)}, f32[2,80,128]{2,1,0:T(8,128)S(1)}, u32[]{:S(2)}, u32[]{:S(2)}) collective-permute-start(f32[2,80,128]{2,1,0:T(8,128)S(1)} %get-tuple-element.41), channel_id=1, source_target_pairs={{0,6},{1,7},{2,0},{3,1},{4,2},{5,3},{6,4},{7,5},{8,14},{9,15},{10,... | collective-permute-start | bytes 245768 | tf_op jit(solution)/shard_map/ppermute | solution.py:474
  13.3 7.7 %collective-permute-start.6 = (f32[2,80,128]{2,1,0:T(8,128)S(1)}, f32[2,80,128]{2,1,0:T(8,128)S(1)}, u32[]{:S(2)}, u32[]{:S(2)}) collective-permute-start(f32[2,80,128]{2,1,0:T(8,128)S(1)} %get-tuple-element.42), channel_id=1, source_target_pairs={{0,2},{1,3},{2,4},{3,5},{4,6},{5,7},{6,0},{7,1},{8,10},{9,11},{10,... | collective-permute-start | bytes 245768 | tf_op jit(solution)/shard_map/ppermute | solution.py:474
  13.3 7.7 %copy-start.3 = (s32[1,1,8]{2,1,0:T(1,128)S(1)}, s32[1,1,8]{2,1,0:T(1,128)}, u32[]{:S(2)}) copy-start(s32[1,1,8]{2,1,0:T(1,128)} %param.11) | copy-start | bytes 100
  13.3 7.7 %copy-start.4 = (s32[1,1,8]{2,1,0:T(1,128)S(1)}, s32[1,1,8]{2,1,0:T(1,128)}, u32[]{:S(2)}) copy-start(s32[1,1,8]{2,1,0:T(1,128)} %param.12) | copy-start | bytes 100
  22.3 5.8 %collective-permute-start.7 = (f32[256,128]{1,0:T(8,128)S(1)}, f32[256,128]{1,0:T(8,128)S(1)}, u32[]{:S(2)}, u32[]{:S(2)}) collective-permute-start(f32[256,128]{1,0:T(8,128)S(1)} %get-tuple-element.45.own_ref), channel_id=1, source_target_pairs={{0,8},{1,17},{2,10},{3,19},{4,12},{5,21},{6,14},{7,23},{8,0},{9,25... | collective-permute-start | bytes 393224 | tf_op jit(solution)/shard_map/ppermute | solution.py:233
  23.9 5.9 %collective-permute-start.9 = (f32[256,128]{1,0:T(8,128)S(1)}, f32[256,128]{1,0:T(8,128)S(1)}, u32[]{:S(2)}, u32[]{:S(2)}) collective-permute-start(f32[256,128]{1,0:T(8,128)S(1)} %get-tuple-element.49.own_ref), channel_id=1, source_target_pairs={{0,16},{1,9},{2,18},{3,11},{4,20},{5,13},{6,22},{7,15},{8,24},{9,1... | collective-permute-start | bytes 393224 | tf_op jit(solution)/shard_map/ppermute | solution.py:233
  28.2 5.0 %collective-permute-start.8 = (f32[256,128]{1,0:T(8,128)S(1)}, f32[256,128]{1,0:T(8,128)S(1)}, u32[]{:S(2)}, u32[]{:S(2)}) collective-permute-start(f32[256,128]{1,0:T(8,128)S(1)} %get-tuple-element.48), channel_id=1, source_target_pairs={{0,16},{1,9},{2,18},{3,11},{4,20},{5,13},{6,22},{7,15},{8,24},{9,1... | collective-permute-start | bytes 393224 | tf_op jit(solution)/shard_map/ppermute | solution.py:239
  29.9 5.0 %collective-permute-start.10 = (f32[256,128]{1,0:T(8,128)S(1)}, f32[256,128]{1,0:T(8,128)S(1)}, u32[]{:S(2)}, u32[]{:S(2)}) collective-permute-start(f32[256,128]{1,0:T(8,128)S(1)} %get-tuple-element.51), channel_id=1, source_target_pairs={{0,8},{1,17},{2,10},{3,19},{4,12},{5,21},{6,14},{7,23},{8,0},{9,25... | collective-permute-start | bytes 393224 | tf_op jit(solution)/shard_map/ppermute | solution.py:239
  34.9 8.1 %copy-start = (f32[1,1,512,512]{3,2,1,0:T(8,128)S(1)}, f32[1,1,512,512]{3,2,1,0:T(8,128)}, u32[]{:S(2)}) copy-start(f32[1,1,512,512]{3,2,1,0:T(8,128)} %param.8) | copy-start | bytes 3145732
  35.3 7.7 %collective-permute-start.11 = (f32[2,80,128]{2,1,0:T(8,128)S(1)}, f32[2,80,128]{2,1,0:T(8,128)S(1)}, u32[]{:S(2)}, u32[]{:S(2)}) collective-permute-start(f32[2,80,128]{2,1,0:T(8,128)S(1)} %get-tuple-element.53), channel_id=1, source_target_pairs={{0,4},{1,5},{2,6},{3,7},{4,0},{5,1},{6,2},{7,3},{8,12},{9,13},{10,... | collective-permute-start | bytes 245768 | tf_op jit(solution)/shard_map/ppermute | solution.py:474
  36.5 6.9 %collective-permute-start.13 = (f32[1,80,128]{2,1,0:T(8,128)S(1)}, f32[1,80,128]{2,1,0:T(8,128)S(1)}, u32[]{:S(2)}, u32[]{:S(2)}) collective-permute-start(f32[1,80,128]{2,1,0:T(8,128)S(1)} %get-tuple-element.56), channel_id=1, source_target_pairs={{0,1},{1,0},{2,3},{3,2},{4,5},{5,4},{6,7},{7,6},{8,9},{9,8},{10,11... | collective-permute-start | bytes 122888 | tf_op jit(solution)/shard_map/ppermute | solution.py:474
  37.1 9.0 %collective-permute-start.14 = (f32[2,80,128]{2,1,0:T(8,128)S(1)}, f32[2,80,128]{2,1,0:T(8,128)S(1)}, u32[]{:S(2)}, u32[]{:S(2)}) collective-permute-start(f32[2,80,128]{2,1,0:T(8,128)S(1)} %get-tuple-element.59), channel_id=1, source_target_pairs={{0,5},{1,6},{2,7},{3,0},{4,1},{5,2},{6,3},{7,4},{8,13},{9,14},{10,... | collective-permute-start | bytes 245768 | tf_op jit(solution)/shard_map/ppermute | solution.py:474
  38.9 9.2 %collective-permute-start.15 = (f32[2,80,128]{2,1,0:T(8,128)S(1)}, f32[2,80,128]{2,1,0:T(8,128)S(1)}, u32[]{:S(2)}, u32[]{:S(2)}) collective-permute-start(f32[2,80,128]{2,1,0:T(8,128)S(1)} %get-tuple-element.60), channel_id=1, source_target_pairs={{0,3},{1,4},{2,5},{3,6},{4,7},{5,0},{6,1},{7,2},{8,11},{9,12},{10,... | collective-permute-start | bytes 245768 | tf_op jit(solution)/shard_map/ppermute | solution.py:474
  38.9 9.2 %collective-permute-start.16 = (f32[2,80,128]{2,1,0:T(8,128)S(1)}, f32[2,80,128]{2,1,0:T(8,128)S(1)}, u32[]{:S(2)}, u32[]{:S(2)}) collective-permute-start(f32[2,80,128]{2,1,0:T(8,128)S(1)} %get-tuple-element.61), channel_id=1, source_target_pairs={{0,6},{1,7},{2,0},{3,1},{4,2},{5,3},{6,4},{7,5},{8,14},{9,15},{10,... | collective-permute-start | bytes 245768 | tf_op jit(solution)/shard_map/ppermute | solution.py:474
  43.0 6.7 %collective-permute-start.17 = (f32[2,80,128]{2,1,0:T(8,128)S(1)}, f32[2,80,128]{2,1,0:T(8,128)S(1)}, u32[]{:S(2)}, u32[]{:S(2)}) collective-permute-start(f32[2,80,128]{2,1,0:T(8,128)S(1)} %get-tuple-element.62), channel_id=1, source_target_pairs={{0,2},{1,3},{2,4},{3,5},{4,6},{5,7},{6,0},{7,1},{8,10},{9,11},{10,... | collective-permute-start | bytes 245768 | tf_op jit(solution)/shard_map/ppermute | solution.py:474
  43.5 6.2 %collective-permute-start.12 = (f32[1,80,128]{2,1,0:T(8,128)S(1)}, f32[1,80,128]{2,1,0:T(8,128)S(1)}, u32[]{:S(2)}, u32[]{:S(2)}) collective-permute-start(f32[1,80,128]{2,1,0:T(8,128)S(1)} %shard_map.90), channel_id=1, source_target_pairs={{0,7},{1,2},{2,1},{3,4},{4,3},{5,6},{6,5},{7,0},{8,15},{9,10},{10,... | collective-permute-start | bytes 122888 | tf_op jit(solution)/shard_map/ppermute | solution.py:474

commit v4 on v3

--- a/solution.py
+++ b/solution.py
@@ -416,24 +416,23 @@
     slots = term_of.shape[0]
     reach = slots // 2
     for slot in range(slots):
-        term_of[slot] = -1
+        term_of[slot] = terms
     for k in range(terms):
         offset = offs_ref[0, k]
         term_of[jnp.where(offset < 0, offset + reach, offset + reach - 1)] = k
     line = lax.broadcasted_iota(jnp.int32, (rank, width), 0)
 
     def pick(got, w, term):
-        @pl.when(term >= 0)
-        def _():
-            kept = jnp.where(line < ranks_ref[0, term], got[w], 0.0)
-            picked[pl.ds(pl.multiple_of(term * rank, rank), rank)] = kept
+        last = ranks_ref[0, jnp.minimum(term, terms - 1)]
+        kept = jnp.where(line < last, got[w], 0.0)
+        picked[pl.ds(pl.multiple_of(term * rank, rank), rank)] = kept
 
     for got, message in zip(gots, messages):
         for w, slot in enumerate(message.slots):
             if message.odd_slots is not None:
                 slot = jnp.where((lax.axis_index("tile") & 1) == 1, slot, message.odd_slots[w])
             pick(got, w, term_of[slot])
-    both = side_by_side(picked[...])
+    both = side_by_side(picked[: terms * rank])
     part = diag_ref.shape[0] // halves
     sent = []
     got = fold(dot(left_ref[...], both))
@@ -456,7 +455,8 @@
 def rows(offsets, ranks, gots, messages, left_split, diag_part, slots, halves, final):
     size, width = diag_part.shape
     total = left_split.shape[1]
-    scratch = [pltpu.VMEM((total, width), f32), pltpu.SMEM((slots,), jnp.int32)]
+    rank = gots[0].shape[1]
+    scratch = [pltpu.VMEM((total + rank, width), f32), pltpu.SMEM((slots,), jnp.int32)]
     if final:
         scratch += [pltpu.VMEM((size, width), f32), pltpu.SemaphoreType.DMA((halves,))]
     return call(

time: 51.9 us -> 51.7 us (level)
  transfers between devices with their start and end apart: 18 -> 18, of which waited for: 6 -> 6; matrix products, arithmetic and copies ran while one was open for 0% -> 0% of each run, Pallas kernels for 7% -> 8%
where the time goes in v4:
time: 51.7 us; the launch traced here: 51.5 us
  starting transfers between devices  26.7 us (52%)
  waiting for transfers between devices  15.4 us (30%)
  Pallas kernels  9.27 us (18%)
    ppermute x14, starting transfers between devices, send(): return lax.ppermute(value, 'tile', message.pairs)  20.5 us
    ppermute x14, waiting for transfers between devices, send(): return lax.ppermute(value, 'tile', message.pairs)  9.13 us
    ppermute x2, waiting for transfers between devices, mix(): lax.ppermute(send, axes, pairs)  3.49 us
    ppermute x2, starting transfers between devices, mix(): lax.ppermute(send, axes, pairs)  3.13 us
    pallas_call x2, Pallas kernels, rows(): call(functools.partial(row_kernel, messages, halves, final), pltpu.HBM((s...  3.1 us
    ppermute x2, starting transfers between devices, mix(): lax.ppermute(part, axes, pairs)  3.08 us
    ppermute x2, waiting for transfers between devices, mix(): lax.ppermute(part, axes, pairs)  2.77 us
    pallas_call x1, Pallas kernels, prepare(): call(functools.partial(prepare_kernel, halves), [struct(size, width), str...  2.21 us
  transfers between devices with their start and end apart: 18, of which 6 were waited for; matrix products, arithmetic and copies ran while one was open for 0% of the time, Pallas kernels for 8%

profile of v4, /device:TPU:0, one launch (start us, length us, event | category | flops | bytes accessed | tf_op | source)
XLA Modules:
  0.0 51.5 jit_solution(1686387572505213567)
XLA Ops:
  0.0 2.0 %shard_map.82 = (f32[2,80,128]{2,1,0:T(8,128)S(1)}, f32[1,80,128]{2,1,0:T(8,128)S(1)}, f32[1,80,128]{2,1,0:T(8,128)S(1)}, bf16[640,512]{1,0:T(8,128)(2,1)S(1)}, ...) custom-call(f32[512,128]{1,0:T(8,128)} %bitcast.21, f32[12,80,512]{2,1,0:T(8,128)} %bitcast.19), custom_call_target="tpu_custom_call" | custom-call | flops 167772160 | bytes 1966080 | tf_op jit(solution)/shard_map/pallas_call | solution.py:161
  2.0 4.6 %collective-permute-start.1 = (f32[1,80,128]{2,1,0:T(8,128)S(1)}, f32[1,80,128]{2,1,0:T(8,128)S(1)}, u32[]{:S(2)}, u32[]{:S(2)}) collective-permute-start(f32[1,80,128]{2,1,0:T(8,128)S(1)} %get-tuple-element.35), channel_id=1, source_target_pairs={{0,7},{1,2},{2,1},{3,4},{4,3},{5,6},{6,5},{7,0},{8,15},{9,10},{10,... | collective-permute-start | bytes 122888 | tf_op jit(solution)/shard_map/ppermute | solution.py:474
  6.5 1.2 %collective-permute-start = (f32[2,80,128]{2,1,0:T(8,128)S(1)}, f32[2,80,128]{2,1,0:T(8,128)S(1)}, u32[]{:S(2)}, u32[]{:S(2)}) collective-permute-start(f32[2,80,128]{2,1,0:T(8,128)S(1)} %get-tuple-element.34), channel_id=1, source_target_pairs={{0,4},{1,5},{2,6},{3,7},{4,0},{5,1},{6,2},{7,3},{8,12},{9,13},{10,... | collective-permute-start | bytes 245768 | tf_op jit(solution)/shard_map/ppermute | solution.py:474
  7.8 0.6 %shard_map.83 = (f32[2,80,128]{2,1,0:T(8,128)S(1)}, f32[2,80,128]{2,1,0:T(8,128)S(1)}, f32[2,80,128]{2,1,0:T(8,128)S(1)}, f32[2,80,128]{2,1,0:T(8,128)S(1)}, bf16[1280,512]{1,0:T(8,128)(2,1)S(1)}) custom-call(bf16[512,256]{1,0:T(8,128)(2,1)S(1)} %get-tuple-element.37.both_ref, f32[8,80,512]{2,1,0:T(8,128)S(1)} %get-tuple-element.38.right_ref), custom_call_target="tpu_custom_call" | custom-call | flops 335544320 | bytes 2621440 | tf_op jit(solution)/shard_map/pallas_call | solution.py:190
  8.4 1.6 %collective-permute-start.3 = (f32[2,80,128]{2,1,0:T(8,128)S(1)}, f32[2,80,128]{2,1,0:T(8,128)S(1)}, u32[]{:S(2)}, u32[]{:S(2)}) collective-permute-start(f32[2,80,128]{2,1,0:T(8,128)S(1)} %get-tuple-element.39), channel_id=1, source_target_pairs={{0,5},{1,6},{2,7},{3,0},{4,1},{5,2},{6,3},{7,4},{8,13},{9,14},{10,... | collective-permute-start | bytes 245768 | tf_op jit(solution)/shard_map/ppermute | solution.py:474
  10.2 3.1 %collective-permute-start.5 = (f32[2,80,128]{2,1,0:T(8,128)S(1)}, f32[2,80,128]{2,1,0:T(8,128)S(1)}, u32[]{:S(2)}, u32[]{:S(2)}) collective-permute-start(f32[2,80,128]{2,1,0:T(8,128)S(1)} %get-tuple-element.41), channel_id=1, source_target_pairs={{0,6},{1,7},{2,0},{3,1},{4,2},{5,3},{6,4},{7,5},{8,14},{9,15},{10,... | collective-permute-start | bytes 245768 | tf_op jit(solution)/shard_map/ppermute | solution.py:474
  13.4 2.2 %shard_map.84 = (f32[512,128]{1,0:T(8,128)S(1)}, bf16[1024,640]{1,0:T(8,128)(2,1)S(1)}, f32[8,256,128]{2,1,0:T(8,128)S(1)}) custom-call(f32[512,512]{1,0:T(8,128)} %bitcast.11, f32[512,128]{1,0:T(8,128)} %bitcast.22, f32[640,512]{1,0:T(8,128)} %bitcast.20, f32[16,64]{1,0:T(8,128)S(1)} %bitcast.13, s32[1,512]{1,0:T(1,128)S(1)} %bitcast.14), custom_call_target="tpu_custom_call" | custom-call | flops 268435456 | bytes 4194304 | tf_op jit(solution)/shard_map/pallas_call | solution.py:385
  15.6 5.4 %collective-permute-done.4.refs_4_ = f32[2,80,128]{2,1,0:T(8,128)S(1)} collective-permute-done((f32[2,80,128]{2,1,0:T(8,128)S(1)}, f32[2,80,128]{2,1,0:T(8,128)S(1)}, u32[]{:S(2)}, u32[]{:S(2)}) %collective-permute-start.4) | collective-permute-done | bytes 81952 | tf_op jit(solution)/shard_map/ppermute | solution.py:474
  21.0 1.2 %shard_map.85 = (f32[256,128]{1,0:T(8,128)S(1)}, f32[256,128]{1,0:T(8,128)S(1)}) custom-call(s32[1,8]{1,0:T(1,128)S(1)} %bitcast.15, s32[1,8]{1,0:T(1,128)S(1)} %bitcast.17, f32[2,80,128]{2,1,0:T(8,128)S(1)} %collective-permute-done.refs_0_, f32[1,80,128]{2,1,0:T(8,128)S(1)} %collective-permute-done.1.refs_1_, ...), custom_call_target="tpu_custom_call" | custom-call | flops 335544320 | bytes 1638400 | tf_op jit(solution)/shard_map/pallas_call | solution.py:462
  22.3 1.5 %collective-permute-start.7 = (f32[256,128]{1,0:T(8,128)S(1)}, f32[256,128]{1,0:T(8,128)S(1)}, u32[]{:S(2)}, u32[]{:S(2)}) collective-permute-start(f32[256,128]{1,0:T(8,128)S(1)} %get-tuple-element.45.own_ref), channel_id=1, source_target_pairs={{0,8},{1,17},{2,10},{3,19},{4,12},{5,21},{6,14},{7,23},{8,0},{9,25... | collective-permute-start | bytes 393224 | tf_op jit(solution)/shard_map/ppermute | solution.py:233
  23.8 1.5 %collective-permute-start.9 = (f32[256,128]{1,0:T(8,128)S(1)}, f32[256,128]{1,0:T(8,128)S(1)}, u32[]{:S(2)}, u32[]{:S(2)}) collective-permute-start(f32[256,128]{1,0:T(8,128)S(1)} %get-tuple-element.49.own_ref), channel_id=1, source_target_pairs={{0,16},{1,9},{2,18},{3,11},{4,20},{5,13},{6,22},{7,15},{8,24},{9,1... | collective-permute-start | bytes 393224 | tf_op jit(solution)/shard_map/ppermute | solution.py:233
  25.3 2.8 %collective-permute-done.7.got_ref = f32[256,128]{1,0:T(8,128)S(1)} collective-permute-done((f32[256,128]{1,0:T(8,128)S(1)}, f32[256,128]{1,0:T(8,128)S(1)}, u32[]{:S(2)}, u32[]{:S(2)}) %collective-permute-start.7) | collective-permute-done | bytes 131104 | tf_op jit(solution)/shard_map/ppermute | solution.py:233
  28.1 1.6 %collective-permute-start.8 = (f32[256,128]{1,0:T(8,128)S(1)}, f32[256,128]{1,0:T(8,128)S(1)}, u32[]{:S(2)}, u32[]{:S(2)}) collective-permute-start(f32[256,128]{1,0:T(8,128)S(1)} %get-tuple-element.48), channel_id=1, source_target_pairs={{0,16},{1,9},{2,18},{3,11},{4,20},{5,13},{6,22},{7,15},{8,24},{9,1... | collective-permute-start | bytes 393224 | tf_op jit(solution)/shard_map/ppermute | solution.py:239
  29.8 1.5 %collective-permute-start.10 = (f32[256,128]{1,0:T(8,128)S(1)}, f32[256,128]{1,0:T(8,128)S(1)}, u32[]{:S(2)}, u32[]{:S(2)}) collective-permute-start(f32[256,128]{1,0:T(8,128)S(1)} %get-tuple-element.51), channel_id=1, source_target_pairs={{0,8},{1,17},{2,10},{3,19},{4,12},{5,21},{6,14},{7,23},{8,0},{9,25... | collective-permute-start | bytes 393224 | tf_op jit(solution)/shard_map/ppermute | solution.py:239
  31.3 1.8 %collective-permute-done.8.refs_1_ = f32[256,128]{1,0:T(8,128)S(1)} collective-permute-done((f32[256,128]{1,0:T(8,128)S(1)}, f32[256,128]{1,0:T(8,128)S(1)}, u32[]{:S(2)}, u32[]{:S(2)}) %collective-permute-start.8) | collective-permute-done | bytes 131104 | tf_op jit(solution)/shard_map/ppermute | solution.py:239
  33.2 1.7 %collective-permute-done.10.refs_3_ = f32[256,128]{1,0:T(8,128)S(1)} collective-permute-done((f32[256,128]{1,0:T(8,128)S(1)}, f32[256,128]{1,0:T(8,128)S(1)}, u32[]{:S(2)}, u32[]{:S(2)}) %collective-permute-start.10) | collective-permute-done | bytes 131104 | tf_op jit(solution)/shard_map/ppermute | solution.py:239
  35.2 1.3 %collective-permute-start.11 = (f32[2,80,128]{2,1,0:T(8,128)S(1)}, f32[2,80,128]{2,1,0:T(8,128)S(1)}, u32[]{:S(2)}, u32[]{:S(2)}) collective-permute-start(f32[2,80,128]{2,1,0:T(8,128)S(1)} %get-tuple-element.53), channel_id=1, source_target_pairs={{0,4},{1,5},{2,6},{3,7},{4,0},{5,1},{6,2},{7,3},{8,12},{9,13},{10,... | collective-permute-start | bytes 245768 | tf_op jit(solution)/shard_map/ppermute | solution.py:474
  36.5 0.5 shard_map.91
  37.0 1.9 %collective-permute-start.14 = (f32[2,80,128]{2,1,0:T(8,128)S(1)}, f32[2,80,128]{2,1,0:T(8,128)S(1)}, u32[]{:S(2)}, u32[]{:S(2)}) collective-permute-start(f32[2,80,128]{2,1,0:T(8,128)S(1)} %get-tuple-element.59), channel_id=1, source_target_pairs={{0,5},{1,6},{2,7},{3,0},{4,1},{5,2},{6,3},{7,4},{8,13},{9,14},{10,... | collective-permute-start | bytes 245768 | tf_op jit(solution)/shard_map/ppermute | solution.py:474
  38.9 4.1 %collective-permute-start.16 = (f32[2,80,128]{2,1,0:T(8,128)S(1)}, f32[2,80,128]{2,1,0:T(8,128)S(1)}, u32[]{:S(2)}, u32[]{:S(2)}) collective-permute-start(f32[2,80,128]{2,1,0:T(8,128)S(1)} %get-tuple-element.61), channel_id=1, source_target_pairs={{0,6},{1,7},{2,0},{3,1},{4,2},{5,3},{6,4},{7,5},{8,14},{9,15},{10,... | collective-permute-start | bytes 245768 | tf_op jit(solution)/shard_map/ppermute | solution.py:474
  43.4 2.5 %collective-permute-start.12 = (f32[1,80,128]{2,1,0:T(8,128)S(1)}, f32[1,80,128]{2,1,0:T(8,128)S(1)}, u32[]{:S(2)}, u32[]{:S(2)}) collective-permute-start(f32[1,80,128]{2,1,0:T(8,128)S(1)} %shard_map.90), channel_id=1, source_target_pairs={{0,7},{1,2},{2,1},{3,4},{4,3},{5,6},{6,5},{7,0},{8,15},{9,10},{10,... | collective-permute-start | bytes 122888 | tf_op jit(solution)/shard_map/ppermute | solution.py:474
  46.0 2.1 %collective-permute-done.15.refs_4_ = f32[2,80,128]{2,1,0:T(8,128)S(1)} collective-permute-done((f32[2,80,128]{2,1,0:T(8,128)S(1)}, f32[2,80,128]{2,1,0:T(8,128)S(1)}, u32[]{:S(2)}, u32[]{:S(2)}) %collective-permute-start.15) | collective-permute-done | bytes 81952 | tf_op jit(solution)/shard_map/ppermute | solution.py:474
  48.0 1.6 %collective-permute-done.17.refs_6_ = f32[2,80,128]{2,1,0:T(8,128)S(1)} collective-permute-done((f32[2,80,128]{2,1,0:T(8,128)S(1)}, f32[2,80,128]{2,1,0:T(8,128)S(1)}, u32[]{:S(2)}, u32[]{:S(2)}) %collective-permute-start.17) | collective-permute-done | bytes 81952 | tf_op jit(solution)/shard_map/ppermute | solution.py:474
  49.6 1.9 %shard_map.92 = f32[512,128]{1,0:T(8,128)} custom-call(s32[1,8]{1,0:T(1,128)S(1)} %bitcast.16, s32[1,8]{1,0:T(1,128)S(1)} %bitcast.18, f32[2,80,128]{2,1,0:T(8,128)S(1)} %collective-permute-done.11.refs_1_.refs_0_, f32[1,80,128]{2,1,0:T(8,128)S(1)} %collective-permute-done.12.refs_1_, f32[1,80,128]{2,1,0:T(8,128)S(1)} %collective-permute-done.13.refs_2_, ...), custom_call_target="tpu_custom_call" | custom-call | flops 335544320 | bytes 1638400 | tf_op jit(solution)/shard_map/pallas_call | solution.py:462
  (33 shorter events, 1.2 us)
Async XLA Ops:
  2.0 11.4 %copy-start.1 = (f32[64,4,4]{0,2,1:T(4,128)S(1)}, f32[64,4,4]{0,2,1:T(4,128)}, u32[]{:S(2)}) copy-start(f32[64,4,4]{0,2,1:T(4,128)} %param.13) | copy-start | bytes 12292
  2.0 11.4 %copy-start.2 = (s32[512]{0:T(512)S(1)}, s32[512]{0:T(512)}, u32[]{:S(2)}) copy-start(s32[512]{0:T(512)} %param.14) | copy-start | bytes 6148
  2.0 8.2 %collective-permute-start.1 = (f32[1,80,128]{2,1,0:T(8,128)S(1)}, f32[1,80,128]{2,1,0:T(8,128)S(1)}, u32[]{:S(2)}, u32[]{:S(2)}) collective-permute-start(f32[1,80,128]{2,1,0:T(8,128)S(1)} %get-tuple-element.35), channel_id=1, source_target_pairs={{0,7},{1,2},{2,1},{3,4},{4,3},{5,6},{6,5},{7,0},{8,15},{9,10},{10,... | collective-permute-start | bytes 122888 | tf_op jit(solution)/shard_map/ppermute | solution.py:474
  6.5 6.8 %collective-permute-start.2 = (f32[1,80,128]{2,1,0:T(8,128)S(1)}, f32[1,80,128]{2,1,0:T(8,128)S(1)}, u32[]{:S(2)}, u32[]{:S(2)}) collective-permute-start(f32[1,80,128]{2,1,0:T(8,128)S(1)} %get-tuple-element.36), channel_id=1, source_target_pairs={{0,1},{1,0},{2,3},{3,2},{4,5},{5,4},{6,7},{7,6},{8,9},{9,8},{10,11... | collective-permute-start | bytes 122888 | tf_op jit(solution)/shard_map/ppermute | solution.py:474
  6.5 9.0 %collective-permute-start = (f32[2,80,128]{2,1,0:T(8,128)S(1)}, f32[2,80,128]{2,1,0:T(8,128)S(1)}, u32[]{:S(2)}, u32[]{:S(2)}) collective-permute-start(f32[2,80,128]{2,1,0:T(8,128)S(1)} %get-tuple-element.34), channel_id=1, source_target_pairs={{0,4},{1,5},{2,6},{3,7},{4,0},{5,1},{6,2},{7,3},{8,12},{9,13},{10,... | collective-permute-start | bytes 245768 | tf_op jit(solution)/shard_map/ppermute | solution.py:474
  8.4 7.2 %collective-permute-start.3 = (f32[2,80,128]{2,1,0:T(8,128)S(1)}, f32[2,80,128]{2,1,0:T(8,128)S(1)}, u32[]{:S(2)}, u32[]{:S(2)}) collective-permute-start(f32[2,80,128]{2,1,0:T(8,128)S(1)} %get-tuple-element.39), channel_id=1, source_target_pairs={{0,5},{1,6},{2,7},{3,0},{4,1},{5,2},{6,3},{7,4},{8,13},{9,14},{10,... | collective-permute-start | bytes 245768 | tf_op jit(solution)/shard_map/ppermute | solution.py:474
  9.9 11.1 %collective-permute-start.4 = (f32[2,80,128]{2,1,0:T(8,128)S(1)}, f32[2,80,128]{2,1,0:T(8,128)S(1)}, u32[]{:S(2)}, u32[]{:S(2)}) collective-permute-start(f32[2,80,128]{2,1,0:T(8,128)S(1)} %get-tuple-element.40), channel_id=1, source_target_pairs={{0,3},{1,4},{2,5},{3,6},{4,7},{5,0},{6,1},{7,2},{8,11},{9,12},{10,... | collective-permute-start | bytes 245768 | tf_op jit(solution)/shard_map/ppermute | solution.py:474
  10.2 10.8 %collective-permute-start.5 = (f32[2,80,128]{2,1,0:T(8,128)S(1)}, f32[2,80,128]{2,1,0:T(8,128)S(1)}, u32[]{:S(2)}, u32[]{:S(2)}) collective-permute-start(f32[2,80,128]{2,1,0:T(8,128)S(1)} %get-tuple-element.41), channel_id=1, source_target_pairs={{0,6},{1,7},{2,0},{3,1},{4,2},{5,3},{6,4},{7,5},{8,14},{9,15},{10,... | collective-permute-start | bytes 245768 | tf_op jit(solution)/shard_map/ppermute | solution.py:474
  13.3 7.7 %collective-permute-start.6 = (f32[2,80,128]{2,1,0:T(8,128)S(1)}, f32[2,80,128]{2,1,0:T(8,128)S(1)}, u32[]{:S(2)}, u32[]{:S(2)}) collective-permute-start(f32[2,80,128]{2,1,0:T(8,128)S(1)} %get-tuple-element.42), channel_id=1, source_target_pairs={{0,2},{1,3},{2,4},{3,5},{4,6},{5,7},{6,0},{7,1},{8,10},{9,11},{10,... | collective-permute-start | bytes 245768 | tf_op jit(solution)/shard_map/ppermute | solution.py:474
  13.3 7.7 %copy-start.3 = (s32[1,1,8]{2,1,0:T(1,128)S(1)}, s32[1,1,8]{2,1,0:T(1,128)}, u32[]{:S(2)}) copy-start(s32[1,1,8]{2,1,0:T(1,128)} %param.11) | copy-start | bytes 100
  13.3 7.7 %copy-start.4 = (s32[1,1,8]{2,1,0:T(1,128)S(1)}, s32[1,1,8]{2,1,0:T(1,128)}, u32[]{:S(2)}) copy-start(s32[1,1,8]{2,1,0:T(1,128)} %param.12) | copy-start | bytes 100
  22.3 5.8 %collective-permute-start.7 = (f32[256,128]{1,0:T(8,128)S(1)}, f32[256,128]{1,0:T(8,128)S(1)}, u32[]{:S(2)}, u32[]{:S(2)}) collective-permute-start(f32[256,128]{1,0:T(8,128)S(1)} %get-tuple-element.45.own_ref), channel_id=1, source_target_pairs={{0,8},{1,17},{2,10},{3,19},{4,12},{5,21},{6,14},{7,23},{8,0},{9,25... | collective-permute-start | bytes 393224 | tf_op jit(solution)/shard_map/ppermute | solution.py:233
  23.8 5.9 %collective-permute-start.9 = (f32[256,128]{1,0:T(8,128)S(1)}, f32[256,128]{1,0:T(8,128)S(1)}, u32[]{:S(2)}, u32[]{:S(2)}) collective-permute-start(f32[256,128]{1,0:T(8,128)S(1)} %get-tuple-element.49.own_ref), channel_id=1, source_target_pairs={{0,16},{1,9},{2,18},{3,11},{4,20},{5,13},{6,22},{7,15},{8,24},{9,1... | collective-permute-start | bytes 393224 | tf_op jit(solution)/shard_map/ppermute | solution.py:233
  28.1 5.0 %collective-permute-start.8 = (f32[256,128]{1,0:T(8,128)S(1)}, f32[256,128]{1,0:T(8,128)S(1)}, u32[]{:S(2)}, u32[]{:S(2)}) collective-permute-start(f32[256,128]{1,0:T(8,128)S(1)} %get-tuple-element.48), channel_id=1, source_target_pairs={{0,16},{1,9},{2,18},{3,11},{4,20},{5,13},{6,22},{7,15},{8,24},{9,1... | collective-permute-start | bytes 393224 | tf_op jit(solution)/shard_map/ppermute | solution.py:239
  29.8 5.0 %collective-permute-start.10 = (f32[256,128]{1,0:T(8,128)S(1)}, f32[256,128]{1,0:T(8,128)S(1)}, u32[]{:S(2)}, u32[]{:S(2)}) collective-permute-start(f32[256,128]{1,0:T(8,128)S(1)} %get-tuple-element.51), channel_id=1, source_target_pairs={{0,8},{1,17},{2,10},{3,19},{4,12},{5,21},{6,14},{7,23},{8,0},{9,25... | collective-permute-start | bytes 393224 | tf_op jit(solution)/shard_map/ppermute | solution.py:239
  34.8 8.1 %copy-start = (f32[1,1,512,512]{3,2,1,0:T(8,128)S(1)}, f32[1,1,512,512]{3,2,1,0:T(8,128)}, u32[]{:S(2)}) copy-start(f32[1,1,512,512]{3,2,1,0:T(8,128)} %param.8) | copy-start | bytes 3145732
  35.2 7.7 %collective-permute-start.11 = (f32[2,80,128]{2,1,0:T(8,128)S(1)}, f32[2,80,128]{2,1,0:T(8,128)S(1)}, u32[]{:S(2)}, u32[]{:S(2)}) collective-permute-start(f32[2,80,128]{2,1,0:T(8,128)S(1)} %get-tuple-element.53), channel_id=1, source_target_pairs={{0,4},{1,5},{2,6},{3,7},{4,0},{5,1},{6,2},{7,3},{8,12},{9,13},{10,... | collective-permute-start | bytes 245768 | tf_op jit(solution)/shard_map/ppermute | solution.py:474
  36.5 6.9 %collective-permute-start.13 = (f32[1,80,128]{2,1,0:T(8,128)S(1)}, f32[1,80,128]{2,1,0:T(8,128)S(1)}, u32[]{:S(2)}, u32[]{:S(2)}) collective-permute-start(f32[1,80,128]{2,1,0:T(8,128)S(1)} %get-tuple-element.56), channel_id=1, source_target_pairs={{0,1},{1,0},{2,3},{3,2},{4,5},{5,4},{6,7},{7,6},{8,9},{9,8},{10,11... | collective-permute-start | bytes 122888 | tf_op jit(solution)/shard_map/ppermute | solution.py:474
  37.0 9.0 %collective-permute-start.14 = (f32[2,80,128]{2,1,0:T(8,128)S(1)}, f32[2,80,128]{2,1,0:T(8,128)S(1)}, u32[]{:S(2)}, u32[]{:S(2)}) collective-permute-start(f32[2,80,128]{2,1,0:T(8,128)S(1)} %get-tuple-element.59), channel_id=1, source_target_pairs={{0,5},{1,6},{2,7},{3,0},{4,1},{5,2},{6,3},{7,4},{8,13},{9,14},{10,... | collective-permute-start | bytes 245768 | tf_op jit(solution)/shard_map/ppermute | solution.py:474
  38.9 9.2 %collective-permute-start.15 = (f32[2,80,128]{2,1,0:T(8,128)S(1)}, f32[2,80,128]{2,1,0:T(8,128)S(1)}, u32[]{:S(2)}, u32[]{:S(2)}) collective-permute-start(f32[2,80,128]{2,1,0:T(8,128)S(1)} %get-tuple-element.60), channel_id=1, source_target_pairs={{0,3},{1,4},{2,5},{3,6},{4,7},{5,0},{6,1},{7,2},{8,11},{9,12},{10,... | collective-permute-start | bytes 245768 | tf_op jit(solution)/shard_map/ppermute | solution.py:474
  38.9 9.2 %collective-permute-start.16 = (f32[2,80,128]{2,1,0:T(8,128)S(1)}, f32[2,80,128]{2,1,0:T(8,128)S(1)}, u32[]{:S(2)}, u32[]{:S(2)}) collective-permute-start(f32[2,80,128]{2,1,0:T(8,128)S(1)} %get-tuple-element.61), channel_id=1, source_target_pairs={{0,6},{1,7},{2,0},{3,1},{4,2},{5,3},{6,4},{7,5},{8,14},{9,15},{10,... | collective-permute-start | bytes 245768 | tf_op jit(solution)/shard_map/ppermute | solution.py:474
  42.9 6.7 %collective-permute-start.17 = (f32[2,80,128]{2,1,0:T(8,128)S(1)}, f32[2,80,128]{2,1,0:T(8,128)S(1)}, u32[]{:S(2)}, u32[]{:S(2)}) collective-permute-start(f32[2,80,128]{2,1,0:T(8,128)S(1)} %get-tuple-element.62), channel_id=1, source_target_pairs={{0,2},{1,3},{2,4},{3,5},{4,6},{5,7},{6,0},{7,1},{8,10},{9,11},{10,... | collective-permute-start | bytes 245768 | tf_op jit(solution)/shard_map/ppermute | solution.py:474
  43.4 6.2 %collective-permute-start.12 = (f32[1,80,128]{2,1,0:T(8,128)S(1)}, f32[1,80,128]{2,1,0:T(8,128)S(1)}, u32[]{:S(2)}, u32[]{:S(2)}) collective-permute-start(f32[1,80,128]{2,1,0:T(8,128)S(1)} %shard_map.90), channel_id=1, source_target_pairs={{0,7},{1,2},{2,1},{3,4},{4,3},{5,6},{6,5},{7,0},{8,15},{9,10},{10,... | collective-permute-start | bytes 122888 | tf_op jit(solution)/shard_map/ppermute | solution.py:474

commit v5 on v4

--- a/solution.py
+++ b/solution.py
@@ -341,8 +341,7 @@
 
 
 def prepare_kernel(
-    halves, diag_hbm, cols_hbm, left_hbm, table_ref, index_ref,
-    diag_out, left_out, weights_ref, diag_ref, cols_ref, left_ref, full_ref, sems,
+    halves, diag_hbm, cols_hbm, left_hbm, diag_out, left_out, diag_ref, cols_ref, left_ref, sems
 ):
     copies = []
     for at, (source, target) in enumerate(
@@ -350,6 +349,43 @@
     ):
         copies.append(pltpu.make_async_copy(source, target, sems.at[at]))
         copies[-1].start()
+    copies[0].wait()
+    copies[1].wait()
+    diag_out[...] = times_diag(diag_ref, cols_ref)
+    copies[2].wait()
+    total, size = left_ref.shape
+    step = 128 if total % 128 == 0 else total
+    part = size // halves
+    for at in range(0, total, step):
+        span = slice(at, at + step)
+        hi, lo = split(left_ref[span].T)
+        for half in range(halves):
+            base = 2 * half * part
+            rows_of = slice(half * part, (half + 1) * part)
+            left_out[base : base + part, span] = hi[rows_of]
+            left_out[base + part : base + 2 * part, span] = lo[rows_of]
+
+
+def prepare(diag_tile, cols, left_rows, halves):
+    size, width = cols.shape
+    total = left_rows.shape[0]
+    return call(
+        functools.partial(prepare_kernel, halves),
+        [struct(size, width), struct(2 * size, total, dtype=bf16)],
+        [in_vmem] * 2,
+        [in_hbm] * 3,
+        [
+            pltpu.VMEM(diag_tile.shape, f32),
+            pltpu.VMEM(cols.shape, f32),
+            pltpu.VMEM(left_rows.shape, f32),
+            pltpu.SemaphoreType.DMA((3,)),
+        ],
+        flops=8 * size * size * width,
+        moved=8 * total * size + 4 * size * (size + 2 * width),
+    )(to_hbm(diag_tile), to_hbm(cols), to_hbm(left_rows))
+
+
+def weights_kernel(table_ref, index_ref, after_ref, weights_ref, full_ref):
     entries = table_ref.shape[1]
     size = index_ref.shape[1]
     hot = (lax.broadcasted_iota(jnp.int32, (entries, size), 0) == index_ref[...]).astype(f32)
@@ -360,47 +396,21 @@
     for at, (row, lanes) in enumerate(weight_rows(size)):
         piece = full_ref[pl.ds(row, 1), lanes]
         weights_ref[at] = jnp.broadcast_to(piece, (width, piece.shape[1])).T
-    copies[0].wait()
-    copies[1].wait()
-    diag_out[...] = times_diag(diag_ref, cols_ref)
-    copies[2].wait()
-    total = left_ref.shape[0]
-    step = 128 if total % 128 == 0 else total
-    part = size // halves
-    for at in range(0, total, step):
-        span = slice(at, at + step)
-        hi, lo = split(left_ref[span].T)
-        for half in range(halves):
-            base = 2 * half * part
-            rows_of = slice(half * part, (half + 1) * part)
-            left_out[base : base + part, span] = hi[rows_of]
-            left_out[base + part : base + 2 * part, span] = lo[rows_of]
-
-
-def prepare(diag_tile, cols, left_rows, table, index, halves):
-    size, width = cols.shape
-    total = left_rows.shape[0]
-    weights = weight_rows(size)
-    part = weights[0][1].stop
-    return call(
-        functools.partial(prepare_kernel, halves),
-        [
-            struct(size, width),
-            struct(2 * size, total, dtype=bf16),
-            struct(len(weights), part, width),
-        ],
-        [in_vmem] * 3,
-        [in_hbm] * 3 + [in_vmem] * 2,
-        [
-            pltpu.VMEM(diag_tile.shape, f32),
-            pltpu.VMEM(cols.shape, f32),
-            pltpu.VMEM(left_rows.shape, f32),
-            pltpu.VMEM((table.shape[0], size), f32),
-            pltpu.SemaphoreType.DMA((3,)),
-        ],
-        flops=8 * size * size * width,
-        moved=8 * total * size + 4 * size * (size + 2 * width),
-    )(to_hbm(diag_tile), to_hbm(cols), to_hbm(left_rows), table, index)
+
+
+def spread_weights(table, index, width, after):
+    size = index.shape[1]
+    rows_of = weight_rows(size)
+    part = rows_of[0][1].stop
+    return call(
+        weights_kernel,
+        struct(len(rows_of), part, width),
+        in_vmem,
+        [in_vmem, in_vmem, in_any],
+        [pltpu.VMEM((table.shape[0], size), f32)],
+        flops=12 * table.size * size,
+        moved=4 * len(rows_of) * part * width,
+    )(table, index, after)
 
 
 def row_kernel(messages, halves, final, offs_ref, ranks_ref, *refs):
@@ -508,11 +518,12 @@
     one, two = message_sets_of(lax.axis_size("tile"), slots)
     messages = one + two
     coeffs, split_one, both, rest = first_coefficients(cols, right_tile, one, two)
-    gots = send_all(coeffs, one)
+    diag_part, left_split = prepare(diag_tile, cols, left_rows, halves)
+    gots = send_all(coeffs, one, diag_part)
     coeffs, split_two = rest_coefficients(both, rest, two)
     gots += send_all(coeffs, two)
-    diag_part, left_split, weights = prepare(diag_tile, cols, left_rows, table, index, halves)
     first = rows(offsets, ranks, gots, messages, left_split, diag_part, slots, halves, False)
+    weights = spread_weights(table, index, cols.shape[1], first[0])
     mixed = mix(first, weights)
     coeffs, cols, both = mixed_coefficients(mixed, split_one, one, rank)
     diag_part = diagonal(diag_tile, cols)

time: 51.7 us -> 53.1 us (1.027)
  starting transfers between devices: 26.7 us -> 28.2 us
    ppermute x14, starting transfers between devices: 20.5 us -> 22.3 us  [send(): return lax.ppermute(value, 'tile', message.pairs)]
  transfers between devices with their start and end apart: 18 -> 18, of which waited for: 6 -> 10; matrix products, arithmetic and copies ran while one was open for 0% -> 0% of each run, Pallas kernels for 8% -> 8%
where the time goes in v5:
time: 53.1 us; the launch traced here: 53 us
  starting transfers between devices  28.2 us (53%)
  waiting for transfers between devices  14.9 us (28%)
  Pallas kernels  9.74 us (18%)
    ppermute x14, starting transfers between devices, send(): return lax.ppermute(value, 'tile', message.pairs)  22.3 us
    ppermute x14, waiting for transfers between devices, send(): return lax.ppermute(value, 'tile', message.pairs)  8.83 us
    ppermute x2, waiting for transfers between devices, mix(): lax.ppermute(send, axes, pairs)  3.61 us
    ppermute x2, starting transfers between devices, mix(): lax.ppermute(send, axes, pairs)  3.27 us
    pallas_call x2, Pallas kernels, rows(): call(functools.partial(row_kernel, messages, halves, final), pltpu.HBM((s...  3.08 us
    ppermute x2, starting transfers between devices, mix(): lax.ppermute(part, axes, pairs)  2.58 us
    ppermute x2, waiting for transfers between devices, mix(): lax.ppermute(part, axes, pairs)  2.48 us
    pallas_call x1, Pallas kernels, prepare(): call(functools.partial(prepare_kernel, halves), [struct(size, width), str...  2.19 us
  transfers between devices with their start and end apart: 18, of which 10 were waited for; matrix products, arithmetic and copies ran while one was open for 0% of the time, Pallas kernels for 8%

profile of v5, /device:TPU:0, one launch (start us, length us, event | category | flops | bytes accessed | tf_op | source)
XLA Modules:
  0.0 53.0 jit_solution(12425434853821897586)
XLA Ops:
  0.0 2.0 %shard_map.82 = (f32[2,80,128]{2,1,0:T(8,128)S(1)}, f32[1,80,128]{2,1,0:T(8,128)S(1)}, f32[1,80,128]{2,1,0:T(8,128)S(1)}, bf16[640,512]{1,0:T(8,128)(2,1)S(1)}, ...) custom-call(f32[512,128]{1,0:T(8,128)} %bitcast.21, f32[12,80,512]{2,1,0:T(8,128)} %bitcast.19), custom_call_target="tpu_custom_call" | custom-call | flops 167772160 | bytes 1966080 | tf_op jit(solution)/shard_map/pallas_call | solution.py:161
  2.0 4.1 %collective-permute-start = (f32[2,80,128]{2,1,0:T(8,128)S(1)}, f32[2,80,128]{2,1,0:T(8,128)S(1)}, u32[]{:S(2)}, u32[]{:S(2)}) collective-permute-start(f32[2,80,128]{2,1,0:T(8,128)S(1)} %get-tuple-element.33), channel_id=1, source_target_pairs={{0,4},{1,5},{2,6},{3,7},{4,0},{5,1},{6,2},{7,3},{8,12},{9,13},{10,... | collective-permute-start | bytes 245768 | tf_op jit(solution)/shard_map/ppermute | solution.py:484
  6.9 1.6 %collective-permute-start.4 = (f32[2,80,128]{2,1,0:T(8,128)S(1)}, f32[2,80,128]{2,1,0:T(8,128)S(1)}, u32[]{:S(2)}, u32[]{:S(2)}) collective-permute-start(f32[2,80,128]{2,1,0:T(8,128)S(1)} %get-tuple-element.40), channel_id=1, source_target_pairs={{0,3},{1,4},{2,5},{3,6},{4,7},{5,0},{6,1},{7,2},{8,11},{9,12},{10,... | collective-permute-start | bytes 245768 | tf_op jit(solution)/shard_map/ppermute | solution.py:484
  8.5 3.1 %collective-permute-start.5 = (f32[2,80,128]{2,1,0:T(8,128)S(1)}, f32[2,80,128]{2,1,0:T(8,128)S(1)}, u32[]{:S(2)}, u32[]{:S(2)}) collective-permute-start(f32[2,80,128]{2,1,0:T(8,128)S(1)} %get-tuple-element.41), channel_id=1, source_target_pairs={{0,6},{1,7},{2,0},{3,1},{4,2},{5,3},{6,4},{7,5},{8,14},{9,15},{10,... | collective-permute-start | bytes 245768 | tf_op jit(solution)/shard_map/ppermute | solution.py:484
  11.6 3.9 %collective-permute-start.6 = (f32[2,80,128]{2,1,0:T(8,128)S(1)}, f32[2,80,128]{2,1,0:T(8,128)S(1)}, u32[]{:S(2)}, u32[]{:S(2)}) collective-permute-start(f32[2,80,128]{2,1,0:T(8,128)S(1)} %get-tuple-element.42), channel_id=1, source_target_pairs={{0,2},{1,3},{2,4},{3,5},{4,6},{5,7},{6,0},{7,1},{8,10},{9,11},{10,... | collective-permute-start | bytes 245768 | tf_op jit(solution)/shard_map/ppermute | solution.py:484
  15.5 2.2 %shard_map.83 = (f32[512,128]{1,0:T(8,128)S(1)}, bf16[1024,640]{1,0:T(8,128)(2,1)S(1)}) custom-call(f32[512,512]{1,0:T(8,128)} %bitcast.11, f32[512,128]{1,0:T(8,128)} %bitcast.22, f32[640,512]{1,0:T(8,128)} %bitcast.20), custom_call_target="tpu_custom_call" | custom-call | flops 268435456 | bytes 4194304 | tf_op jit(solution)/shard_map/pallas_call | solution.py:372
  17.8 2.2 %collective-permute-start.1 = (f32[1,80,128]{2,1,0:T(8,128)S(1)}, f32[1,80,128]{2,1,0:T(8,128)S(1)}, u32[]{:S(2)}, u32[]{:S(2)}) collective-permute-start(f32[1,80,128]{2,1,0:T(8,128)S(1)} %shard_map.84), channel_id=1, source_target_pairs={{0,7},{1,2},{2,1},{3,4},{4,3},{5,6},{6,5},{7,0},{8,15},{9,10},{10,... | collective-permute-start | bytes 122888 | tf_op jit(solution)/shard_map/ppermute | solution.py:484
  20.0 0.9 %collective-permute-done.6.refs_6_ = f32[2,80,128]{2,1,0:T(8,128)S(1)} collective-permute-done((f32[2,80,128]{2,1,0:T(8,128)S(1)}, f32[2,80,128]{2,1,0:T(8,128)S(1)}, u32[]{:S(2)}, u32[]{:S(2)}) %collective-permute-start.6) | collective-permute-done | bytes 81952 | tf_op jit(solution)/shard_map/ppermute | solution.py:484
  21.0 2.1 %collective-permute-done.1.refs_1_ = f32[1,80,128]{2,1,0:T(8,128)S(1)} collective-permute-done((f32[1,80,128]{2,1,0:T(8,128)S(1)}, f32[1,80,128]{2,1,0:T(8,128)S(1)}, u32[]{:S(2)}, u32[]{:S(2)}) %collective-permute-start.1) | collective-permute-done | bytes 40992 | tf_op jit(solution)/shard_map/ppermute | solution.py:484
  23.1 1.2 %shard_map.86 = (f32[256,128]{1,0:T(8,128)S(1)}, f32[256,128]{1,0:T(8,128)S(1)}) custom-call(s32[1,8]{1,0:T(1,128)S(1)} %bitcast.15, s32[1,8]{1,0:T(1,128)S(1)} %bitcast.17, f32[2,80,128]{2,1,0:T(8,128)S(1)} %collective-permute-done.refs_1_.refs_0_, f32[1,80,128]{2,1,0:T(8,128)S(1)} %collective-permute-done.1.refs_1_, ...), custom_call_target="tpu_custom_call" | custom-call | flops 335544320 | bytes 1638400 | tf_op jit(solution)/shard_map/pallas_call | solution.py:472
  24.3 1.1 %collective-permute-start.9 = (f32[256,128]{1,0:T(8,128)S(1)}, f32[256,128]{1,0:T(8,128)S(1)}, u32[]{:S(2)}, u32[]{:S(2)}) collective-permute-start(f32[256,128]{1,0:T(8,128)S(1)} %get-tuple-element.47.own_ref), channel_id=1, source_target_pairs={{0,16},{1,9},{2,18},{3,11},{4,20},{5,13},{6,22},{7,15},{8,24},{9,1... | collective-permute-start | bytes 393224 | tf_op jit(solution)/shard_map/ppermute | solution.py:233
  25.4 1.4 %collective-permute-start.7 = (f32[256,128]{1,0:T(8,128)S(1)}, f32[256,128]{1,0:T(8,128)S(1)}, u32[]{:S(2)}, u32[]{:S(2)}) collective-permute-start(f32[256,128]{1,0:T(8,128)S(1)} %get-tuple-element.44.after_ref.own_ref), channel_id=1, source_target_pairs={{0,8},{1,17},{2,10},{3,19},{4,12},{5,21},{6,14},{7,23},{8,0},{9,25... | collective-permute-start | bytes 393224 | tf_op jit(solution)/shard_map/ppermute | solution.py:233
  27.4 2.4 %collective-permute-done.9.got_ref = f32[256,128]{1,0:T(8,128)S(1)} collective-permute-done((f32[256,128]{1,0:T(8,128)S(1)}, f32[256,128]{1,0:T(8,128)S(1)}, u32[]{:S(2)}, u32[]{:S(2)}) %collective-permute-start.9) | collective-permute-done | bytes 131104 | tf_op jit(solution)/shard_map/ppermute | solution.py:233
  29.9 1.8 %collective-permute-start.10 = (f32[256,128]{1,0:T(8,128)S(1)}, f32[256,128]{1,0:T(8,128)S(1)}, u32[]{:S(2)}, u32[]{:S(2)}) collective-permute-start(f32[256,128]{1,0:T(8,128)S(1)} %get-tuple-element.49), channel_id=1, source_target_pairs={{0,8},{1,17},{2,10},{3,19},{4,12},{5,21},{6,14},{7,23},{8,0},{9,25... | collective-permute-start | bytes 393224 | tf_op jit(solution)/shard_map/ppermute | solution.py:239
  31.8 1.4 %collective-permute-start.8 = (f32[256,128]{1,0:T(8,128)S(1)}, f32[256,128]{1,0:T(8,128)S(1)}, u32[]{:S(2)}, u32[]{:S(2)}) collective-permute-start(f32[256,128]{1,0:T(8,128)S(1)} %get-tuple-element.46), channel_id=1, source_target_pairs={{0,16},{1,9},{2,18},{3,11},{4,20},{5,13},{6,22},{7,15},{8,24},{9,1... | collective-permute-start | bytes 393224 | tf_op jit(solution)/shard_map/ppermute | solution.py:239
  33.3 1.7 %collective-permute-done.10.refs_3_ = f32[256,128]{1,0:T(8,128)S(1)} collective-permute-done((f32[256,128]{1,0:T(8,128)S(1)}, f32[256,128]{1,0:T(8,128)S(1)}, u32[]{:S(2)}, u32[]{:S(2)}) %collective-permute-start.10) | collective-permute-done | bytes 131104 | tf_op jit(solution)/shard_map/ppermute | solution.py:239
  34.9 1.9 %collective-permute-done.8.refs_1_ = f32[256,128]{1,0:T(8,128)S(1)} collective-permute-done((f32[256,128]{1,0:T(8,128)S(1)}, f32[256,128]{1,0:T(8,128)S(1)}, u32[]{:S(2)}, u32[]{:S(2)}) %collective-permute-start.8) | collective-permute-done | bytes 131104 | tf_op jit(solution)/shard_map/ppermute | solution.py:239
  37.2 0.9 %collective-permute-start.11 = (f32[2,80,128]{2,1,0:T(8,128)S(1)}, f32[2,80,128]{2,1,0:T(8,128)S(1)}, u32[]{:S(2)}, u32[]{:S(2)}) collective-permute-start(f32[2,80,128]{2,1,0:T(8,128)S(1)} %get-tuple-element.51), channel_id=1, source_target_pairs={{0,4},{1,5},{2,6},{3,7},{4,0},{5,1},{6,2},{7,3},{8,12},{9,13},{10,... | collective-permute-start | bytes 245768 | tf_op jit(solution)/shard_map/ppermute | solution.py:484
  38.7 2.2 %collective-permute-start.14 = (f32[2,80,128]{2,1,0:T(8,128)S(1)}, f32[2,80,128]{2,1,0:T(8,128)S(1)}, u32[]{:S(2)}, u32[]{:S(2)}) collective-permute-start(f32[2,80,128]{2,1,0:T(8,128)S(1)} %get-tuple-element.57), channel_id=1, source_target_pairs={{0,5},{1,6},{2,7},{3,0},{4,1},{5,2},{6,3},{7,4},{8,13},{9,14},{10,... | collective-permute-start | bytes 245768 | tf_op jit(solution)/shard_map/ppermute | solution.py:484
  40.9 1.8 %collective-permute-start.16 = (f32[2,80,128]{2,1,0:T(8,128)S(1)}, f32[2,80,128]{2,1,0:T(8,128)S(1)}, u32[]{:S(2)}, u32[]{:S(2)}) collective-permute-start(f32[2,80,128]{2,1,0:T(8,128)S(1)} %get-tuple-element.59), channel_id=1, source_target_pairs={{0,6},{1,7},{2,0},{3,1},{4,2},{5,3},{6,4},{7,5},{8,14},{9,15},{10,... | collective-permute-start | bytes 245768 | tf_op jit(solution)/shard_map/ppermute | solution.py:484
  43.7 2.1 %collective-permute-start.12 = (f32[1,80,128]{2,1,0:T(8,128)S(1)}, f32[1,80,128]{2,1,0:T(8,128)S(1)}, u32[]{:S(2)}, u32[]{:S(2)}) collective-permute-start(f32[1,80,128]{2,1,0:T(8,128)S(1)} %shard_map.92), channel_id=1, source_target_pairs={{0,7},{1,2},{2,1},{3,4},{4,3},{5,6},{6,5},{7,0},{8,15},{9,10},{10,... | collective-permute-start | bytes 122888 | tf_op jit(solution)/shard_map/ppermute | solution.py:484
  45.8 2.8 %collective-permute-done.15.refs_4_ = f32[2,80,128]{2,1,0:T(8,128)S(1)} collective-permute-done((f32[2,80,128]{2,1,0:T(8,128)S(1)}, f32[2,80,128]{2,1,0:T(8,128)S(1)}, u32[]{:S(2)}, u32[]{:S(2)}) %collective-permute-start.15) | collective-permute-done | bytes 81952 | tf_op jit(solution)/shard_map/ppermute | solution.py:484
  48.6 1.9 %collective-permute-done.17.refs_6_ = f32[2,80,128]{2,1,0:T(8,128)S(1)} collective-permute-done((f32[2,80,128]{2,1,0:T(8,128)S(1)}, f32[2,80,128]{2,1,0:T(8,128)S(1)}, u32[]{:S(2)}, u32[]{:S(2)}) %collective-permute-start.17) | collective-permute-done | bytes 81952 | tf_op jit(solution)/shard_map/ppermute | solution.py:484
  51.1 1.9 %shard_map.94 = f32[512,128]{1,0:T(8,128)} custom-call(s32[1,8]{1,0:T(1,128)S(1)} %bitcast.16, s32[1,8]{1,0:T(1,128)S(1)} %bitcast.18, f32[2,80,128]{2,1,0:T(8,128)S(1)} %collective-permute-done.11.refs_1_.refs_0_, f32[1,80,128]{2,1,0:T(8,128)S(1)} %collective-permute-done.12.refs_1_, f32[1,80,128]{2,1,0:T(8,128)S(1)} %collective-permute-done.13.refs_2_, ...), custom_call_target="tpu_custom_call" | custom-call | flops 335544320 | bytes 1638400 | tf_op jit(solution)/shard_map/pallas_call | solution.py:472
  (35 shorter events, 3.9 us)
Async XLA Ops:
  2.0 9.6 %collective-permute-start = (f32[2,80,128]{2,1,0:T(8,128)S(1)}, f32[2,80,128]{2,1,0:T(8,128)S(1)}, u32[]{:S(2)}, u32[]{:S(2)}) collective-permute-start(f32[2,80,128]{2,1,0:T(8,128)S(1)} %get-tuple-element.33), channel_id=1, source_target_pairs={{0,4},{1,5},{2,6},{3,7},{4,0},{5,1},{6,2},{7,3},{8,12},{9,13},{10,... | collective-permute-start | bytes 245768 | tf_op jit(solution)/shard_map/ppermute | solution.py:484
  6.1 11.7 %collective-permute-start.2 = (f32[1,80,128]{2,1,0:T(8,128)S(1)}, f32[1,80,128]{2,1,0:T(8,128)S(1)}, u32[]{:S(2)}, u32[]{:S(2)}) collective-permute-start(f32[1,80,128]{2,1,0:T(8,128)S(1)} %get-tuple-element.36), channel_id=1, source_target_pairs={{0,1},{1,0},{2,3},{3,2},{4,5},{5,4},{6,7},{7,6},{8,9},{9,8},{10,11... | collective-permute-start | bytes 122888 | tf_op jit(solution)/shard_map/ppermute | solution.py:484
  6.7 13.4 %collective-permute-start.3 = (f32[2,80,128]{2,1,0:T(8,128)S(1)}, f32[2,80,128]{2,1,0:T(8,128)S(1)}, u32[]{:S(2)}, u32[]{:S(2)}) collective-permute-start(f32[2,80,128]{2,1,0:T(8,128)S(1)} %get-tuple-element.39), channel_id=1, source_target_pairs={{0,5},{1,6},{2,7},{3,0},{4,1},{5,2},{6,3},{7,4},{8,13},{9,14},{10,... | collective-permute-start | bytes 245768 | tf_op jit(solution)/shard_map/ppermute | solution.py:484
  6.9 13.1 %collective-permute-start.4 = (f32[2,80,128]{2,1,0:T(8,128)S(1)}, f32[2,80,128]{2,1,0:T(8,128)S(1)}, u32[]{:S(2)}, u32[]{:S(2)}) collective-permute-start(f32[2,80,128]{2,1,0:T(8,128)S(1)} %get-tuple-element.40), channel_id=1, source_target_pairs={{0,3},{1,4},{2,5},{3,6},{4,7},{5,0},{6,1},{7,2},{8,11},{9,12},{10,... | collective-permute-start | bytes 245768 | tf_op jit(solution)/shard_map/ppermute | solution.py:484
  8.5 11.6 %collective-permute-start.5 = (f32[2,80,128]{2,1,0:T(8,128)S(1)}, f32[2,80,128]{2,1,0:T(8,128)S(1)}, u32[]{:S(2)}, u32[]{:S(2)}) collective-permute-start(f32[2,80,128]{2,1,0:T(8,128)S(1)} %get-tuple-element.41), channel_id=1, source_target_pairs={{0,6},{1,7},{2,0},{3,1},{4,2},{5,3},{6,4},{7,5},{8,14},{9,15},{10,... | collective-permute-start | bytes 245768 | tf_op jit(solution)/shard_map/ppermute | solution.py:484
  11.6 9.4 %collective-permute-start.6 = (f32[2,80,128]{2,1,0:T(8,128)S(1)}, f32[2,80,128]{2,1,0:T(8,128)S(1)}, u32[]{:S(2)}, u32[]{:S(2)}) collective-permute-start(f32[2,80,128]{2,1,0:T(8,128)S(1)} %get-tuple-element.42), channel_id=1, source_target_pairs={{0,2},{1,3},{2,4},{3,5},{4,6},{5,7},{6,0},{7,1},{8,10},{9,11},{10,... | collective-permute-start | bytes 245768 | tf_op jit(solution)/shard_map/ppermute | solution.py:484
  15.5 7.6 %copy-start.3 = (s32[1,1,8]{2,1,0:T(1,128)S(1)}, s32[1,1,8]{2,1,0:T(1,128)}, u32[]{:S(2)}) copy-start(s32[1,1,8]{2,1,0:T(1,128)} %param.11) | copy-start | bytes 100
  15.5 7.6 %copy-start.4 = (s32[1,1,8]{2,1,0:T(1,128)S(1)}, s32[1,1,8]{2,1,0:T(1,128)}, u32[]{:S(2)}) copy-start(s32[1,1,8]{2,1,0:T(1,128)} %param.12) | copy-start | bytes 100
  17.7 9.2 %copy-start.1 = (f32[64,4,4]{0,2,1:T(4,128)S(1)}, f32[64,4,4]{0,2,1:T(4,128)}, u32[]{:S(2)}) copy-start(f32[64,4,4]{0,2,1:T(4,128)} %param.13) | copy-start | bytes 12292
  17.7 9.1 %copy-start.2 = (s32[512]{0:T(512)S(1)}, s32[512]{0:T(512)}, u32[]{:S(2)}) copy-start(s32[512]{0:T(512)} %param.14) | copy-start | bytes 6148
  17.8 5.3 %collective-permute-start.1 = (f32[1,80,128]{2,1,0:T(8,128)S(1)}, f32[1,80,128]{2,1,0:T(8,128)S(1)}, u32[]{:S(2)}, u32[]{:S(2)}) collective-permute-start(f32[1,80,128]{2,1,0:T(8,128)S(1)} %shard_map.84), channel_id=1, source_target_pairs={{0,7},{1,2},{2,1},{3,4},{4,3},{5,6},{6,5},{7,0},{8,15},{9,10},{10,... | collective-permute-start | bytes 122888 | tf_op jit(solution)/shard_map/ppermute | solution.py:484
  24.3 5.5 %collective-permute-start.9 = (f32[256,128]{1,0:T(8,128)S(1)}, f32[256,128]{1,0:T(8,128)S(1)}, u32[]{:S(2)}, u32[]{:S(2)}) collective-permute-start(f32[256,128]{1,0:T(8,128)S(1)} %get-tuple-element.47.own_ref), channel_id=1, source_target_pairs={{0,16},{1,9},{2,18},{3,11},{4,20},{5,13},{6,22},{7,15},{8,24},{9,1... | collective-permute-start | bytes 393224 | tf_op jit(solution)/shard_map/ppermute | solution.py:233
  25.4 6.3 %collective-permute-start.7 = (f32[256,128]{1,0:T(8,128)S(1)}, f32[256,128]{1,0:T(8,128)S(1)}, u32[]{:S(2)}, u32[]{:S(2)}) collective-permute-start(f32[256,128]{1,0:T(8,128)S(1)} %get-tuple-element.44.after_ref.own_ref), channel_id=1, source_target_pairs={{0,8},{1,17},{2,10},{3,19},{4,12},{5,21},{6,14},{7,23},{8,0},{9,25... | collective-permute-start | bytes 393224 | tf_op jit(solution)/shard_map/ppermute | solution.py:233
  29.9 5.0 %collective-permute-start.10 = (f32[256,128]{1,0:T(8,128)S(1)}, f32[256,128]{1,0:T(8,128)S(1)}, u32[]{:S(2)}, u32[]{:S(2)}) collective-permute-start(f32[256,128]{1,0:T(8,128)S(1)} %get-tuple-element.49), channel_id=1, source_target_pairs={{0,8},{1,17},{2,10},{3,19},{4,12},{5,21},{6,14},{7,23},{8,0},{9,25... | collective-permute-start | bytes 393224 | tf_op jit(solution)/shard_map/ppermute | solution.py:239
  31.8 5.0 %collective-permute-start.8 = (f32[256,128]{1,0:T(8,128)S(1)}, f32[256,128]{1,0:T(8,128)S(1)}, u32[]{:S(2)}, u32[]{:S(2)}) collective-permute-start(f32[256,128]{1,0:T(8,128)S(1)} %get-tuple-element.46), channel_id=1, source_target_pairs={{0,16},{1,9},{2,18},{3,11},{4,20},{5,13},{6,22},{7,15},{8,24},{9,1... | collective-permute-start | bytes 393224 | tf_op jit(solution)/shard_map/ppermute | solution.py:239
  36.9 6.4 %copy-start = (f32[1,1,512,512]{3,2,1,0:T(8,128)S(1)}, f32[1,1,512,512]{3,2,1,0:T(8,128)}, u32[]{:S(2)}) copy-start(f32[1,1,512,512]{3,2,1,0:T(8,128)} %param.8) | copy-start | bytes 3145732
  37.2 6.0 %collective-permute-start.11 = (f32[2,80,128]{2,1,0:T(8,128)S(1)}, f32[2,80,128]{2,1,0:T(8,128)S(1)}, u32[]{:S(2)}, u32[]{:S(2)}) collective-permute-start(f32[2,80,128]{2,1,0:T(8,128)S(1)} %get-tuple-element.51), channel_id=1, source_target_pairs={{0,4},{1,5},{2,6},{3,7},{4,0},{5,1},{6,2},{7,3},{8,12},{9,13},{10,... | collective-permute-start | bytes 245768 | tf_op jit(solution)/shard_map/ppermute | solution.py:484
  38.2 5.5 %collective-permute-start.13 = (f32[1,80,128]{2,1,0:T(8,128)S(1)}, f32[1,80,128]{2,1,0:T(8,128)S(1)}, u32[]{:S(2)}, u32[]{:S(2)}) collective-permute-start(f32[1,80,128]{2,1,0:T(8,128)S(1)} %get-tuple-element.54), channel_id=1, source_target_pairs={{0,1},{1,0},{2,3},{3,2},{4,5},{5,4},{6,7},{7,6},{8,9},{9,8},{10,11... | collective-permute-start | bytes 122888 | tf_op jit(solution)/shard_map/ppermute | solution.py:484
  38.7 7.1 %collective-permute-start.14 = (f32[2,80,128]{2,1,0:T(8,128)S(1)}, f32[2,80,128]{2,1,0:T(8,128)S(1)}, u32[]{:S(2)}, u32[]{:S(2)}) collective-permute-start(f32[2,80,128]{2,1,0:T(8,128)S(1)} %get-tuple-element.57), channel_id=1, source_target_pairs={{0,5},{1,6},{2,7},{3,0},{4,1},{5,2},{6,3},{7,4},{8,13},{9,14},{10,... | collective-permute-start | bytes 245768 | tf_op jit(solution)/shard_map/ppermute | solution.py:484
  40.9 7.7 %collective-permute-start.15 = (f32[2,80,128]{2,1,0:T(8,128)S(1)}, f32[2,80,128]{2,1,0:T(8,128)S(1)}, u32[]{:S(2)}, u32[]{:S(2)}) collective-permute-start(f32[2,80,128]{2,1,0:T(8,128)S(1)} %get-tuple-element.58), channel_id=1, source_target_pairs={{0,3},{1,4},{2,5},{3,6},{4,7},{5,0},{6,1},{7,2},{8,11},{9,12},{10,... | collective-permute-start | bytes 245768 | tf_op jit(solution)/shard_map/ppermute | solution.py:484
  40.9 7.7 %collective-permute-start.16 = (f32[2,80,128]{2,1,0:T(8,128)S(1)}, f32[2,80,128]{2,1,0:T(8,128)S(1)}, u32[]{:S(2)}, u32[]{:S(2)}) collective-permute-start(f32[2,80,128]{2,1,0:T(8,128)S(1)} %get-tuple-element.59), channel_id=1, source_target_pairs={{0,6},{1,7},{2,0},{3,1},{4,2},{5,3},{6,4},{7,5},{8,14},{9,15},{10,... | collective-permute-start | bytes 245768 | tf_op jit(solution)/shard_map/ppermute | solution.py:484
  43.2 7.3 %collective-permute-start.17 = (f32[2,80,128]{2,1,0:T(8,128)S(1)}, f32[2,80,128]{2,1,0:T(8,128)S(1)}, u32[]{:S(2)}, u32[]{:S(2)}) collective-permute-start(f32[2,80,128]{2,1,0:T(8,128)S(1)} %get-tuple-element.60), channel_id=1, source_target_pairs={{0,2},{1,3},{2,4},{3,5},{4,6},{5,7},{6,0},{7,1},{8,10},{9,11},{10,... | collective-permute-start | bytes 245768 | tf_op jit(solution)/shard_map/ppermute | solution.py:484
  43.7 7.4 %collective-permute-start.12 = (f32[1,80,128]{2,1,0:T(8,128)S(1)}, f32[1,80,128]{2,1,0:T(8,128)S(1)}, u32[]{:S(2)}, u32[]{:S(2)}) collective-permute-start(f32[1,80,128]{2,1,0:T(8,128)S(1)} %shard_map.92), channel_id=1, source_target_pairs={{0,7},{1,2},{2,1},{3,4},{4,3},{5,6},{6,5},{7,0},{8,15},{9,10},{10,... | collective-permute-start | bytes 122888 | tf_op jit(solution)/shard_map/ppermute | solution.py:484

commit v6 on v4

--- a/solution.py
+++ b/solution.py
@@ -80,7 +80,7 @@
     for ahead, group in groups.items():
         messages.append(Message([(at, (at - ahead) % count) for at in range(count)], group))
     messages.sort(key=lambda message: -message.across)
-    first = messages[:1] + [m for m in messages[1:] if m.odd_slots is not None]
+    first = messages[:1] + [m for m in messages[:0:-1] if m.odd_slots is not None]
     return [first, [message for message in messages if message not in first]]
 
 
@@ -474,13 +474,13 @@
     return lax.ppermute(value, "tile", message.pairs)
 
 
-def send_all(coeffs, messages, after=None):
+def send_all(one, two, coeffs, more, waited, beside):
     gots = []
-    for value, message in zip(coeffs, messages):
-        if after is not None and message.odd_slots is not None and message.across:
-            value = relay([value], [gots[0], after])[0]
+    for value, message in zip(coeffs, one):
+        if message.odd_slots is not None and message.across:
+            value = relay([value], [gots[waited], more[0], beside])[0]
         gots.append(send(value, message))
-    return gots
+    return gots + [send(value, message) for value, message in zip(more, two)]
 
 
 def local(
@@ -508,16 +508,15 @@
     one, two = message_sets_of(lax.axis_size("tile"), slots)
     messages = one + two
     coeffs, split_one, both, rest = first_coefficients(cols, right_tile, one, two)
-    gots = send_all(coeffs, one)
-    coeffs, split_two = rest_coefficients(both, rest, two)
-    gots += send_all(coeffs, two)
+    more, split_two = rest_coefficients(both, rest, two)
     diag_part, left_split, weights = prepare(diag_tile, cols, left_rows, table, index, halves)
+    gots = send_all(one, two, coeffs, more, -1, diag_part)
     first = rows(offsets, ranks, gots, messages, left_split, diag_part, slots, halves, False)
     mixed = mix(first, weights)
     coeffs, cols, both = mixed_coefficients(mixed, split_one, one, rank)
+    more = next_coefficients(both, split_two, two, rank)
     diag_part = diagonal(diag_tile, cols)
-    gots = send_all(coeffs, one, diag_part)
-    gots += send_all(next_coefficients(both, split_two, two, rank), two)
+    gots = send_all(one, two, coeffs, more, 0, diag_part)
     return rows(offsets, ranks, gots, messages, left_split, diag_part, slots, halves, True)[None]
 
 

time: 51.7 us -> 50.3 us (0.973); the launches traced: 51.5 us -> 49.6 us
  waiting for transfers between devices: 15.4 us -> 11.9 us
  starting transfers between devices: 26.7 us -> 28.3 us
    ppermute x14, waiting for transfers between devices: 9.13 us -> 6.31 us  [send(): return lax.ppermute(value, 'tile', message.pairs)]
    ppermute x2, starting transfers between devices: 3.13 us -> 4.21 us  [mix(): lax.ppermute(send, axes, pairs)]
    ppermute x2, waiting for transfers between devices: 2.77 us -> 2.05 us  [mix(): lax.ppermute(part, axes, pairs)]
  transfers between devices with their start and end apart: 18 -> 18, of which waited for: 6 -> 7; matrix products, arithmetic and copies ran while one was open for 0% -> 0% of each run, Pallas kernels for 8% -> 8%
where the time goes in v6:
time: 50.3 us; the launch traced here: 49.6 us
  starting transfers between devices  28.3 us (56%)
  waiting for transfers between devices  11.9 us (24%)
  Pallas kernels  9.27 us (18%)
    ppermute x14, starting transfers between devices, send(): return lax.ppermute(value, 'tile', message.pairs)  21 us
    ppermute x14, waiting for transfers between devices, send(): return lax.ppermute(value, 'tile', message.pairs)  6.31 us
    ppermute x2, starting transfers between devices, mix(): lax.ppermute(send, axes, pairs)  4.21 us
    ppermute x2, waiting for transfers between devices, mix(): lax.ppermute(send, axes, pairs)  3.52 us
    pallas_call x2, Pallas kernels, rows(): call(functools.partial(row_kernel, messages, halves, final), pltpu.HBM((s...  3.1 us
    ppermute x2, starting transfers between devices, mix(): lax.ppermute(part, axes, pairs)  3.07 us
    pallas_call x1, Pallas kernels, prepare(): call(functools.partial(prepare_kernel, halves), [struct(size, width), str...  2.21 us
    ppermute x2, waiting for transfers between devices, mix(): lax.ppermute(part, axes, pairs)  2.05 us
  transfers between devices with their start and end apart: 18, of which 7 were waited for; matrix products, arithmetic and copies ran while one was open for 0% of the time, Pallas kernels for 8%

profile of v6, /device:TPU:0, one launch (start us, length us, event | category | flops | bytes accessed | tf_op | source)
XLA Modules:
  0.0 49.6 jit_solution(7853715041720449198)
XLA Ops:
  0.0 2.0 %shard_map.82 = (f32[2,80,128]{2,1,0:T(8,128)S(1)}, f32[1,80,128]{2,1,0:T(8,128)S(1)}, f32[1,80,128]{2,1,0:T(8,128)S(1)}, bf16[640,512]{1,0:T(8,128)(2,1)S(1)}, ...) custom-call(f32[512,128]{1,0:T(8,128)} %bitcast.21, f32[12,80,512]{2,1,0:T(8,128)} %bitcast.19), custom_call_target="tpu_custom_call" | custom-call | flops 167772160 | bytes 1966080 | tf_op jit(solution)/shard_map/pallas_call | solution.py:161
  2.0 0.5 %collective-permute-start.1 = (f32[1,80,128]{2,1,0:T(8,128)S(1)}, f32[1,80,128]{2,1,0:T(8,128)S(1)}, u32[]{:S(2)}, u32[]{:S(2)}) collective-permute-start(f32[1,80,128]{2,1,0:T(8,128)S(1)} %get-tuple-element.35), channel_id=1, source_target_pairs={{0,1},{1,0},{2,3},{3,2},{4,5},{5,4},{6,7},{7,6},{8,9},{9,8},{10,11... | collective-permute-start | bytes 122888 | tf_op jit(solution)/shard_map/ppermute | solution.py:474
  2.5 3.7 %collective-permute-start = (f32[2,80,128]{2,1,0:T(8,128)S(1)}, f32[2,80,128]{2,1,0:T(8,128)S(1)}, u32[]{:S(2)}, u32[]{:S(2)}) collective-permute-start(f32[2,80,128]{2,1,0:T(8,128)S(1)} %get-tuple-element.34), channel_id=1, source_target_pairs={{0,4},{1,5},{2,6},{3,7},{4,0},{5,1},{6,2},{7,3},{8,12},{9,13},{10,... | collective-permute-start | bytes 245768 | tf_op jit(solution)/shard_map/ppermute | solution.py:474
  6.2 0.6 %shard_map.83 = (f32[2,80,128]{2,1,0:T(8,128)S(1)}, f32[2,80,128]{2,1,0:T(8,128)S(1)}, f32[2,80,128]{2,1,0:T(8,128)S(1)}, f32[2,80,128]{2,1,0:T(8,128)S(1)}, bf16[1280,512]{1,0:T(8,128)(2,1)S(1)}) custom-call(bf16[512,256]{1,0:T(8,128)(2,1)S(1)} %get-tuple-element.37.both_ref, f32[8,80,512]{2,1,0:T(8,128)S(1)} %get-tuple-element.38.right_ref), custom_call_target="tpu_custom_call" | custom-call | flops 335544320 | bytes 2621440 | tf_op jit(solution)/shard_map/pallas_call | solution.py:190
  6.8 1.4 %collective-permute-start.4 = (f32[2,80,128]{2,1,0:T(8,128)S(1)}, f32[2,80,128]{2,1,0:T(8,128)S(1)}, u32[]{:S(2)}, u32[]{:S(2)}) collective-permute-start(f32[2,80,128]{2,1,0:T(8,128)S(1)} %get-tuple-element.41), channel_id=1, source_target_pairs={{0,3},{1,4},{2,5},{3,6},{4,7},{5,0},{6,1},{7,2},{8,11},{9,12},{10,... | collective-permute-start | bytes 245768 | tf_op jit(solution)/shard_map/ppermute | solution.py:474
  8.1 2.3 %collective-permute-start.5 = (f32[2,80,128]{2,1,0:T(8,128)S(1)}, f32[2,80,128]{2,1,0:T(8,128)S(1)}, u32[]{:S(2)}, u32[]{:S(2)}) collective-permute-start(f32[2,80,128]{2,1,0:T(8,128)S(1)} %get-tuple-element.42), channel_id=1, source_target_pairs={{0,6},{1,7},{2,0},{3,1},{4,2},{5,3},{6,4},{7,5},{8,14},{9,15},{10,... | collective-permute-start | bytes 245768 | tf_op jit(solution)/shard_map/ppermute | solution.py:474
  10.4 0.5 %collective-permute-start.3 = (f32[2,80,128]{2,1,0:T(8,128)S(1)}, f32[2,80,128]{2,1,0:T(8,128)S(1)}, u32[]{:S(2)}, u32[]{:S(2)}) collective-permute-start(f32[2,80,128]{2,1,0:T(8,128)S(1)} %get-tuple-element.39.refs_2_), channel_id=1, source_target_pairs={{0,5},{1,6},{2,7},{3,0},{4,1},{5,2},{6,3},{7,4},{8,13},{9,14},{10,... | collective-permute-start | bytes 245768 | tf_op jit(solution)/shard_map/ppermute | solution.py:474
  10.9 2.2 %shard_map.84 = (f32[512,128]{1,0:T(8,128)S(1)}, bf16[1024,640]{1,0:T(8,128)(2,1)S(1)}, f32[8,256,128]{2,1,0:T(8,128)S(1)}) custom-call(f32[512,512]{1,0:T(8,128)} %bitcast.11, f32[512,128]{1,0:T(8,128)} %bitcast.22, f32[640,512]{1,0:T(8,128)} %bitcast.20, f32[16,64]{1,0:T(8,128)S(1)} %bitcast.13, s32[1,512]{1,0:T(1,128)S(1)} %bitcast.14), custom_call_target="tpu_custom_call" | custom-call | flops 268435456 | bytes 4194304 | tf_op jit(solution)/shard_map/pallas_call | solution.py:385
  13.2 3.3 %collective-permute-start.2 = (f32[1,80,128]{2,1,0:T(8,128)S(1)}, f32[1,80,128]{2,1,0:T(8,128)S(1)}, u32[]{:S(2)}, u32[]{:S(2)}) collective-permute-start(f32[1,80,128]{2,1,0:T(8,128)S(1)} %shard_map.85), channel_id=1, source_target_pairs={{0,7},{1,2},{2,1},{3,4},{4,3},{5,6},{6,5},{7,0},{8,15},{9,10},{10,... | collective-permute-start | bytes 122888 | tf_op jit(solution)/shard_map/ppermute | solution.py:474
  16.5 1.1 %collective-permute-done.6.refs_6_ = f32[2,80,128]{2,1,0:T(8,128)S(1)} collective-permute-done((f32[2,80,128]{2,1,0:T(8,128)S(1)}, f32[2,80,128]{2,1,0:T(8,128)S(1)}, u32[]{:S(2)}, u32[]{:S(2)}) %collective-permute-start.6) | collective-permute-done | bytes 81952 | tf_op jit(solution)/shard_map/ppermute | solution.py:474
  17.6 1.5 %collective-permute-done.2.refs_2_ = f32[1,80,128]{2,1,0:T(8,128)S(1)} collective-permute-done((f32[1,80,128]{2,1,0:T(8,128)S(1)}, f32[1,80,128]{2,1,0:T(8,128)S(1)}, u32[]{:S(2)}, u32[]{:S(2)}) %collective-permute-start.2) | collective-permute-done | bytes 40992 | tf_op jit(solution)/shard_map/ppermute | solution.py:474
  19.1 1.2 %shard_map.86 = (f32[256,128]{1,0:T(8,128)S(1)}, f32[256,128]{1,0:T(8,128)S(1)}) custom-call(s32[1,8]{1,0:T(1,128)S(1)} %bitcast.15, s32[1,8]{1,0:T(1,128)S(1)} %bitcast.17, f32[2,80,128]{2,1,0:T(8,128)S(1)} %collective-permute-done.refs_0_, f32[1,80,128]{2,1,0:T(8,128)S(1)} %collective-permute-done.1.refs_1_, ...), custom_call_target="tpu_custom_call" | custom-call | flops 335544320 | bytes 1638400 | tf_op jit(solution)/shard_map/pallas_call | solution.py:462
  20.3 1.6 %collective-permute-start.7 = (f32[256,128]{1,0:T(8,128)S(1)}, f32[256,128]{1,0:T(8,128)S(1)}, u32[]{:S(2)}, u32[]{:S(2)}) collective-permute-start(f32[256,128]{1,0:T(8,128)S(1)} %get-tuple-element.45.own_ref), channel_id=1, source_target_pairs={{0,8},{1,17},{2,10},{3,19},{4,12},{5,21},{6,14},{7,23},{8,0},{9,25... | collective-permute-start | bytes 393224 | tf_op jit(solution)/shard_map/ppermute | solution.py:233
  21.9 1.5 %collective-permute-start.9 = (f32[256,128]{1,0:T(8,128)S(1)}, f32[256,128]{1,0:T(8,128)S(1)}, u32[]{:S(2)}, u32[]{:S(2)}) collective-permute-start(f32[256,128]{1,0:T(8,128)S(1)} %get-tuple-element.49.own_ref), channel_id=1, source_target_pairs={{0,16},{1,9},{2,18},{3,11},{4,20},{5,13},{6,22},{7,15},{8,24},{9,1... | collective-permute-start | bytes 393224 | tf_op jit(solution)/shard_map/ppermute | solution.py:233
  23.4 2.0 %collective-permute-done.7.got_ref = f32[256,128]{1,0:T(8,128)S(1)} collective-permute-done((f32[256,128]{1,0:T(8,128)S(1)}, f32[256,128]{1,0:T(8,128)S(1)}, u32[]{:S(2)}, u32[]{:S(2)}) %collective-permute-start.7) | collective-permute-done | bytes 131104 | tf_op jit(solution)/shard_map/ppermute | solution.py:233
  25.5 2.7 %collective-permute-start.8 = (f32[256,128]{1,0:T(8,128)S(1)}, f32[256,128]{1,0:T(8,128)S(1)}, u32[]{:S(2)}, u32[]{:S(2)}) collective-permute-start(f32[256,128]{1,0:T(8,128)S(1)} %get-tuple-element.48), channel_id=1, source_target_pairs={{0,16},{1,9},{2,18},{3,11},{4,20},{5,13},{6,22},{7,15},{8,24},{9,1... | collective-permute-start | bytes 393224 | tf_op jit(solution)/shard_map/ppermute | solution.py:239
  28.3 1.5 %collective-permute-start.10 = (f32[256,128]{1,0:T(8,128)S(1)}, f32[256,128]{1,0:T(8,128)S(1)}, u32[]{:S(2)}, u32[]{:S(2)}) collective-permute-start(f32[256,128]{1,0:T(8,128)S(1)} %get-tuple-element.51), channel_id=1, source_target_pairs={{0,8},{1,17},{2,10},{3,19},{4,12},{5,21},{6,14},{7,23},{8,0},{9,25... | collective-permute-start | bytes 393224 | tf_op jit(solution)/shard_map/ppermute | solution.py:239
  29.8 2.1 %collective-permute-done.8.refs_1_ = f32[256,128]{1,0:T(8,128)S(1)} collective-permute-done((f32[256,128]{1,0:T(8,128)S(1)}, f32[256,128]{1,0:T(8,128)S(1)}, u32[]{:S(2)}, u32[]{:S(2)}) %collective-permute-start.8) | collective-permute-done | bytes 131104 | tf_op jit(solution)/shard_map/ppermute | solution.py:239
  31.8 1.5 %collective-permute-done.10.refs_3_ = f32[256,128]{1,0:T(8,128)S(1)} collective-permute-done((f32[256,128]{1,0:T(8,128)S(1)}, f32[256,128]{1,0:T(8,128)S(1)}, u32[]{:S(2)}, u32[]{:S(2)}) %collective-permute-start.10) | collective-permute-done | bytes 131104 | tf_op jit(solution)/shard_map/ppermute | solution.py:239
  33.7 2.6 %collective-permute-start.11 = (f32[2,80,128]{2,1,0:T(8,128)S(1)}, f32[2,80,128]{2,1,0:T(8,128)S(1)}, u32[]{:S(2)}, u32[]{:S(2)}) collective-permute-start(f32[2,80,128]{2,1,0:T(8,128)S(1)} %get-tuple-element.53), channel_id=1, source_target_pairs={{0,4},{1,5},{2,6},{3,7},{4,0},{5,1},{6,2},{7,3},{8,12},{9,13},{10,... | collective-permute-start | bytes 245768 | tf_op jit(solution)/shard_map/ppermute | solution.py:474
  37.1 3.6 %collective-permute-start.16 = (f32[2,80,128]{2,1,0:T(8,128)S(1)}, f32[2,80,128]{2,1,0:T(8,128)S(1)}, u32[]{:S(2)}, u32[]{:S(2)}) collective-permute-start(f32[2,80,128]{2,1,0:T(8,128)S(1)} %get-tuple-element.61), channel_id=1, source_target_pairs={{0,6},{1,7},{2,0},{3,1},{4,2},{5,3},{6,4},{7,5},{8,14},{9,15},{10,... | collective-permute-start | bytes 245768 | tf_op jit(solution)/shard_map/ppermute | solution.py:474
  41.4 2.6 %collective-permute-start.13 = (f32[1,80,128]{2,1,0:T(8,128)S(1)}, f32[1,80,128]{2,1,0:T(8,128)S(1)}, u32[]{:S(2)}, u32[]{:S(2)}) collective-permute-start(f32[1,80,128]{2,1,0:T(8,128)S(1)} %shard_map.92), channel_id=1, source_target_pairs={{0,7},{1,2},{2,1},{3,4},{4,3},{5,6},{6,5},{7,0},{8,15},{9,10},{10,... | collective-permute-start | bytes 122888 | tf_op jit(solution)/shard_map/ppermute | solution.py:474
  44.0 3.6 %collective-permute-done.17.refs_6_ = f32[2,80,128]{2,1,0:T(8,128)S(1)} collective-permute-done((f32[2,80,128]{2,1,0:T(8,128)S(1)}, f32[2,80,128]{2,1,0:T(8,128)S(1)}, u32[]{:S(2)}, u32[]{:S(2)}) %collective-permute-start.17) | collective-permute-done | bytes 81952 | tf_op jit(solution)/shard_map/ppermute | solution.py:474
  47.7 1.9 %shard_map.93 = f32[512,128]{1,0:T(8,128)} custom-call(s32[1,8]{1,0:T(1,128)S(1)} %bitcast.16, s32[1,8]{1,0:T(1,128)S(1)} %bitcast.18, f32[2,80,128]{2,1,0:T(8,128)S(1)} %collective-permute-done.11.refs_1_.refs_0_, f32[1,80,128]{2,1,0:T(8,128)S(1)} %collective-permute-done.12.refs_1_, f32[1,80,128]{2,1,0:T(8,128)S(1)} %collective-permute-done.13.refs_2_, ...), custom_call_target="tpu_custom_call" | custom-call | flops 335544320 | bytes 1638400 | tf_op jit(solution)/shard_map/pallas_call | solution.py:462
  (34 shorter events, 2.1 us)
Async XLA Ops:
  2.0 9.0 %copy-start.1 = (f32[64,4,4]{0,2,1:T(4,128)S(1)}, f32[64,4,4]{0,2,1:T(4,128)}, u32[]{:S(2)}) copy-start(f32[64,4,4]{0,2,1:T(4,128)} %param.13) | copy-start | bytes 12292
  2.0 9.0 %copy-start.2 = (s32[512]{0:T(512)S(1)}, s32[512]{0:T(512)}, u32[]{:S(2)}) copy-start(s32[512]{0:T(512)} %param.14) | copy-start | bytes 6148
  2.0 8.4 %collective-permute-start.1 = (f32[1,80,128]{2,1,0:T(8,128)S(1)}, f32[1,80,128]{2,1,0:T(8,128)S(1)}, u32[]{:S(2)}, u32[]{:S(2)}) collective-permute-start(f32[1,80,128]{2,1,0:T(8,128)S(1)} %get-tuple-element.35), channel_id=1, source_target_pairs={{0,1},{1,0},{2,3},{3,2},{4,5},{5,4},{6,7},{7,6},{8,9},{9,8},{10,11... | collective-permute-start | bytes 122888 | tf_op jit(solution)/shard_map/ppermute | solution.py:474
  2.5 10.7 %collective-permute-start = (f32[2,80,128]{2,1,0:T(8,128)S(1)}, f32[2,80,128]{2,1,0:T(8,128)S(1)}, u32[]{:S(2)}, u32[]{:S(2)}) collective-permute-start(f32[2,80,128]{2,1,0:T(8,128)S(1)} %get-tuple-element.34), channel_id=1, source_target_pairs={{0,4},{1,5},{2,6},{3,7},{4,0},{5,1},{6,2},{7,3},{8,12},{9,13},{10,... | collective-permute-start | bytes 245768 | tf_op jit(solution)/shard_map/ppermute | solution.py:474
  6.8 9.8 %collective-permute-start.4 = (f32[2,80,128]{2,1,0:T(8,128)S(1)}, f32[2,80,128]{2,1,0:T(8,128)S(1)}, u32[]{:S(2)}, u32[]{:S(2)}) collective-permute-start(f32[2,80,128]{2,1,0:T(8,128)S(1)} %get-tuple-element.41), channel_id=1, source_target_pairs={{0,3},{1,4},{2,5},{3,6},{4,7},{5,0},{6,1},{7,2},{8,11},{9,12},{10,... | collective-permute-start | bytes 245768 | tf_op jit(solution)/shard_map/ppermute | solution.py:474
  8.1 8.4 %collective-permute-start.5 = (f32[2,80,128]{2,1,0:T(8,128)S(1)}, f32[2,80,128]{2,1,0:T(8,128)S(1)}, u32[]{:S(2)}, u32[]{:S(2)}) collective-permute-start(f32[2,80,128]{2,1,0:T(8,128)S(1)} %get-tuple-element.42), channel_id=1, source_target_pairs={{0,6},{1,7},{2,0},{3,1},{4,2},{5,3},{6,4},{7,5},{8,14},{9,15},{10,... | collective-permute-start | bytes 245768 | tf_op jit(solution)/shard_map/ppermute | solution.py:474
  10.4 7.2 %collective-permute-start.6 = (f32[2,80,128]{2,1,0:T(8,128)S(1)}, f32[2,80,128]{2,1,0:T(8,128)S(1)}, u32[]{:S(2)}, u32[]{:S(2)}) collective-permute-start(f32[2,80,128]{2,1,0:T(8,128)S(1)} %get-tuple-element.43), channel_id=1, source_target_pairs={{0,2},{1,3},{2,4},{3,5},{4,6},{5,7},{6,0},{7,1},{8,10},{9,11},{10,... | collective-permute-start | bytes 245768 | tf_op jit(solution)/shard_map/ppermute | solution.py:474
  10.4 7.2 %collective-permute-start.3 = (f32[2,80,128]{2,1,0:T(8,128)S(1)}, f32[2,80,128]{2,1,0:T(8,128)S(1)}, u32[]{:S(2)}, u32[]{:S(2)}) collective-permute-start(f32[2,80,128]{2,1,0:T(8,128)S(1)} %get-tuple-element.39.refs_2_), channel_id=1, source_target_pairs={{0,5},{1,6},{2,7},{3,0},{4,1},{5,2},{6,3},{7,4},{8,13},{9,14},{10,... | collective-permute-start | bytes 245768 | tf_op jit(solution)/shard_map/ppermute | solution.py:474
  10.9 8.2 %copy-start.3 = (s32[1,1,8]{2,1,0:T(1,128)S(1)}, s32[1,1,8]{2,1,0:T(1,128)}, u32[]{:S(2)}) copy-start(s32[1,1,8]{2,1,0:T(1,128)} %param.11) | copy-start | bytes 100
  10.9 8.2 %copy-start.4 = (s32[1,1,8]{2,1,0:T(1,128)S(1)}, s32[1,1,8]{2,1,0:T(1,128)}, u32[]{:S(2)}) copy-start(s32[1,1,8]{2,1,0:T(1,128)} %param.12) | copy-start | bytes 100
  13.2 5.9 %collective-permute-start.2 = (f32[1,80,128]{2,1,0:T(8,128)S(1)}, f32[1,80,128]{2,1,0:T(8,128)S(1)}, u32[]{:S(2)}, u32[]{:S(2)}) collective-permute-start(f32[1,80,128]{2,1,0:T(8,128)S(1)} %shard_map.85), channel_id=1, source_target_pairs={{0,7},{1,2},{2,1},{3,4},{4,3},{5,6},{6,5},{7,0},{8,15},{9,10},{10,... | collective-permute-start | bytes 122888 | tf_op jit(solution)/shard_map/ppermute | solution.py:474
  20.3 5.1 %collective-permute-start.7 = (f32[256,128]{1,0:T(8,128)S(1)}, f32[256,128]{1,0:T(8,128)S(1)}, u32[]{:S(2)}, u32[]{:S(2)}) collective-permute-start(f32[256,128]{1,0:T(8,128)S(1)} %get-tuple-element.45.own_ref), channel_id=1, source_target_pairs={{0,8},{1,17},{2,10},{3,19},{4,12},{5,21},{6,14},{7,23},{8,0},{9,25... | collective-permute-start | bytes 393224 | tf_op jit(solution)/shard_map/ppermute | solution.py:233
  21.9 6.3 %collective-permute-start.9 = (f32[256,128]{1,0:T(8,128)S(1)}, f32[256,128]{1,0:T(8,128)S(1)}, u32[]{:S(2)}, u32[]{:S(2)}) collective-permute-start(f32[256,128]{1,0:T(8,128)S(1)} %get-tuple-element.49.own_ref), channel_id=1, source_target_pairs={{0,16},{1,9},{2,18},{3,11},{4,20},{5,13},{6,22},{7,15},{8,24},{9,1... | collective-permute-start | bytes 393224 | tf_op jit(solution)/shard_map/ppermute | solution.py:233
  25.5 6.3 %collective-permute-start.8 = (f32[256,128]{1,0:T(8,128)S(1)}, f32[256,128]{1,0:T(8,128)S(1)}, u32[]{:S(2)}, u32[]{:S(2)}) collective-permute-start(f32[256,128]{1,0:T(8,128)S(1)} %get-tuple-element.48), channel_id=1, source_target_pairs={{0,16},{1,9},{2,18},{3,11},{4,20},{5,13},{6,22},{7,15},{8,24},{9,1... | collective-permute-start | bytes 393224 | tf_op jit(solution)/shard_map/ppermute | solution.py:239
  28.3 5.0 %collective-permute-start.10 = (f32[256,128]{1,0:T(8,128)S(1)}, f32[256,128]{1,0:T(8,128)S(1)}, u32[]{:S(2)}, u32[]{:S(2)}) collective-permute-start(f32[256,128]{1,0:T(8,128)S(1)} %get-tuple-element.51), channel_id=1, source_target_pairs={{0,8},{1,17},{2,10},{3,19},{4,12},{5,21},{6,14},{7,23},{8,0},{9,25... | collective-permute-start | bytes 393224 | tf_op jit(solution)/shard_map/ppermute | solution.py:239
  33.3 7.6 %copy-start = (f32[1,1,512,512]{3,2,1,0:T(8,128)S(1)}, f32[1,1,512,512]{3,2,1,0:T(8,128)}, u32[]{:S(2)}) copy-start(f32[1,1,512,512]{3,2,1,0:T(8,128)} %param.8) | copy-start | bytes 3145732
  33.7 7.1 %collective-permute-start.11 = (f32[2,80,128]{2,1,0:T(8,128)S(1)}, f32[2,80,128]{2,1,0:T(8,128)S(1)}, u32[]{:S(2)}, u32[]{:S(2)}) collective-permute-start(f32[2,80,128]{2,1,0:T(8,128)S(1)} %get-tuple-element.53), channel_id=1, source_target_pairs={{0,4},{1,5},{2,6},{3,7},{4,0},{5,1},{6,2},{7,3},{8,12},{9,13},{10,... | collective-permute-start | bytes 245768 | tf_op jit(solution)/shard_map/ppermute | solution.py:474
  36.2 5.2 %collective-permute-start.12 = (f32[1,80,128]{2,1,0:T(8,128)S(1)}, f32[1,80,128]{2,1,0:T(8,128)S(1)}, u32[]{:S(2)}, u32[]{:S(2)}) collective-permute-start(f32[1,80,128]{2,1,0:T(8,128)S(1)} %get-tuple-element.54), channel_id=1, source_target_pairs={{0,1},{1,0},{2,3},{3,2},{4,5},{5,4},{6,7},{7,6},{8,9},{9,8},{10,11... | collective-permute-start | bytes 122888 | tf_op jit(solution)/shard_map/ppermute | solution.py:474
  36.7 7.3 %collective-permute-start.15 = (f32[2,80,128]{2,1,0:T(8,128)S(1)}, f32[2,80,128]{2,1,0:T(8,128)S(1)}, u32[]{:S(2)}, u32[]{:S(2)}) collective-permute-start(f32[2,80,128]{2,1,0:T(8,128)S(1)} %get-tuple-element.60), channel_id=1, source_target_pairs={{0,3},{1,4},{2,5},{3,6},{4,7},{5,0},{6,1},{7,2},{8,11},{9,12},{10,... | collective-permute-start | bytes 245768 | tf_op jit(solution)/shard_map/ppermute | solution.py:474
  37.1 6.9 %collective-permute-start.16 = (f32[2,80,128]{2,1,0:T(8,128)S(1)}, f32[2,80,128]{2,1,0:T(8,128)S(1)}, u32[]{:S(2)}, u32[]{:S(2)}) collective-permute-start(f32[2,80,128]{2,1,0:T(8,128)S(1)} %get-tuple-element.61), channel_id=1, source_target_pairs={{0,6},{1,7},{2,0},{3,1},{4,2},{5,3},{6,4},{7,5},{8,14},{9,15},{10,... | collective-permute-start | bytes 245768 | tf_op jit(solution)/shard_map/ppermute | solution.py:474
  40.7 6.9 %collective-permute-start.17 = (f32[2,80,128]{2,1,0:T(8,128)S(1)}, f32[2,80,128]{2,1,0:T(8,128)S(1)}, u32[]{:S(2)}, u32[]{:S(2)}) collective-permute-start(f32[2,80,128]{2,1,0:T(8,128)S(1)} %get-tuple-element.62), channel_id=1, source_target_pairs={{0,2},{1,3},{2,4},{3,5},{4,6},{5,7},{6,0},{7,1},{8,10},{9,11},{10,... | collective-permute-start | bytes 245768 | tf_op jit(solution)/shard_map/ppermute | solution.py:474
  40.7 6.9 %collective-permute-start.14 = (f32[2,80,128]{2,1,0:T(8,128)S(1)}, f32[2,80,128]{2,1,0:T(8,128)S(1)}, u32[]{:S(2)}, u32[]{:S(2)}) collective-permute-start(f32[2,80,128]{2,1,0:T(8,128)S(1)} %get-tuple-element.58.refs_2_), channel_id=1, source_target_pairs={{0,5},{1,6},{2,7},{3,0},{4,1},{5,2},{6,3},{7,4},{8,13},{9,14},{10,... | collective-permute-start | bytes 245768 | tf_op jit(solution)/shard_map/ppermute | solution.py:474
  41.4 6.3 %collective-permute-start.13 = (f32[1,80,128]{2,1,0:T(8,128)S(1)}, f32[1,80,128]{2,1,0:T(8,128)S(1)}, u32[]{:S(2)}, u32[]{:S(2)}) collective-permute-start(f32[1,80,128]{2,1,0:T(8,128)S(1)} %shard_map.92), channel_id=1, source_target_pairs={{0,7},{1,2},{2,1},{3,4},{4,3},{5,6},{6,5},{7,0},{8,15},{9,10},{10,... | collective-permute-start | bytes 122888 | tf_op jit(solution)/shard_map/ppermute | solution.py:474

commit v7 on v6

--- a/solution.py
+++ b/solution.py
@@ -474,11 +474,11 @@
     return lax.ppermute(value, "tile", message.pairs)
 
 
-def send_all(one, two, coeffs, more, waited, beside):
+def send_all(one, two, coeffs, more, beside):
     gots = []
     for value, message in zip(coeffs, one):
         if message.odd_slots is not None and message.across:
-            value = relay([value], [gots[waited], more[0], beside])[0]
+            value = relay([value], [gots[-1], more[0], beside])[0]
         gots.append(send(value, message))
     return gots + [send(value, message) for value, message in zip(more, two)]
 
@@ -510,13 +510,13 @@
     coeffs, split_one, both, rest = first_coefficients(cols, right_tile, one, two)
     more, split_two = rest_coefficients(both, rest, two)
     diag_part, left_split, weights = prepare(diag_tile, cols, left_rows, table, index, halves)
-    gots = send_all(one, two, coeffs, more, -1, diag_part)
+    gots = send_all(one, two, coeffs, more, diag_part)
     first = rows(offsets, ranks, gots, messages, left_split, diag_part, slots, halves, False)
     mixed = mix(first, weights)
     coeffs, cols, both = mixed_coefficients(mixed, split_one, one, rank)
     more = next_coefficients(both, split_two, two, rank)
     diag_part = diagonal(diag_tile, cols)
-    gots = send_all(one, two, coeffs, more, 0, diag_part)
+    gots = send_all(one, two, coeffs, more, diag_part)
     return rows(offsets, ranks, gots, messages, left_split, diag_part, slots, halves, True)[None]
 
 

time: 50.3 us -> 51.5 us (1.024)
  waiting for transfers between devices: 11.9 us -> 15.7 us
  starting transfers between devices: 28.3 us -> 25.8 us
    ppermute x14, waiting for transfers between devices: 6.31 us -> 10.1 us  [send(): return lax.ppermute(value, 'tile', message.pairs)]
    ppermute x14, starting transfers between devices: 21 us -> 18.5 us  [send(): return lax.ppermute(value, 'tile', message.pairs)]
  transfers between devices with their start and end apart: 18 -> 18, of which waited for: 7 -> 9; matrix products, arithmetic and copies ran while one was open for 0% -> 0% of each run, Pallas kernels for 8% -> 8%
where the time goes in v7:
time: 51.5 us; the launch traced here: 50.9 us
  starting transfers between devices  25.8 us (50%)
  waiting for transfers between devices  15.7 us (30%)
  Pallas kernels  9.28 us (18%)
    ppermute x14, starting transfers between devices, send(): return lax.ppermute(value, 'tile', message.pairs)  18.5 us
    ppermute x14, waiting for transfers between devices, send(): return lax.ppermute(value, 'tile', message.pairs)  10.1 us
    ppermute x2, starting transfers between devices, mix(): lax.ppermute(send, axes, pairs)  4.21 us
    ppermute x2, waiting for transfers between devices, mix(): lax.ppermute(send, axes, pairs)  3.53 us
    pallas_call x2, Pallas kernels, rows(): call(functools.partial(row_kernel, messages, halves, final), pltpu.HBM((s...  3.1 us
    ppermute x2, starting transfers between devices, mix(): lax.ppermute(part, axes, pairs)  3.07 us
    pallas_call x1, Pallas kernels, prepare(): call(functools.partial(prepare_kernel, halves), [struct(size, width), str...  2.21 us
    ppermute x2, waiting for transfers between devices, mix(): lax.ppermute(part, axes, pairs)  2.05 us
  transfers between devices with their start and end apart: 18, of which 9 were waited for; matrix products, arithmetic and copies ran while one was open for 0% of the time, Pallas kernels for 8%

profile of v7, /device:TPU:0, one launch (start us, length us, event | category | flops | bytes accessed | tf_op | source)
XLA Modules:
  0.0 50.9 jit_solution(16418686787123241473)
XLA Ops:
  0.0 2.0 %shard_map.82 = (f32[2,80,128]{2,1,0:T(8,128)S(1)}, f32[1,80,128]{2,1,0:T(8,128)S(1)}, f32[1,80,128]{2,1,0:T(8,128)S(1)}, bf16[640,512]{1,0:T(8,128)(2,1)S(1)}, ...) custom-call(f32[512,128]{1,0:T(8,128)} %bitcast.21, f32[12,80,512]{2,1,0:T(8,128)} %bitcast.19), custom_call_target="tpu_custom_call" | custom-call | flops 167772160 | bytes 1966080 | tf_op jit(solution)/shard_map/pallas_call | solution.py:161
  2.5 3.7 %collective-permute-start = (f32[2,80,128]{2,1,0:T(8,128)S(1)}, f32[2,80,128]{2,1,0:T(8,128)S(1)}, u32[]{:S(2)}, u32[]{:S(2)}) collective-permute-start(f32[2,80,128]{2,1,0:T(8,128)S(1)} %get-tuple-element.34), channel_id=1, source_target_pairs={{0,4},{1,5},{2,6},{3,7},{4,0},{5,1},{6,2},{7,3},{8,12},{9,13},{10,... | collective-permute-start | bytes 245768 | tf_op jit(solution)/shard_map/ppermute | solution.py:474
  6.2 0.6 %shard_map.83 = (f32[2,80,128]{2,1,0:T(8,128)S(1)}, f32[2,80,128]{2,1,0:T(8,128)S(1)}, f32[2,80,128]{2,1,0:T(8,128)S(1)}, f32[2,80,128]{2,1,0:T(8,128)S(1)}, bf16[1280,512]{1,0:T(8,128)(2,1)S(1)}) custom-call(bf16[512,256]{1,0:T(8,128)(2,1)S(1)} %get-tuple-element.37.both_ref, f32[8,80,512]{2,1,0:T(8,128)S(1)} %get-tuple-element.38.right_ref), custom_call_target="tpu_custom_call" | custom-call | flops 335544320 | bytes 2621440 | tf_op jit(solution)/shard_map/pallas_call | solution.py:190
  6.8 1.4 %collective-permute-start.4 = (f32[2,80,128]{2,1,0:T(8,128)S(1)}, f32[2,80,128]{2,1,0:T(8,128)S(1)}, u32[]{:S(2)}, u32[]{:S(2)}) collective-permute-start(f32[2,80,128]{2,1,0:T(8,128)S(1)} %get-tuple-element.41), channel_id=1, source_target_pairs={{0,3},{1,4},{2,5},{3,6},{4,7},{5,0},{6,1},{7,2},{8,11},{9,12},{10,... | collective-permute-start | bytes 245768 | tf_op jit(solution)/shard_map/ppermute | solution.py:474
  8.1 2.3 %collective-permute-start.5 = (f32[2,80,128]{2,1,0:T(8,128)S(1)}, f32[2,80,128]{2,1,0:T(8,128)S(1)}, u32[]{:S(2)}, u32[]{:S(2)}) collective-permute-start(f32[2,80,128]{2,1,0:T(8,128)S(1)} %get-tuple-element.42), channel_id=1, source_target_pairs={{0,6},{1,7},{2,0},{3,1},{4,2},{5,3},{6,4},{7,5},{8,14},{9,15},{10,... | collective-permute-start | bytes 245768 | tf_op jit(solution)/shard_map/ppermute | solution.py:474
  10.9 2.2 %shard_map.84 = (f32[512,128]{1,0:T(8,128)S(1)}, bf16[1024,640]{1,0:T(8,128)(2,1)S(1)}, f32[8,256,128]{2,1,0:T(8,128)S(1)}) custom-call(f32[512,512]{1,0:T(8,128)} %bitcast.11, f32[512,128]{1,0:T(8,128)} %bitcast.22, f32[640,512]{1,0:T(8,128)} %bitcast.20, f32[16,64]{1,0:T(8,128)S(1)} %bitcast.13, s32[1,512]{1,0:T(1,128)S(1)} %bitcast.14), custom_call_target="tpu_custom_call" | custom-call | flops 268435456 | bytes 4194304 | tf_op jit(solution)/shard_map/pallas_call | solution.py:385
  13.2 3.3 %collective-permute-start.2 = (f32[1,80,128]{2,1,0:T(8,128)S(1)}, f32[1,80,128]{2,1,0:T(8,128)S(1)}, u32[]{:S(2)}, u32[]{:S(2)}) collective-permute-start(f32[1,80,128]{2,1,0:T(8,128)S(1)} %shard_map.85), channel_id=1, source_target_pairs={{0,7},{1,2},{2,1},{3,4},{4,3},{5,6},{6,5},{7,0},{8,15},{9,10},{10,... | collective-permute-start | bytes 122888 | tf_op jit(solution)/shard_map/ppermute | solution.py:474
  16.5 1.1 %collective-permute-done.6.refs_6_ = f32[2,80,128]{2,1,0:T(8,128)S(1)} collective-permute-done((f32[2,80,128]{2,1,0:T(8,128)S(1)}, f32[2,80,128]{2,1,0:T(8,128)S(1)}, u32[]{:S(2)}, u32[]{:S(2)}) %collective-permute-start.6) | collective-permute-done | bytes 81952 | tf_op jit(solution)/shard_map/ppermute | solution.py:474
  17.6 1.5 %collective-permute-done.2.refs_2_ = f32[1,80,128]{2,1,0:T(8,128)S(1)} collective-permute-done((f32[1,80,128]{2,1,0:T(8,128)S(1)}, f32[1,80,128]{2,1,0:T(8,128)S(1)}, u32[]{:S(2)}, u32[]{:S(2)}) %collective-permute-start.2) | collective-permute-done | bytes 40992 | tf_op jit(solution)/shard_map/ppermute | solution.py:474
  19.1 1.2 %shard_map.86 = (f32[256,128]{1,0:T(8,128)S(1)}, f32[256,128]{1,0:T(8,128)S(1)}) custom-call(s32[1,8]{1,0:T(1,128)S(1)} %bitcast.15, s32[1,8]{1,0:T(1,128)S(1)} %bitcast.17, f32[2,80,128]{2,1,0:T(8,128)S(1)} %collective-permute-done.refs_0_, f32[1,80,128]{2,1,0:T(8,128)S(1)} %collective-permute-done.1.refs_1_, ...), custom_call_target="tpu_custom_call" | custom-call | flops 335544320 | bytes 1638400 | tf_op jit(solution)/shard_map/pallas_call | solution.py:462
  20.3 1.6 %collective-permute-start.7 = (f32[256,128]{1,0:T(8,128)S(1)}, f32[256,128]{1,0:T(8,128)S(1)}, u32[]{:S(2)}, u32[]{:S(2)}) collective-permute-start(f32[256,128]{1,0:T(8,128)S(1)} %get-tuple-element.45.own_ref), channel_id=1, source_target_pairs={{0,8},{1,17},{2,10},{3,19},{4,12},{5,21},{6,14},{7,23},{8,0},{9,25... | collective-permute-start | bytes 393224 | tf_op jit(solution)/shard_map/ppermute | solution.py:233
  21.9 1.5 %collective-permute-start.9 = (f32[256,128]{1,0:T(8,128)S(1)}, f32[256,128]{1,0:T(8,128)S(1)}, u32[]{:S(2)}, u32[]{:S(2)}) collective-permute-start(f32[256,128]{1,0:T(8,128)S(1)} %get-tuple-element.49.own_ref), channel_id=1, source_target_pairs={{0,16},{1,9},{2,18},{3,11},{4,20},{5,13},{6,22},{7,15},{8,24},{9,1... | collective-permute-start | bytes 393224 | tf_op jit(solution)/shard_map/ppermute | solution.py:233
  23.4 2.0 %collective-permute-done.7.got_ref = f32[256,128]{1,0:T(8,128)S(1)} collective-permute-done((f32[256,128]{1,0:T(8,128)S(1)}, f32[256,128]{1,0:T(8,128)S(1)}, u32[]{:S(2)}, u32[]{:S(2)}) %collective-permute-start.7) | collective-permute-done | bytes 131104 | tf_op jit(solution)/shard_map/ppermute | solution.py:233
  25.5 2.7 %collective-permute-start.8 = (f32[256,128]{1,0:T(8,128)S(1)}, f32[256,128]{1,0:T(8,128)S(1)}, u32[]{:S(2)}, u32[]{:S(2)}) collective-permute-start(f32[256,128]{1,0:T(8,128)S(1)} %get-tuple-element.48), channel_id=1, source_target_pairs={{0,16},{1,9},{2,18},{3,11},{4,20},{5,13},{6,22},{7,15},{8,24},{9,1... | collective-permute-start | bytes 393224 | tf_op jit(solution)/shard_map/ppermute | solution.py:239
  28.3 1.5 %collective-permute-start.10 = (f32[256,128]{1,0:T(8,128)S(1)}, f32[256,128]{1,0:T(8,128)S(1)}, u32[]{:S(2)}, u32[]{:S(2)}) collective-permute-start(f32[256,128]{1,0:T(8,128)S(1)} %get-tuple-element.51), channel_id=1, source_target_pairs={{0,8},{1,17},{2,10},{3,19},{4,12},{5,21},{6,14},{7,23},{8,0},{9,25... | collective-permute-start | bytes 393224 | tf_op jit(solution)/shard_map/ppermute | solution.py:239
  29.8 2.1 %collective-permute-done.8.refs_1_ = f32[256,128]{1,0:T(8,128)S(1)} collective-permute-done((f32[256,128]{1,0:T(8,128)S(1)}, f32[256,128]{1,0:T(8,128)S(1)}, u32[]{:S(2)}, u32[]{:S(2)}) %collective-permute-start.8) | collective-permute-done | bytes 131104 | tf_op jit(solution)/shard_map/ppermute | solution.py:239
  31.8 1.5 %collective-permute-done.10.refs_3_ = f32[256,128]{1,0:T(8,128)S(1)} collective-permute-done((f32[256,128]{1,0:T(8,128)S(1)}, f32[256,128]{1,0:T(8,128)S(1)}, u32[]{:S(2)}, u32[]{:S(2)}) %collective-permute-start.10) | collective-permute-done | bytes 131104 | tf_op jit(solution)/shard_map/ppermute | solution.py:239
  33.7 2.6 %collective-permute-start.11 = (f32[2,80,128]{2,1,0:T(8,128)S(1)}, f32[2,80,128]{2,1,0:T(8,128)S(1)}, u32[]{:S(2)}, u32[]{:S(2)}) collective-permute-start(f32[2,80,128]{2,1,0:T(8,128)S(1)} %get-tuple-element.53), channel_id=1, source_target_pairs={{0,4},{1,5},{2,6},{3,7},{4,0},{5,1},{6,2},{7,3},{8,12},{9,13},{10,... | collective-permute-start | bytes 245768 | tf_op jit(solution)/shard_map/ppermute | solution.py:474
  36.9 3.6 %collective-permute-start.16 = (f32[2,80,128]{2,1,0:T(8,128)S(1)}, f32[2,80,128]{2,1,0:T(8,128)S(1)}, u32[]{:S(2)}, u32[]{:S(2)}) collective-permute-start(f32[2,80,128]{2,1,0:T(8,128)S(1)} %get-tuple-element.61), channel_id=1, source_target_pairs={{0,6},{1,7},{2,0},{3,1},{4,2},{5,3},{6,4},{7,5},{8,14},{9,15},{10,... | collective-permute-start | bytes 245768 | tf_op jit(solution)/shard_map/ppermute | solution.py:474
  41.5 1.8 %collective-permute-done.11.refs_0_ = f32[2,80,128]{2,1,0:T(8,128)S(1)} collective-permute-done((f32[2,80,128]{2,1,0:T(8,128)S(1)}, f32[2,80,128]{2,1,0:T(8,128)S(1)}, u32[]{:S(2)}, u32[]{:S(2)}) %collective-permute-start.11) | collective-permute-done | bytes 81952 | tf_op jit(solution)/shard_map/ppermute | solution.py:474
  43.3 1.7 %collective-permute-done.15.refs_4_ = f32[2,80,128]{2,1,0:T(8,128)S(1)} collective-permute-done((f32[2,80,128]{2,1,0:T(8,128)S(1)}, f32[2,80,128]{2,1,0:T(8,128)S(1)}, u32[]{:S(2)}, u32[]{:S(2)}) %collective-permute-start.15) | collective-permute-done | bytes 81952 | tf_op jit(solution)/shard_map/ppermute | solution.py:474
  45.0 2.3 %collective-permute-done.17.refs_6_ = f32[2,80,128]{2,1,0:T(8,128)S(1)} collective-permute-done((f32[2,80,128]{2,1,0:T(8,128)S(1)}, f32[2,80,128]{2,1,0:T(8,128)S(1)}, u32[]{:S(2)}, u32[]{:S(2)}) %collective-permute-start.17) | collective-permute-done | bytes 81952 | tf_op jit(solution)/shard_map/ppermute | solution.py:474
  47.2 1.8 %collective-permute-done.13.refs_2_ = f32[1,80,128]{2,1,0:T(8,128)S(1)} collective-permute-done((f32[1,80,128]{2,1,0:T(8,128)S(1)}, f32[1,80,128]{2,1,0:T(8,128)S(1)}, u32[]{:S(2)}, u32[]{:S(2)}) %collective-permute-start.13) | collective-permute-done | bytes 40992 | tf_op jit(solution)/shard_map/ppermute | solution.py:474
  49.0 1.9 %shard_map.93 = f32[512,128]{1,0:T(8,128)} custom-call(s32[1,8]{1,0:T(1,128)S(1)} %bitcast.16, s32[1,8]{1,0:T(1,128)S(1)} %bitcast.18, f32[2,80,128]{2,1,0:T(8,128)S(1)} %collective-permute-done.11.refs_0_, f32[1,80,128]{2,1,0:T(8,128)S(1)} %collective-permute-done.12.refs_1_, f32[1,80,128]{2,1,0:T(8,128)S(1)} %collective-permute-done.13.refs_2_, ...), custom_call_target="tpu_custom_call" | custom-call | flops 335544320 | bytes 1638400 | tf_op jit(solution)/shard_map/pallas_call | solution.py:462
  (34 shorter events, 3.2 us)
Async XLA Ops:
  2.0 9.0 %copy-start.1 = (f32[64,4,4]{0,2,1:T(4,128)S(1)}, f32[64,4,4]{0,2,1:T(4,128)}, u32[]{:S(2)}) copy-start(f32[64,4,4]{0,2,1:T(4,128)} %param.13) | copy-start | bytes 12292
  2.0 9.0 %copy-start.2 = (s32[512]{0:T(512)S(1)}, s32[512]{0:T(512)}, u32[]{:S(2)}) copy-start(s32[512]{0:T(512)} %param.14) | copy-start | bytes 6148
  2.0 8.4 %collective-permute-start.1 = (f32[1,80,128]{2,1,0:T(8,128)S(1)}, f32[1,80,128]{2,1,0:T(8,128)S(1)}, u32[]{:S(2)}, u32[]{:S(2)}) collective-permute-start(f32[1,80,128]{2,1,0:T(8,128)S(1)} %get-tuple-element.35), channel_id=1, source_target_pairs={{0,1},{1,0},{2,3},{3,2},{4,5},{5,4},{6,7},{7,6},{8,9},{9,8},{10,11... | collective-permute-start | bytes 122888 | tf_op jit(solution)/shard_map/ppermute | solution.py:474
  2.5 10.7 %collective-permute-start = (f32[2,80,128]{2,1,0:T(8,128)S(1)}, f32[2,80,128]{2,1,0:T(8,128)S(1)}, u32[]{:S(2)}, u32[]{:S(2)}) collective-permute-start(f32[2,80,128]{2,1,0:T(8,128)S(1)} %get-tuple-element.34), channel_id=1, source_target_pairs={{0,4},{1,5},{2,6},{3,7},{4,0},{5,1},{6,2},{7,3},{8,12},{9,13},{10,... | collective-permute-start | bytes 245768 | tf_op jit(solution)/shard_map/ppermute | solution.py:474
  6.8 9.8 %collective-permute-start.4 = (f32[2,80,128]{2,1,0:T(8,128)S(1)}, f32[2,80,128]{2,1,0:T(8,128)S(1)}, u32[]{:S(2)}, u32[]{:S(2)}) collective-permute-start(f32[2,80,128]{2,1,0:T(8,128)S(1)} %get-tuple-element.41), channel_id=1, source_target_pairs={{0,3},{1,4},{2,5},{3,6},{4,7},{5,0},{6,1},{7,2},{8,11},{9,12},{10,... | collective-permute-start | bytes 245768 | tf_op jit(solution)/shard_map/ppermute | solution.py:474
  8.1 8.4 %collective-permute-start.5 = (f32[2,80,128]{2,1,0:T(8,128)S(1)}, f32[2,80,128]{2,1,0:T(8,128)S(1)}, u32[]{:S(2)}, u32[]{:S(2)}) collective-permute-start(f32[2,80,128]{2,1,0:T(8,128)S(1)} %get-tuple-element.42), channel_id=1, source_target_pairs={{0,6},{1,7},{2,0},{3,1},{4,2},{5,3},{6,4},{7,5},{8,14},{9,15},{10,... | collective-permute-start | bytes 245768 | tf_op jit(solution)/shard_map/ppermute | solution.py:474
  10.4 7.2 %collective-permute-start.6 = (f32[2,80,128]{2,1,0:T(8,128)S(1)}, f32[2,80,128]{2,1,0:T(8,128)S(1)}, u32[]{:S(2)}, u32[]{:S(2)}) collective-permute-start(f32[2,80,128]{2,1,0:T(8,128)S(1)} %get-tuple-element.43), channel_id=1, source_target_pairs={{0,2},{1,3},{2,4},{3,5},{4,6},{5,7},{6,0},{7,1},{8,10},{9,11},{10,... | collective-permute-start | bytes 245768 | tf_op jit(solution)/shard_map/ppermute | solution.py:474
  10.4 7.2 %collective-permute-start.3 = (f32[2,80,128]{2,1,0:T(8,128)S(1)}, f32[2,80,128]{2,1,0:T(8,128)S(1)}, u32[]{:S(2)}, u32[]{:S(2)}) collective-permute-start(f32[2,80,128]{2,1,0:T(8,128)S(1)} %get-tuple-element.39.refs_2_), channel_id=1, source_target_pairs={{0,5},{1,6},{2,7},{3,0},{4,1},{5,2},{6,3},{7,4},{8,13},{9,14},{10,... | collective-permute-start | bytes 245768 | tf_op jit(solution)/shard_map/ppermute | solution.py:474
  10.9 8.2 %copy-start.3 = (s32[1,1,8]{2,1,0:T(1,128)S(1)}, s32[1,1,8]{2,1,0:T(1,128)}, u32[]{:S(2)}) copy-start(s32[1,1,8]{2,1,0:T(1,128)} %param.11) | copy-start | bytes 100
  10.9 8.2 %copy-start.4 = (s32[1,1,8]{2,1,0:T(1,128)S(1)}, s32[1,1,8]{2,1,0:T(1,128)}, u32[]{:S(2)}) copy-start(s32[1,1,8]{2,1,0:T(1,128)} %param.12) | copy-start | bytes 100
  13.2 5.9 %collective-permute-start.2 = (f32[1,80,128]{2,1,0:T(8,128)S(1)}, f32[1,80,128]{2,1,0:T(8,128)S(1)}, u32[]{:S(2)}, u32[]{:S(2)}) collective-permute-start(f32[1,80,128]{2,1,0:T(8,128)S(1)} %shard_map.85), channel_id=1, source_target_pairs={{0,7},{1,2},{2,1},{3,4},{4,3},{5,6},{6,5},{7,0},{8,15},{9,10},{10,... | collective-permute-start | bytes 122888 | tf_op jit(solution)/shard_map/ppermute | solution.py:474
  20.3 5.1 %collective-permute-start.7 = (f32[256,128]{1,0:T(8,128)S(1)}, f32[256,128]{1,0:T(8,128)S(1)}, u32[]{:S(2)}, u32[]{:S(2)}) collective-permute-start(f32[256,128]{1,0:T(8,128)S(1)} %get-tuple-element.45.own_ref), channel_id=1, source_target_pairs={{0,8},{1,17},{2,10},{3,19},{4,12},{5,21},{6,14},{7,23},{8,0},{9,25... | collective-permute-start | bytes 393224 | tf_op jit(solution)/shard_map/ppermute | solution.py:233
  21.9 6.3 %collective-permute-start.9 = (f32[256,128]{1,0:T(8,128)S(1)}, f32[256,128]{1,0:T(8,128)S(1)}, u32[]{:S(2)}, u32[]{:S(2)}) collective-permute-start(f32[256,128]{1,0:T(8,128)S(1)} %get-tuple-element.49.own_ref), channel_id=1, source_target_pairs={{0,16},{1,9},{2,18},{3,11},{4,20},{5,13},{6,22},{7,15},{8,24},{9,1... | collective-permute-start | bytes 393224 | tf_op jit(solution)/shard_map/ppermute | solution.py:233
  25.5 6.3 %collective-permute-start.8 = (f32[256,128]{1,0:T(8,128)S(1)}, f32[256,128]{1,0:T(8,128)S(1)}, u32[]{:S(2)}, u32[]{:S(2)}) collective-permute-start(f32[256,128]{1,0:T(8,128)S(1)} %get-tuple-element.48), channel_id=1, source_target_pairs={{0,16},{1,9},{2,18},{3,11},{4,20},{5,13},{6,22},{7,15},{8,24},{9,1... | collective-permute-start | bytes 393224 | tf_op jit(solution)/shard_map/ppermute | solution.py:239
  28.3 5.0 %collective-permute-start.10 = (f32[256,128]{1,0:T(8,128)S(1)}, f32[256,128]{1,0:T(8,128)S(1)}, u32[]{:S(2)}, u32[]{:S(2)}) collective-permute-start(f32[256,128]{1,0:T(8,128)S(1)} %get-tuple-element.51), channel_id=1, source_target_pairs={{0,8},{1,17},{2,10},{3,19},{4,12},{5,21},{6,14},{7,23},{8,0},{9,25... | collective-permute-start | bytes 393224 | tf_op jit(solution)/shard_map/ppermute | solution.py:239
  33.3 7.7 %copy-start = (f32[1,1,512,512]{3,2,1,0:T(8,128)S(1)}, f32[1,1,512,512]{3,2,1,0:T(8,128)}, u32[]{:S(2)}) copy-start(f32[1,1,512,512]{3,2,1,0:T(8,128)} %param.8) | copy-start | bytes 3145732
  33.7 6.8 %collective-permute-start.12 = (f32[1,80,128]{2,1,0:T(8,128)S(1)}, f32[1,80,128]{2,1,0:T(8,128)S(1)}, u32[]{:S(2)}, u32[]{:S(2)}) collective-permute-start(f32[1,80,128]{2,1,0:T(8,128)S(1)} %get-tuple-element.54), channel_id=1, source_target_pairs={{0,1},{1,0},{2,3},{3,2},{4,5},{5,4},{6,7},{7,6},{8,9},{9,8},{10,11... | collective-permute-start | bytes 122888 | tf_op jit(solution)/shard_map/ppermute | solution.py:474
  33.7 9.6 %collective-permute-start.11 = (f32[2,80,128]{2,1,0:T(8,128)S(1)}, f32[2,80,128]{2,1,0:T(8,128)S(1)}, u32[]{:S(2)}, u32[]{:S(2)}) collective-permute-start(f32[2,80,128]{2,1,0:T(8,128)S(1)} %get-tuple-element.53), channel_id=1, source_target_pairs={{0,4},{1,5},{2,6},{3,7},{4,0},{5,1},{6,2},{7,3},{8,12},{9,13},{10,... | collective-permute-start | bytes 245768 | tf_op jit(solution)/shard_map/ppermute | solution.py:474
  36.8 8.1 %collective-permute-start.15 = (f32[2,80,128]{2,1,0:T(8,128)S(1)}, f32[2,80,128]{2,1,0:T(8,128)S(1)}, u32[]{:S(2)}, u32[]{:S(2)}) collective-permute-start(f32[2,80,128]{2,1,0:T(8,128)S(1)} %get-tuple-element.60), channel_id=1, source_target_pairs={{0,3},{1,4},{2,5},{3,6},{4,7},{5,0},{6,1},{7,2},{8,11},{9,12},{10,... | collective-permute-start | bytes 245768 | tf_op jit(solution)/shard_map/ppermute | solution.py:474
  36.9 8.1 %collective-permute-start.16 = (f32[2,80,128]{2,1,0:T(8,128)S(1)}, f32[2,80,128]{2,1,0:T(8,128)S(1)}, u32[]{:S(2)}, u32[]{:S(2)}) collective-permute-start(f32[2,80,128]{2,1,0:T(8,128)S(1)} %get-tuple-element.61), channel_id=1, source_target_pairs={{0,6},{1,7},{2,0},{3,1},{4,2},{5,3},{6,4},{7,5},{8,14},{9,15},{10,... | collective-permute-start | bytes 245768 | tf_op jit(solution)/shard_map/ppermute | solution.py:474
  40.5 6.7 %collective-permute-start.17 = (f32[2,80,128]{2,1,0:T(8,128)S(1)}, f32[2,80,128]{2,1,0:T(8,128)S(1)}, u32[]{:S(2)}, u32[]{:S(2)}) collective-permute-start(f32[2,80,128]{2,1,0:T(8,128)S(1)} %get-tuple-element.62), channel_id=1, source_target_pairs={{0,2},{1,3},{2,4},{3,5},{4,6},{5,7},{6,0},{7,1},{8,10},{9,11},{10,... | collective-permute-start | bytes 245768 | tf_op jit(solution)/shard_map/ppermute | solution.py:474
  40.5 6.7 %collective-permute-start.14 = (f32[2,80,128]{2,1,0:T(8,128)S(1)}, f32[2,80,128]{2,1,0:T(8,128)S(1)}, u32[]{:S(2)}, u32[]{:S(2)}) collective-permute-start(f32[2,80,128]{2,1,0:T(8,128)S(1)} %get-tuple-element.58.refs_2_), channel_id=1, source_target_pairs={{0,5},{1,6},{2,7},{3,0},{4,1},{5,2},{6,3},{7,4},{8,13},{9,14},{10,... | collective-permute-start | bytes 245768 | tf_op jit(solution)/shard_map/ppermute | solution.py:474
  43.3 5.7 %collective-permute-start.13 = (f32[1,80,128]{2,1,0:T(8,128)S(1)}, f32[1,80,128]{2,1,0:T(8,128)S(1)}, u32[]{:S(2)}, u32[]{:S(2)}) collective-permute-start(f32[1,80,128]{2,1,0:T(8,128)S(1)} %shard_map.92), channel_id=1, source_target_pairs={{0,7},{1,2},{2,1},{3,4},{4,3},{5,6},{6,5},{7,0},{8,15},{9,10},{10,... | collective-permute-start | bytes 122888 | tf_op jit(solution)/shard_map/ppermute | solution.py:474

commit v8 on v6

--- a/solution.py
+++ b/solution.py
@@ -81,7 +81,8 @@
         messages.append(Message([(at, (at - ahead) % count) for at in range(count)], group))
     messages.sort(key=lambda message: -message.across)
     first = messages[:1] + [m for m in messages[:0:-1] if m.odd_slots is not None]
-    return [first, [message for message in messages if message not in first]]
+    rest = [message for message in messages if message not in first]
+    return [first, rest[-1:] + rest[:-1]]
 
 
 def slots_of(messages):

time: 50.3 us -> 50.4 us (level); the launches traced: 49.6 us -> 50.2 us
  starting transfers between devices: 28.3 us -> 29.5 us
  waiting for transfers between devices: 11.9 us -> 11.2 us
    ppermute x14, starting transfers between devices: 21 us -> 23.6 us  [send(): return lax.ppermute(value, 'tile', message.pairs)]
    ppermute x2, starting transfers between devices: 4.21 us -> 2.85 us  [mix(): lax.ppermute(send, axes, pairs)]
    ppermute x14, waiting for transfers between devices: 6.31 us -> 5.53 us  [send(): return lax.ppermute(value, 'tile', message.pairs)]
  transfers between devices with their start and end apart: 18 -> 18, of which waited for: 7 -> 8; matrix products, arithmetic and copies ran while one was open for 0% -> 0% of each run, Pallas kernels for 8% -> 8%
where the time goes in v8:
time: 50.4 us; the launch traced here: 50.2 us
  starting transfers between devices  29.5 us (59%)
  waiting for transfers between devices  11.2 us (22%)
  Pallas kernels  9.26 us (18%)
    ppermute x14, starting transfers between devices, send(): return lax.ppermute(value, 'tile', message.pairs)  23.6 us
    ppermute x14, waiting for transfers between devices, send(): return lax.ppermute(value, 'tile', message.pairs)  5.53 us
    ppermute x2, waiting for transfers between devices, mix(): lax.ppermute(send, axes, pairs)  3.47 us
    pallas_call x2, Pallas kernels, rows(): call(functools.partial(row_kernel, messages, halves, final), pltpu.HBM((s...  3.1 us
    ppermute x2, starting transfers between devices, mix(): lax.ppermute(part, axes, pairs)  3.08 us
    ppermute x2, starting transfers between devices, mix(): lax.ppermute(send, axes, pairs)  2.85 us
    ppermute x2, waiting for transfers between devices, mix(): lax.ppermute(part, axes, pairs)  2.25 us
    pallas_call x1, Pallas kernels, prepare(): call(functools.partial(prepare_kernel, halves), [struct(size, width), str...  2.21 us
  transfers between devices with their start and end apart: 18, of which 8 were waited for; matrix products, arithmetic and copies ran while one was open for 0% of the time, Pallas kernels for 8%

profile of v8, /device:TPU:0, one launch (start us, length us, event | category | flops | bytes accessed | tf_op | source)
XLA Modules:
  0.0 50.2 jit_solution(16070673755183260444)
XLA Ops:
  0.0 2.0 %shard_map.82 = (f32[2,80,128]{2,1,0:T(8,128)S(1)}, f32[1,80,128]{2,1,0:T(8,128)S(1)}, f32[1,80,128]{2,1,0:T(8,128)S(1)}, bf16[640,512]{1,0:T(8,128)(2,1)S(1)}, ...) custom-call(f32[512,128]{1,0:T(8,128)} %bitcast.21, f32[12,80,512]{2,1,0:T(8,128)} %bitcast.19), custom_call_target="tpu_custom_call" | custom-call | flops 167772160 | bytes 1966080 | tf_op jit(solution)/shard_map/pallas_call | solution.py:162
  2.5 3.7 %collective-permute-start = (f32[2,80,128]{2,1,0:T(8,128)S(1)}, f32[2,80,128]{2,1,0:T(8,128)S(1)}, u32[]{:S(2)}, u32[]{:S(2)}) collective-permute-start(f32[2,80,128]{2,1,0:T(8,128)S(1)} %get-tuple-element.34), channel_id=1, source_target_pairs={{0,4},{1,5},{2,6},{3,7},{4,0},{5,1},{6,2},{7,3},{8,12},{9,13},{10,... | collective-permute-start | bytes 245768 | tf_op jit(solution)/shard_map/ppermute | solution.py:475
  6.2 0.6 %shard_map.83 = (f32[2,80,128]{2,1,0:T(8,128)S(1)}, f32[2,80,128]{2,1,0:T(8,128)S(1)}, f32[2,80,128]{2,1,0:T(8,128)S(1)}, f32[2,80,128]{2,1,0:T(8,128)S(1)}, bf16[1280,512]{1,0:T(8,128)(2,1)S(1)}) custom-call(bf16[512,256]{1,0:T(8,128)(2,1)S(1)} %get-tuple-element.37.both_ref, f32[8,80,512]{2,1,0:T(8,128)S(1)} %get-tuple-element.38.right_ref), custom_call_target="tpu_custom_call" | custom-call | flops 335544320 | bytes 2621440 | tf_op jit(solution)/shard_map/pallas_call | solution.py:191
  6.8 1.7 %collective-permute-start.5 = (f32[2,80,128]{2,1,0:T(8,128)S(1)}, f32[2,80,128]{2,1,0:T(8,128)S(1)}, u32[]{:S(2)}, u32[]{:S(2)}) collective-permute-start(f32[2,80,128]{2,1,0:T(8,128)S(1)} %get-tuple-element.42), channel_id=1, source_target_pairs={{0,3},{1,4},{2,5},{3,6},{4,7},{5,0},{6,1},{7,2},{8,11},{9,12},{10,... | collective-permute-start | bytes 245768 | tf_op jit(solution)/shard_map/ppermute | solution.py:475
  8.6 3.1 %collective-permute-start.6 = (f32[2,80,128]{2,1,0:T(8,128)S(1)}, f32[2,80,128]{2,1,0:T(8,128)S(1)}, u32[]{:S(2)}, u32[]{:S(2)}) collective-permute-start(f32[2,80,128]{2,1,0:T(8,128)S(1)} %get-tuple-element.43), channel_id=1, source_target_pairs={{0,6},{1,7},{2,0},{3,1},{4,2},{5,3},{6,4},{7,5},{8,14},{9,15},{10,... | collective-permute-start | bytes 245768 | tf_op jit(solution)/shard_map/ppermute | solution.py:475
  11.8 2.2 %shard_map.84 = (f32[512,128]{1,0:T(8,128)S(1)}, bf16[1024,640]{1,0:T(8,128)(2,1)S(1)}, f32[8,256,128]{2,1,0:T(8,128)S(1)}) custom-call(f32[512,512]{1,0:T(8,128)} %bitcast.11, f32[512,128]{1,0:T(8,128)} %bitcast.22, f32[640,512]{1,0:T(8,128)} %bitcast.20, f32[16,64]{1,0:T(8,128)S(1)} %bitcast.13, s32[1,512]{1,0:T(1,128)S(1)} %bitcast.14), custom_call_target="tpu_custom_call" | custom-call | flops 268435456 | bytes 4194304 | tf_op jit(solution)/shard_map/pallas_call | solution.py:386
  14.0 4.5 %collective-permute-start.2 = (f32[1,80,128]{2,1,0:T(8,128)S(1)}, f32[1,80,128]{2,1,0:T(8,128)S(1)}, u32[]{:S(2)}, u32[]{:S(2)}) collective-permute-start(f32[1,80,128]{2,1,0:T(8,128)S(1)} %shard_map.85), channel_id=1, source_target_pairs={{0,7},{1,2},{2,1},{3,4},{4,3},{5,6},{6,5},{7,0},{8,15},{9,10},{10,... | collective-permute-start | bytes 122888 | tf_op jit(solution)/shard_map/ppermute | solution.py:475
  18.8 1.6 %collective-permute-done.2.refs_2_ = f32[1,80,128]{2,1,0:T(8,128)S(1)} collective-permute-done((f32[1,80,128]{2,1,0:T(8,128)S(1)}, f32[1,80,128]{2,1,0:T(8,128)S(1)}, u32[]{:S(2)}, u32[]{:S(2)}) %collective-permute-start.2) | collective-permute-done | bytes 40992 | tf_op jit(solution)/shard_map/ppermute | solution.py:475
  20.3 1.2 %shard_map.86 = (f32[256,128]{1,0:T(8,128)S(1)}, f32[256,128]{1,0:T(8,128)S(1)}) custom-call(s32[1,8]{1,0:T(1,128)S(1)} %bitcast.15, s32[1,8]{1,0:T(1,128)S(1)} %bitcast.17, f32[2,80,128]{2,1,0:T(8,128)S(1)} %collective-permute-done.refs_0_, f32[1,80,128]{2,1,0:T(8,128)S(1)} %collective-permute-done.1.refs_1_, ...), custom_call_target="tpu_custom_call" | custom-call | flops 335544320 | bytes 1638400 | tf_op jit(solution)/shard_map/pallas_call | solution.py:463
  21.6 1.5 %collective-permute-start.7 = (f32[256,128]{1,0:T(8,128)S(1)}, f32[256,128]{1,0:T(8,128)S(1)}, u32[]{:S(2)}, u32[]{:S(2)}) collective-permute-start(f32[256,128]{1,0:T(8,128)S(1)} %get-tuple-element.45.own_ref), channel_id=1, source_target_pairs={{0,8},{1,17},{2,10},{3,19},{4,12},{5,21},{6,14},{7,23},{8,0},{9,25... | collective-permute-start | bytes 393224 | tf_op jit(solution)/shard_map/ppermute | solution.py:234
  23.1 1.5 %collective-permute-start.9 = (f32[256,128]{1,0:T(8,128)S(1)}, f32[256,128]{1,0:T(8,128)S(1)}, u32[]{:S(2)}, u32[]{:S(2)}) collective-permute-start(f32[256,128]{1,0:T(8,128)S(1)} %get-tuple-element.49.own_ref), channel_id=1, source_target_pairs={{0,16},{1,9},{2,18},{3,11},{4,20},{5,13},{6,22},{7,15},{8,24},{9,1... | collective-permute-start | bytes 393224 | tf_op jit(solution)/shard_map/ppermute | solution.py:234
  24.6 2.2 %collective-permute-done.7.got_ref = f32[256,128]{1,0:T(8,128)S(1)} collective-permute-done((f32[256,128]{1,0:T(8,128)S(1)}, f32[256,128]{1,0:T(8,128)S(1)}, u32[]{:S(2)}, u32[]{:S(2)}) %collective-permute-start.7) | collective-permute-done | bytes 131104 | tf_op jit(solution)/shard_map/ppermute | solution.py:234
  26.9 1.3 %collective-permute-start.8 = (f32[256,128]{1,0:T(8,128)S(1)}, f32[256,128]{1,0:T(8,128)S(1)}, u32[]{:S(2)}, u32[]{:S(2)}) collective-permute-start(f32[256,128]{1,0:T(8,128)S(1)} %get-tuple-element.48), channel_id=1, source_target_pairs={{0,16},{1,9},{2,18},{3,11},{4,20},{5,13},{6,22},{7,15},{8,24},{9,1... | collective-permute-start | bytes 393224 | tf_op jit(solution)/shard_map/ppermute | solution.py:240
  28.3 1.6 %collective-permute-start.10 = (f32[256,128]{1,0:T(8,128)S(1)}, f32[256,128]{1,0:T(8,128)S(1)}, u32[]{:S(2)}, u32[]{:S(2)}) collective-permute-start(f32[256,128]{1,0:T(8,128)S(1)} %get-tuple-element.51), channel_id=1, source_target_pairs={{0,8},{1,17},{2,10},{3,19},{4,12},{5,21},{6,14},{7,23},{8,0},{9,25... | collective-permute-start | bytes 393224 | tf_op jit(solution)/shard_map/ppermute | solution.py:240
  29.8 2.1 %collective-permute-done.8.refs_1_ = f32[256,128]{1,0:T(8,128)S(1)} collective-permute-done((f32[256,128]{1,0:T(8,128)S(1)}, f32[256,128]{1,0:T(8,128)S(1)}, u32[]{:S(2)}, u32[]{:S(2)}) %collective-permute-start.8) | collective-permute-done | bytes 131104 | tf_op jit(solution)/shard_map/ppermute | solution.py:240
  32.0 1.4 %collective-permute-done.10.refs_3_ = f32[256,128]{1,0:T(8,128)S(1)} collective-permute-done((f32[256,128]{1,0:T(8,128)S(1)}, f32[256,128]{1,0:T(8,128)S(1)}, u32[]{:S(2)}, u32[]{:S(2)}) %collective-permute-start.10) | collective-permute-done | bytes 131104 | tf_op jit(solution)/shard_map/ppermute | solution.py:240
  33.7 2.6 %collective-permute-start.11 = (f32[2,80,128]{2,1,0:T(8,128)S(1)}, f32[2,80,128]{2,1,0:T(8,128)S(1)}, u32[]{:S(2)}, u32[]{:S(2)}) collective-permute-start(f32[2,80,128]{2,1,0:T(8,128)S(1)} %get-tuple-element.53), channel_id=1, source_target_pairs={{0,4},{1,5},{2,6},{3,7},{4,0},{5,1},{6,2},{7,3},{8,12},{9,13},{10,... | collective-permute-start | bytes 245768 | tf_op jit(solution)/shard_map/ppermute | solution.py:475
  36.8 0.6 %collective-permute-start.15 = (f32[2,80,128]{2,1,0:T(8,128)S(1)}, f32[2,80,128]{2,1,0:T(8,128)S(1)}, u32[]{:S(2)}, u32[]{:S(2)}) collective-permute-start(f32[2,80,128]{2,1,0:T(8,128)S(1)} %get-tuple-element.60), channel_id=1, source_target_pairs={{0,5},{1,6},{2,7},{3,0},{4,1},{5,2},{6,3},{7,4},{8,13},{9,14},{10,... | collective-permute-start | bytes 245768 | tf_op jit(solution)/shard_map/ppermute | solution.py:475
  37.3 1.2 %collective-permute-start.16 = (f32[2,80,128]{2,1,0:T(8,128)S(1)}, f32[2,80,128]{2,1,0:T(8,128)S(1)}, u32[]{:S(2)}, u32[]{:S(2)}) collective-permute-start(f32[2,80,128]{2,1,0:T(8,128)S(1)} %get-tuple-element.61), channel_id=1, source_target_pairs={{0,3},{1,4},{2,5},{3,6},{4,7},{5,0},{6,1},{7,2},{8,11},{9,12},{10,... | collective-permute-start | bytes 245768 | tf_op jit(solution)/shard_map/ppermute | solution.py:475
  38.6 3.0 %collective-permute-start.17 = (f32[2,80,128]{2,1,0:T(8,128)S(1)}, f32[2,80,128]{2,1,0:T(8,128)S(1)}, u32[]{:S(2)}, u32[]{:S(2)}) collective-permute-start(f32[2,80,128]{2,1,0:T(8,128)S(1)} %get-tuple-element.62), channel_id=1, source_target_pairs={{0,6},{1,7},{2,0},{3,1},{4,2},{5,3},{6,4},{7,5},{8,14},{9,15},{10,... | collective-permute-start | bytes 245768 | tf_op jit(solution)/shard_map/ppermute | solution.py:475
  42.0 2.5 %collective-permute-start.13 = (f32[1,80,128]{2,1,0:T(8,128)S(1)}, f32[1,80,128]{2,1,0:T(8,128)S(1)}, u32[]{:S(2)}, u32[]{:S(2)}) collective-permute-start(f32[1,80,128]{2,1,0:T(8,128)S(1)} %shard_map.92), channel_id=1, source_target_pairs={{0,7},{1,2},{2,1},{3,4},{4,3},{5,6},{6,5},{7,0},{8,15},{9,10},{10,... | collective-permute-start | bytes 122888 | tf_op jit(solution)/shard_map/ppermute | solution.py:475
  44.6 1.1 %collective-permute-done.16.refs_5_ = f32[2,80,128]{2,1,0:T(8,128)S(1)} collective-permute-done((f32[2,80,128]{2,1,0:T(8,128)S(1)}, f32[2,80,128]{2,1,0:T(8,128)S(1)}, u32[]{:S(2)}, u32[]{:S(2)}) %collective-permute-start.16) | collective-permute-done | bytes 81952 | tf_op jit(solution)/shard_map/ppermute | solution.py:475
  46.1 2.2 %collective-permute-done.14.refs_3_ = f32[2,80,128]{2,1,0:T(8,128)S(1)} collective-permute-done((f32[2,80,128]{2,1,0:T(8,128)S(1)}, f32[2,80,128]{2,1,0:T(8,128)S(1)}, u32[]{:S(2)}, u32[]{:S(2)}) %collective-permute-start.14) | collective-permute-done | bytes 81952 | tf_op jit(solution)/shard_map/ppermute | solution.py:475
  48.3 1.9 %shard_map.93 = f32[512,128]{1,0:T(8,128)} custom-call(s32[1,8]{1,0:T(1,128)S(1)} %bitcast.16, s32[1,8]{1,0:T(1,128)S(1)} %bitcast.18, f32[2,80,128]{2,1,0:T(8,128)S(1)} %collective-permute-done.11.refs_1_.refs_0_, f32[1,80,128]{2,1,0:T(8,128)S(1)} %collective-permute-done.12.refs_1_, f32[1,80,128]{2,1,0:T(8,128)S(1)} %collective-permute-done.13.refs_2_, ...), custom_call_target="tpu_custom_call" | custom-call | flops 335544320 | bytes 1638400 | tf_op jit(solution)/shard_map/pallas_call | solution.py:463
  (34 shorter events, 2.7 us)
Async XLA Ops:
  2.0 9.8 %copy-start.1 = (f32[64,4,4]{0,2,1:T(4,128)S(1)}, f32[64,4,4]{0,2,1:T(4,128)}, u32[]{:S(2)}) copy-start(f32[64,4,4]{0,2,1:T(4,128)} %param.13) | copy-start | bytes 12292
  2.0 9.7 %copy-start.2 = (s32[512]{0:T(512)S(1)}, s32[512]{0:T(512)}, u32[]{:S(2)}) copy-start(s32[512]{0:T(512)} %param.14) | copy-start | bytes 6148
  2.0 9.7 %collective-permute-start.1 = (f32[1,80,128]{2,1,0:T(8,128)S(1)}, f32[1,80,128]{2,1,0:T(8,128)S(1)}, u32[]{:S(2)}, u32[]{:S(2)}) collective-permute-start(f32[1,80,128]{2,1,0:T(8,128)S(1)} %get-tuple-element.35), channel_id=1, source_target_pairs={{0,1},{1,0},{2,3},{3,2},{4,5},{5,4},{6,7},{7,6},{8,9},{9,8},{10,11... | collective-permute-start | bytes 122888 | tf_op jit(solution)/shard_map/ppermute | solution.py:475
  2.5 11.5 %collective-permute-start = (f32[2,80,128]{2,1,0:T(8,128)S(1)}, f32[2,80,128]{2,1,0:T(8,128)S(1)}, u32[]{:S(2)}, u32[]{:S(2)}) collective-permute-start(f32[2,80,128]{2,1,0:T(8,128)S(1)} %get-tuple-element.34), channel_id=1, source_target_pairs={{0,4},{1,5},{2,6},{3,7},{4,0},{5,1},{6,2},{7,3},{8,12},{9,13},{10,... | collective-permute-start | bytes 245768 | tf_op jit(solution)/shard_map/ppermute | solution.py:475
  6.8 11.8 %collective-permute-start.4 = (f32[2,80,128]{2,1,0:T(8,128)S(1)}, f32[2,80,128]{2,1,0:T(8,128)S(1)}, u32[]{:S(2)}, u32[]{:S(2)}) collective-permute-start(f32[2,80,128]{2,1,0:T(8,128)S(1)} %get-tuple-element.41), channel_id=1, source_target_pairs={{0,5},{1,6},{2,7},{3,0},{4,1},{5,2},{6,3},{7,4},{8,13},{9,14},{10,... | collective-permute-start | bytes 245768 | tf_op jit(solution)/shard_map/ppermute | solution.py:475
  6.8 11.9 %collective-permute-start.5 = (f32[2,80,128]{2,1,0:T(8,128)S(1)}, f32[2,80,128]{2,1,0:T(8,128)S(1)}, u32[]{:S(2)}, u32[]{:S(2)}) collective-permute-start(f32[2,80,128]{2,1,0:T(8,128)S(1)} %get-tuple-element.42), channel_id=1, source_target_pairs={{0,3},{1,4},{2,5},{3,6},{4,7},{5,0},{6,1},{7,2},{8,11},{9,12},{10,... | collective-permute-start | bytes 245768 | tf_op jit(solution)/shard_map/ppermute | solution.py:475
  8.6 10.2 %collective-permute-start.6 = (f32[2,80,128]{2,1,0:T(8,128)S(1)}, f32[2,80,128]{2,1,0:T(8,128)S(1)}, u32[]{:S(2)}, u32[]{:S(2)}) collective-permute-start(f32[2,80,128]{2,1,0:T(8,128)S(1)} %get-tuple-element.43), channel_id=1, source_target_pairs={{0,6},{1,7},{2,0},{3,1},{4,2},{5,3},{6,4},{7,5},{8,14},{9,15},{10,... | collective-permute-start | bytes 245768 | tf_op jit(solution)/shard_map/ppermute | solution.py:475
  11.7 7.1 %collective-permute-start.3 = (f32[2,80,128]{2,1,0:T(8,128)S(1)}, f32[2,80,128]{2,1,0:T(8,128)S(1)}, u32[]{:S(2)}, u32[]{:S(2)}) collective-permute-start(f32[2,80,128]{2,1,0:T(8,128)S(1)} %get-tuple-element.39.refs_2_), channel_id=1, source_target_pairs={{0,2},{1,3},{2,4},{3,5},{4,6},{5,7},{6,0},{7,1},{8,10},{9,11},{10,... | collective-permute-start | bytes 245768 | tf_op jit(solution)/shard_map/ppermute | solution.py:475
  11.7 8.6 %copy-start.3 = (s32[1,1,8]{2,1,0:T(1,128)S(1)}, s32[1,1,8]{2,1,0:T(1,128)}, u32[]{:S(2)}) copy-start(s32[1,1,8]{2,1,0:T(1,128)} %param.11) | copy-start | bytes 100
  11.7 8.6 %copy-start.4 = (s32[1,1,8]{2,1,0:T(1,128)S(1)}, s32[1,1,8]{2,1,0:T(1,128)}, u32[]{:S(2)}) copy-start(s32[1,1,8]{2,1,0:T(1,128)} %param.12) | copy-start | bytes 100
  14.0 6.3 %collective-permute-start.2 = (f32[1,80,128]{2,1,0:T(8,128)S(1)}, f32[1,80,128]{2,1,0:T(8,128)S(1)}, u32[]{:S(2)}, u32[]{:S(2)}) collective-permute-start(f32[1,80,128]{2,1,0:T(8,128)S(1)} %shard_map.85), channel_id=1, source_target_pairs={{0,7},{1,2},{2,1},{3,4},{4,3},{5,6},{6,5},{7,0},{8,15},{9,10},{10,... | collective-permute-start | bytes 122888 | tf_op jit(solution)/shard_map/ppermute | solution.py:475
  21.6 5.3 %collective-permute-start.7 = (f32[256,128]{1,0:T(8,128)S(1)}, f32[256,128]{1,0:T(8,128)S(1)}, u32[]{:S(2)}, u32[]{:S(2)}) collective-permute-start(f32[256,128]{1,0:T(8,128)S(1)} %get-tuple-element.45.own_ref), channel_id=1, source_target_pairs={{0,8},{1,17},{2,10},{3,19},{4,12},{5,21},{6,14},{7,23},{8,0},{9,25... | collective-permute-start | bytes 393224 | tf_op jit(solution)/shard_map/ppermute | solution.py:234
  23.1 5.1 %collective-permute-start.9 = (f32[256,128]{1,0:T(8,128)S(1)}, f32[256,128]{1,0:T(8,128)S(1)}, u32[]{:S(2)}, u32[]{:S(2)}) collective-permute-start(f32[256,128]{1,0:T(8,128)S(1)} %get-tuple-element.49.own_ref), channel_id=1, source_target_pairs={{0,16},{1,9},{2,18},{3,11},{4,20},{5,13},{6,22},{7,15},{8,24},{9,1... | collective-permute-start | bytes 393224 | tf_op jit(solution)/shard_map/ppermute | solution.py:234
  26.9 5.0 %collective-permute-start.8 = (f32[256,128]{1,0:T(8,128)S(1)}, f32[256,128]{1,0:T(8,128)S(1)}, u32[]{:S(2)}, u32[]{:S(2)}) collective-permute-start(f32[256,128]{1,0:T(8,128)S(1)} %get-tuple-element.48), channel_id=1, source_target_pairs={{0,16},{1,9},{2,18},{3,11},{4,20},{5,13},{6,22},{7,15},{8,24},{9,1... | collective-permute-start | bytes 393224 | tf_op jit(solution)/shard_map/ppermute | solution.py:240
  28.3 5.0 %collective-permute-start.10 = (f32[256,128]{1,0:T(8,128)S(1)}, f32[256,128]{1,0:T(8,128)S(1)}, u32[]{:S(2)}, u32[]{:S(2)}) collective-permute-start(f32[256,128]{1,0:T(8,128)S(1)} %get-tuple-element.51), channel_id=1, source_target_pairs={{0,8},{1,17},{2,10},{3,19},{4,12},{5,21},{6,14},{7,23},{8,0},{9,25... | collective-permute-start | bytes 393224 | tf_op jit(solution)/shard_map/ppermute | solution.py:240
  33.3 8.2 %copy-start = (f32[1,1,512,512]{3,2,1,0:T(8,128)S(1)}, f32[1,1,512,512]{3,2,1,0:T(8,128)}, u32[]{:S(2)}) copy-start(f32[1,1,512,512]{3,2,1,0:T(8,128)} %param.8) | copy-start | bytes 3145732
  33.7 7.9 %collective-permute-start.11 = (f32[2,80,128]{2,1,0:T(8,128)S(1)}, f32[2,80,128]{2,1,0:T(8,128)S(1)}, u32[]{:S(2)}, u32[]{:S(2)}) collective-permute-start(f32[2,80,128]{2,1,0:T(8,128)S(1)} %get-tuple-element.53), channel_id=1, source_target_pairs={{0,4},{1,5},{2,6},{3,7},{4,0},{5,1},{6,2},{7,3},{8,12},{9,13},{10,... | collective-permute-start | bytes 245768 | tf_op jit(solution)/shard_map/ppermute | solution.py:475
  36.3 5.8 %collective-permute-start.12 = (f32[1,80,128]{2,1,0:T(8,128)S(1)}, f32[1,80,128]{2,1,0:T(8,128)S(1)}, u32[]{:S(2)}, u32[]{:S(2)}) collective-permute-start(f32[1,80,128]{2,1,0:T(8,128)S(1)} %get-tuple-element.54), channel_id=1, source_target_pairs={{0,1},{1,0},{2,3},{3,2},{4,5},{5,4},{6,7},{7,6},{8,9},{9,8},{10,11... | collective-permute-start | bytes 122888 | tf_op jit(solution)/shard_map/ppermute | solution.py:475
  36.8 7.8 %collective-permute-start.15 = (f32[2,80,128]{2,1,0:T(8,128)S(1)}, f32[2,80,128]{2,1,0:T(8,128)S(1)}, u32[]{:S(2)}, u32[]{:S(2)}) collective-permute-start(f32[2,80,128]{2,1,0:T(8,128)S(1)} %get-tuple-element.60), channel_id=1, source_target_pairs={{0,5},{1,6},{2,7},{3,0},{4,1},{5,2},{6,3},{7,4},{8,13},{9,14},{10,... | collective-permute-start | bytes 245768 | tf_op jit(solution)/shard_map/ppermute | solution.py:475
  37.3 8.4 %collective-permute-start.16 = (f32[2,80,128]{2,1,0:T(8,128)S(1)}, f32[2,80,128]{2,1,0:T(8,128)S(1)}, u32[]{:S(2)}, u32[]{:S(2)}) collective-permute-start(f32[2,80,128]{2,1,0:T(8,128)S(1)} %get-tuple-element.61), channel_id=1, source_target_pairs={{0,3},{1,4},{2,5},{3,6},{4,7},{5,0},{6,1},{7,2},{8,11},{9,12},{10,... | collective-permute-start | bytes 245768 | tf_op jit(solution)/shard_map/ppermute | solution.py:475
  38.6 7.6 %collective-permute-start.17 = (f32[2,80,128]{2,1,0:T(8,128)S(1)}, f32[2,80,128]{2,1,0:T(8,128)S(1)}, u32[]{:S(2)}, u32[]{:S(2)}) collective-permute-start(f32[2,80,128]{2,1,0:T(8,128)S(1)} %get-tuple-element.62), channel_id=1, source_target_pairs={{0,6},{1,7},{2,0},{3,1},{4,2},{5,3},{6,4},{7,5},{8,14},{9,15},{10,... | collective-permute-start | bytes 245768 | tf_op jit(solution)/shard_map/ppermute | solution.py:475
  41.6 6.8 %collective-permute-start.14 = (f32[2,80,128]{2,1,0:T(8,128)S(1)}, f32[2,80,128]{2,1,0:T(8,128)S(1)}, u32[]{:S(2)}, u32[]{:S(2)}) collective-permute-start(f32[2,80,128]{2,1,0:T(8,128)S(1)} %get-tuple-element.58.refs_2_), channel_id=1, source_target_pairs={{0,2},{1,3},{2,4},{3,5},{4,6},{5,7},{6,0},{7,1},{8,10},{9,11},{10,... | collective-permute-start | bytes 245768 | tf_op jit(solution)/shard_map/ppermute | solution.py:475
  42.0 6.3 %collective-permute-start.13 = (f32[1,80,128]{2,1,0:T(8,128)S(1)}, f32[1,80,128]{2,1,0:T(8,128)S(1)}, u32[]{:S(2)}, u32[]{:S(2)}) collective-permute-start(f32[1,80,128]{2,1,0:T(8,128)S(1)} %shard_map.92), channel_id=1, source_target_pairs={{0,7},{1,2},{2,1},{3,4},{4,3},{5,6},{6,5},{7,0},{8,15},{9,10},{10,... | collective-permute-start | bytes 122888 | tf_op jit(solution)/shard_map/ppermute | solution.py:475

commit v9 on v8

--- a/solution.py
+++ b/solution.py
@@ -228,7 +228,7 @@
     for group in range(groups):
         for tile in range(count):
             for turn, pairs in enumerate(steps):
-                dest = group ^ (1 + (turn + tile) % 2)
+                dest = group ^ (2 - (turn + tile) % 2)
                 pairs.append((group * count + tile, dest * count + tile))
     axes = ("kern", "tile")
     came = [lax.ppermute(part, axes, pairs) for part, pairs in zip(first, steps)]
@@ -332,7 +332,7 @@
         return [(me * groups + b, slice(0, size)) for b in range(groups)]
     rows_of = []
     odd = lax.axis_index("tile") & 1
-    one, two = me ^ (1 + odd), me ^ (2 - odd)
+    one, two = me ^ (2 - odd), me ^ (1 + odd)
     for half, (first, second) in enumerate(((one, two), (two, one))):
         lanes = slice(half * (size // 2), (half + 1) * (size // 2))
         for a in (me, second):

time: 50.4 us -> 50.4 us (level)
  no operation moved by 1% of the time
where the time goes in v9:
time: 50.4 us; the launch traced here: 50.2 us
  starting transfers between devices  29.6 us (59%)
  waiting for transfers between devices  11.2 us (22%)
  Pallas kernels  9.26 us (18%)
    ppermute x14, starting transfers between devices, send(): return lax.ppermute(value, 'tile', message.pairs)  23.6 us
    ppermute x14, waiting for transfers between devices, send(): return lax.ppermute(value, 'tile', message.pairs)  5.53 us
    ppermute x2, waiting for transfers between devices, mix(): lax.ppermute(send, axes, pairs)  3.42 us
    pallas_call x2, Pallas kernels, rows(): call(functools.partial(row_kernel, messages, halves, final), pltpu.HBM((s...  3.1 us
    ppermute x2, starting transfers between devices, mix(): lax.ppermute(part, axes, pairs)  3.08 us
    ppermute x2, starting transfers between devices, mix(): lax.ppermute(send, axes, pairs)  2.9 us
    pallas_call x1, Pallas kernels, prepare(): call(functools.partial(prepare_kernel, halves), [struct(size, width), str...  2.21 us
    ppermute x2, waiting for transfers between devices, mix(): lax.ppermute(part, axes, pairs)  2.2 us
  transfers between devices with their start and end apart: 18, of which 8 were waited for; matrix products, arithmetic and copies ran while one was open for 0% of the time, Pallas kernels for 8%

profile of v9, /device:TPU:0, one launch (start us, length us, event | category | flops | bytes accessed | tf_op | source)
XLA Modules:
  0.0 50.2 jit_solution(7431907905900145341)
XLA Ops:
  0.0 2.0 %shard_map.82 = (f32[2,80,128]{2,1,0:T(8,128)S(1)}, f32[1,80,128]{2,1,0:T(8,128)S(1)}, f32[1,80,128]{2,1,0:T(8,128)S(1)}, bf16[640,512]{1,0:T(8,128)(2,1)S(1)}, ...) custom-call(f32[512,128]{1,0:T(8,128)} %bitcast.21, f32[12,80,512]{2,1,0:T(8,128)} %bitcast.19), custom_call_target="tpu_custom_call" | custom-call | flops 167772160 | bytes 1966080 | tf_op jit(solution)/shard_map/pallas_call | solution.py:162
  2.5 3.7 %collective-permute-start = (f32[2,80,128]{2,1,0:T(8,128)S(1)}, f32[2,80,128]{2,1,0:T(8,128)S(1)}, u32[]{:S(2)}, u32[]{:S(2)}) collective-permute-start(f32[2,80,128]{2,1,0:T(8,128)S(1)} %get-tuple-element.34), channel_id=1, source_target_pairs={{0,4},{1,5},{2,6},{3,7},{4,0},{5,1},{6,2},{7,3},{8,12},{9,13},{10,... | collective-permute-start | bytes 245768 | tf_op jit(solution)/shard_map/ppermute | solution.py:475
  6.2 0.6 %shard_map.83 = (f32[2,80,128]{2,1,0:T(8,128)S(1)}, f32[2,80,128]{2,1,0:T(8,128)S(1)}, f32[2,80,128]{2,1,0:T(8,128)S(1)}, f32[2,80,128]{2,1,0:T(8,128)S(1)}, bf16[1280,512]{1,0:T(8,128)(2,1)S(1)}) custom-call(bf16[512,256]{1,0:T(8,128)(2,1)S(1)} %get-tuple-element.37.both_ref, f32[8,80,512]{2,1,0:T(8,128)S(1)} %get-tuple-element.38.right_ref), custom_call_target="tpu_custom_call" | custom-call | flops 335544320 | bytes 2621440 | tf_op jit(solution)/shard_map/pallas_call | solution.py:191
  6.8 1.7 %collective-permute-start.5 = (f32[2,80,128]{2,1,0:T(8,128)S(1)}, f32[2,80,128]{2,1,0:T(8,128)S(1)}, u32[]{:S(2)}, u32[]{:S(2)}) collective-permute-start(f32[2,80,128]{2,1,0:T(8,128)S(1)} %get-tuple-element.42), channel_id=1, source_target_pairs={{0,3},{1,4},{2,5},{3,6},{4,7},{5,0},{6,1},{7,2},{8,11},{9,12},{10,... | collective-permute-start | bytes 245768 | tf_op jit(solution)/shard_map/ppermute | solution.py:475
  8.6 3.1 %collective-permute-start.6 = (f32[2,80,128]{2,1,0:T(8,128)S(1)}, f32[2,80,128]{2,1,0:T(8,128)S(1)}, u32[]{:S(2)}, u32[]{:S(2)}) collective-permute-start(f32[2,80,128]{2,1,0:T(8,128)S(1)} %get-tuple-element.43), channel_id=1, source_target_pairs={{0,6},{1,7},{2,0},{3,1},{4,2},{5,3},{6,4},{7,5},{8,14},{9,15},{10,... | collective-permute-start | bytes 245768 | tf_op jit(solution)/shard_map/ppermute | solution.py:475
  11.8 2.2 %shard_map.84 = (f32[512,128]{1,0:T(8,128)S(1)}, bf16[1024,640]{1,0:T(8,128)(2,1)S(1)}, f32[8,256,128]{2,1,0:T(8,128)S(1)}) custom-call(f32[512,512]{1,0:T(8,128)} %bitcast.11, f32[512,128]{1,0:T(8,128)} %bitcast.22, f32[640,512]{1,0:T(8,128)} %bitcast.20, f32[16,64]{1,0:T(8,128)S(1)} %bitcast.13, s32[1,512]{1,0:T(1,128)S(1)} %bitcast.14), custom_call_target="tpu_custom_call" | custom-call | flops 268435456 | bytes 4194304 | tf_op jit(solution)/shard_map/pallas_call | solution.py:386
  14.0 4.5 %collective-permute-start.2 = (f32[1,80,128]{2,1,0:T(8,128)S(1)}, f32[1,80,128]{2,1,0:T(8,128)S(1)}, u32[]{:S(2)}, u32[]{:S(2)}) collective-permute-start(f32[1,80,128]{2,1,0:T(8,128)S(1)} %shard_map.85), channel_id=1, source_target_pairs={{0,7},{1,2},{2,1},{3,4},{4,3},{5,6},{6,5},{7,0},{8,15},{9,10},{10,... | collective-permute-start | bytes 122888 | tf_op jit(solution)/shard_map/ppermute | solution.py:475
  18.8 1.6 %collective-permute-done.2.refs_2_ = f32[1,80,128]{2,1,0:T(8,128)S(1)} collective-permute-done((f32[1,80,128]{2,1,0:T(8,128)S(1)}, f32[1,80,128]{2,1,0:T(8,128)S(1)}, u32[]{:S(2)}, u32[]{:S(2)}) %collective-permute-start.2) | collective-permute-done | bytes 40992 | tf_op jit(solution)/shard_map/ppermute | solution.py:475
  20.3 1.2 %shard_map.86 = (f32[256,128]{1,0:T(8,128)S(1)}, f32[256,128]{1,0:T(8,128)S(1)}) custom-call(s32[1,8]{1,0:T(1,128)S(1)} %bitcast.15, s32[1,8]{1,0:T(1,128)S(1)} %bitcast.17, f32[2,80,128]{2,1,0:T(8,128)S(1)} %collective-permute-done.refs_0_, f32[1,80,128]{2,1,0:T(8,128)S(1)} %collective-permute-done.1.refs_1_, ...), custom_call_target="tpu_custom_call" | custom-call | flops 335544320 | bytes 1638400 | tf_op jit(solution)/shard_map/pallas_call | solution.py:463
  21.6 1.6 %collective-permute-start.7 = (f32[256,128]{1,0:T(8,128)S(1)}, f32[256,128]{1,0:T(8,128)S(1)}, u32[]{:S(2)}, u32[]{:S(2)}) collective-permute-start(f32[256,128]{1,0:T(8,128)S(1)} %get-tuple-element.45.own_ref), channel_id=1, source_target_pairs={{0,16},{1,9},{2,18},{3,11},{4,20},{5,13},{6,22},{7,15},{8,24},{9,1... | collective-permute-start | bytes 393224 | tf_op jit(solution)/shard_map/ppermute | solution.py:234
  23.1 1.5 %collective-permute-start.9 = (f32[256,128]{1,0:T(8,128)S(1)}, f32[256,128]{1,0:T(8,128)S(1)}, u32[]{:S(2)}, u32[]{:S(2)}) collective-permute-start(f32[256,128]{1,0:T(8,128)S(1)} %get-tuple-element.49.own_ref), channel_id=1, source_target_pairs={{0,8},{1,17},{2,10},{3,19},{4,12},{5,21},{6,14},{7,23},{8,0},{9,25... | collective-permute-start | bytes 393224 | tf_op jit(solution)/shard_map/ppermute | solution.py:234
  24.6 2.2 %collective-permute-done.7.got_ref = f32[256,128]{1,0:T(8,128)S(1)} collective-permute-done((f32[256,128]{1,0:T(8,128)S(1)}, f32[256,128]{1,0:T(8,128)S(1)}, u32[]{:S(2)}, u32[]{:S(2)}) %collective-permute-start.7) | collective-permute-done | bytes 131104 | tf_op jit(solution)/shard_map/ppermute | solution.py:234
  26.9 1.3 %collective-permute-start.8 = (f32[256,128]{1,0:T(8,128)S(1)}, f32[256,128]{1,0:T(8,128)S(1)}, u32[]{:S(2)}, u32[]{:S(2)}) collective-permute-start(f32[256,128]{1,0:T(8,128)S(1)} %get-tuple-element.48), channel_id=1, source_target_pairs={{0,8},{1,17},{2,10},{3,19},{4,12},{5,21},{6,14},{7,23},{8,0},{9,25... | collective-permute-start | bytes 393224 | tf_op jit(solution)/shard_map/ppermute | solution.py:240
  28.2 1.6 %collective-permute-start.10 = (f32[256,128]{1,0:T(8,128)S(1)}, f32[256,128]{1,0:T(8,128)S(1)}, u32[]{:S(2)}, u32[]{:S(2)}) collective-permute-start(f32[256,128]{1,0:T(8,128)S(1)} %get-tuple-element.51), channel_id=1, source_target_pairs={{0,16},{1,9},{2,18},{3,11},{4,20},{5,13},{6,22},{7,15},{8,24},{9,1... | collective-permute-start | bytes 393224 | tf_op jit(solution)/shard_map/ppermute | solution.py:240
  29.8 2.1 %collective-permute-done.8.refs_1_ = f32[256,128]{1,0:T(8,128)S(1)} collective-permute-done((f32[256,128]{1,0:T(8,128)S(1)}, f32[256,128]{1,0:T(8,128)S(1)}, u32[]{:S(2)}, u32[]{:S(2)}) %collective-permute-start.8) | collective-permute-done | bytes 131104 | tf_op jit(solution)/shard_map/ppermute | solution.py:240
  31.9 1.4 %collective-permute-done.10.refs_3_ = f32[256,128]{1,0:T(8,128)S(1)} collective-permute-done((f32[256,128]{1,0:T(8,128)S(1)}, f32[256,128]{1,0:T(8,128)S(1)}, u32[]{:S(2)}, u32[]{:S(2)}) %collective-permute-start.10) | collective-permute-done | bytes 131104 | tf_op jit(solution)/shard_map/ppermute | solution.py:240
  33.6 2.6 %collective-permute-start.11 = (f32[2,80,128]{2,1,0:T(8,128)S(1)}, f32[2,80,128]{2,1,0:T(8,128)S(1)}, u32[]{:S(2)}, u32[]{:S(2)}) collective-permute-start(f32[2,80,128]{2,1,0:T(8,128)S(1)} %get-tuple-element.53), channel_id=1, source_target_pairs={{0,4},{1,5},{2,6},{3,7},{4,0},{5,1},{6,2},{7,3},{8,12},{9,13},{10,... | collective-permute-start | bytes 245768 | tf_op jit(solution)/shard_map/ppermute | solution.py:475
  36.7 0.6 %collective-permute-start.15 = (f32[2,80,128]{2,1,0:T(8,128)S(1)}, f32[2,80,128]{2,1,0:T(8,128)S(1)}, u32[]{:S(2)}, u32[]{:S(2)}) collective-permute-start(f32[2,80,128]{2,1,0:T(8,128)S(1)} %get-tuple-element.60), channel_id=1, source_target_pairs={{0,5},{1,6},{2,7},{3,0},{4,1},{5,2},{6,3},{7,4},{8,13},{9,14},{10,... | collective-permute-start | bytes 245768 | tf_op jit(solution)/shard_map/ppermute | solution.py:475
  37.3 1.2 %collective-permute-start.16 = (f32[2,80,128]{2,1,0:T(8,128)S(1)}, f32[2,80,128]{2,1,0:T(8,128)S(1)}, u32[]{:S(2)}, u32[]{:S(2)}) collective-permute-start(f32[2,80,128]{2,1,0:T(8,128)S(1)} %get-tuple-element.61), channel_id=1, source_target_pairs={{0,3},{1,4},{2,5},{3,6},{4,7},{5,0},{6,1},{7,2},{8,11},{9,12},{10,... | collective-permute-start | bytes 245768 | tf_op jit(solution)/shard_map/ppermute | solution.py:475
  38.5 3.0 %collective-permute-start.17 = (f32[2,80,128]{2,1,0:T(8,128)S(1)}, f32[2,80,128]{2,1,0:T(8,128)S(1)}, u32[]{:S(2)}, u32[]{:S(2)}) collective-permute-start(f32[2,80,128]{2,1,0:T(8,128)S(1)} %get-tuple-element.62), channel_id=1, source_target_pairs={{0,6},{1,7},{2,0},{3,1},{4,2},{5,3},{6,4},{7,5},{8,14},{9,15},{10,... | collective-permute-start | bytes 245768 | tf_op jit(solution)/shard_map/ppermute | solution.py:475
  42.0 2.5 %collective-permute-start.13 = (f32[1,80,128]{2,1,0:T(8,128)S(1)}, f32[1,80,128]{2,1,0:T(8,128)S(1)}, u32[]{:S(2)}, u32[]{:S(2)}) collective-permute-start(f32[1,80,128]{2,1,0:T(8,128)S(1)} %shard_map.92), channel_id=1, source_target_pairs={{0,7},{1,2},{2,1},{3,4},{4,3},{5,6},{6,5},{7,0},{8,15},{9,10},{10,... | collective-permute-start | bytes 122888 | tf_op jit(solution)/shard_map/ppermute | solution.py:475
  44.6 1.0 %collective-permute-done.16.refs_5_ = f32[2,80,128]{2,1,0:T(8,128)S(1)} collective-permute-done((f32[2,80,128]{2,1,0:T(8,128)S(1)}, f32[2,80,128]{2,1,0:T(8,128)S(1)}, u32[]{:S(2)}, u32[]{:S(2)}) %collective-permute-start.16) | collective-permute-done | bytes 81952 | tf_op jit(solution)/shard_map/ppermute | solution.py:475
  45.8 2.5 %collective-permute-done.14.refs_3_ = f32[2,80,128]{2,1,0:T(8,128)S(1)} collective-permute-done((f32[2,80,128]{2,1,0:T(8,128)S(1)}, f32[2,80,128]{2,1,0:T(8,128)S(1)}, u32[]{:S(2)}, u32[]{:S(2)}) %collective-permute-start.14) | collective-permute-done | bytes 81952 | tf_op jit(solution)/shard_map/ppermute | solution.py:475
  48.3 1.9 %shard_map.93 = f32[512,128]{1,0:T(8,128)} custom-call(s32[1,8]{1,0:T(1,128)S(1)} %bitcast.16, s32[1,8]{1,0:T(1,128)S(1)} %bitcast.18, f32[2,80,128]{2,1,0:T(8,128)S(1)} %collective-permute-done.11.refs_1_.refs_0_, f32[1,80,128]{2,1,0:T(8,128)S(1)} %collective-permute-done.12.refs_1_, f32[1,80,128]{2,1,0:T(8,128)S(1)} %collective-permute-done.13.refs_2_, ...), custom_call_target="tpu_custom_call" | custom-call | flops 335544320 | bytes 1638400 | tf_op jit(solution)/shard_map/pallas_call | solution.py:463
  (34 shorter events, 2.6 us)
Async XLA Ops:
  2.0 9.8 %copy-start.1 = (f32[64,4,4]{0,2,1:T(4,128)S(1)}, f32[64,4,4]{0,2,1:T(4,128)}, u32[]{:S(2)}) copy-start(f32[64,4,4]{0,2,1:T(4,128)} %param.13) | copy-start | bytes 12292
  2.0 9.7 %copy-start.2 = (s32[512]{0:T(512)S(1)}, s32[512]{0:T(512)}, u32[]{:S(2)}) copy-start(s32[512]{0:T(512)} %param.14) | copy-start | bytes 6148
  2.0 9.7 %collective-permute-start.1 = (f32[1,80,128]{2,1,0:T(8,128)S(1)}, f32[1,80,128]{2,1,0:T(8,128)S(1)}, u32[]{:S(2)}, u32[]{:S(2)}) collective-permute-start(f32[1,80,128]{2,1,0:T(8,128)S(1)} %get-tuple-element.35), channel_id=1, source_target_pairs={{0,1},{1,0},{2,3},{3,2},{4,5},{5,4},{6,7},{7,6},{8,9},{9,8},{10,11... | collective-permute-start | bytes 122888 | tf_op jit(solution)/shard_map/ppermute | solution.py:475
  2.5 11.5 %collective-permute-start = (f32[2,80,128]{2,1,0:T(8,128)S(1)}, f32[2,80,128]{2,1,0:T(8,128)S(1)}, u32[]{:S(2)}, u32[]{:S(2)}) collective-permute-start(f32[2,80,128]{2,1,0:T(8,128)S(1)} %get-tuple-element.34), channel_id=1, source_target_pairs={{0,4},{1,5},{2,6},{3,7},{4,0},{5,1},{6,2},{7,3},{8,12},{9,13},{10,... | collective-permute-start | bytes 245768 | tf_op jit(solution)/shard_map/ppermute | solution.py:475
  6.8 11.8 %collective-permute-start.4 = (f32[2,80,128]{2,1,0:T(8,128)S(1)}, f32[2,80,128]{2,1,0:T(8,128)S(1)}, u32[]{:S(2)}, u32[]{:S(2)}) collective-permute-start(f32[2,80,128]{2,1,0:T(8,128)S(1)} %get-tuple-element.41), channel_id=1, source_target_pairs={{0,5},{1,6},{2,7},{3,0},{4,1},{5,2},{6,3},{7,4},{8,13},{9,14},{10,... | collective-permute-start | bytes 245768 | tf_op jit(solution)/shard_map/ppermute | solution.py:475
  6.8 11.9 %collective-permute-start.5 = (f32[2,80,128]{2,1,0:T(8,128)S(1)}, f32[2,80,128]{2,1,0:T(8,128)S(1)}, u32[]{:S(2)}, u32[]{:S(2)}) collective-permute-start(f32[2,80,128]{2,1,0:T(8,128)S(1)} %get-tuple-element.42), channel_id=1, source_target_pairs={{0,3},{1,4},{2,5},{3,6},{4,7},{5,0},{6,1},{7,2},{8,11},{9,12},{10,... | collective-permute-start | bytes 245768 | tf_op jit(solution)/shard_map/ppermute | solution.py:475
  8.6 10.2 %collective-permute-start.6 = (f32[2,80,128]{2,1,0:T(8,128)S(1)}, f32[2,80,128]{2,1,0:T(8,128)S(1)}, u32[]{:S(2)}, u32[]{:S(2)}) collective-permute-start(f32[2,80,128]{2,1,0:T(8,128)S(1)} %get-tuple-element.43), channel_id=1, source_target_pairs={{0,6},{1,7},{2,0},{3,1},{4,2},{5,3},{6,4},{7,5},{8,14},{9,15},{10,... | collective-permute-start | bytes 245768 | tf_op jit(solution)/shard_map/ppermute | solution.py:475
  11.7 7.1 %collective-permute-start.3 = (f32[2,80,128]{2,1,0:T(8,128)S(1)}, f32[2,80,128]{2,1,0:T(8,128)S(1)}, u32[]{:S(2)}, u32[]{:S(2)}) collective-permute-start(f32[2,80,128]{2,1,0:T(8,128)S(1)} %get-tuple-element.39.refs_2_), channel_id=1, source_target_pairs={{0,2},{1,3},{2,4},{3,5},{4,6},{5,7},{6,0},{7,1},{8,10},{9,11},{10,... | collective-permute-start | bytes 245768 | tf_op jit(solution)/shard_map/ppermute | solution.py:475
  11.7 8.6 %copy-start.3 = (s32[1,1,8]{2,1,0:T(1,128)S(1)}, s32[1,1,8]{2,1,0:T(1,128)}, u32[]{:S(2)}) copy-start(s32[1,1,8]{2,1,0:T(1,128)} %param.11) | copy-start | bytes 100
  11.7 8.6 %copy-start.4 = (s32[1,1,8]{2,1,0:T(1,128)S(1)}, s32[1,1,8]{2,1,0:T(1,128)}, u32[]{:S(2)}) copy-start(s32[1,1,8]{2,1,0:T(1,128)} %param.12) | copy-start | bytes 100
  14.0 6.3 %collective-permute-start.2 = (f32[1,80,128]{2,1,0:T(8,128)S(1)}, f32[1,80,128]{2,1,0:T(8,128)S(1)}, u32[]{:S(2)}, u32[]{:S(2)}) collective-permute-start(f32[1,80,128]{2,1,0:T(8,128)S(1)} %shard_map.85), channel_id=1, source_target_pairs={{0,7},{1,2},{2,1},{3,4},{4,3},{5,6},{6,5},{7,0},{8,15},{9,10},{10,... | collective-permute-start | bytes 122888 | tf_op jit(solution)/shard_map/ppermute | solution.py:475
  21.6 5.3 %collective-permute-start.7 = (f32[256,128]{1,0:T(8,128)S(1)}, f32[256,128]{1,0:T(8,128)S(1)}, u32[]{:S(2)}, u32[]{:S(2)}) collective-permute-start(f32[256,128]{1,0:T(8,128)S(1)} %get-tuple-element.45.own_ref), channel_id=1, source_target_pairs={{0,16},{1,9},{2,18},{3,11},{4,20},{5,13},{6,22},{7,15},{8,24},{9,1... | collective-permute-start | bytes 393224 | tf_op jit(solution)/shard_map/ppermute | solution.py:234
  23.1 5.0 %collective-permute-start.9 = (f32[256,128]{1,0:T(8,128)S(1)}, f32[256,128]{1,0:T(8,128)S(1)}, u32[]{:S(2)}, u32[]{:S(2)}) collective-permute-start(f32[256,128]{1,0:T(8,128)S(1)} %get-tuple-element.49.own_ref), channel_id=1, source_target_pairs={{0,8},{1,17},{2,10},{3,19},{4,12},{5,21},{6,14},{7,23},{8,0},{9,25... | collective-permute-start | bytes 393224 | tf_op jit(solution)/shard_map/ppermute | solution.py:234
  26.9 5.0 %collective-permute-start.8 = (f32[256,128]{1,0:T(8,128)S(1)}, f32[256,128]{1,0:T(8,128)S(1)}, u32[]{:S(2)}, u32[]{:S(2)}) collective-permute-start(f32[256,128]{1,0:T(8,128)S(1)} %get-tuple-element.48), channel_id=1, source_target_pairs={{0,8},{1,17},{2,10},{3,19},{4,12},{5,21},{6,14},{7,23},{8,0},{9,25... | collective-permute-start | bytes 393224 | tf_op jit(solution)/shard_map/ppermute | solution.py:240
  28.2 5.0 %collective-permute-start.10 = (f32[256,128]{1,0:T(8,128)S(1)}, f32[256,128]{1,0:T(8,128)S(1)}, u32[]{:S(2)}, u32[]{:S(2)}) collective-permute-start(f32[256,128]{1,0:T(8,128)S(1)} %get-tuple-element.51), channel_id=1, source_target_pairs={{0,16},{1,9},{2,18},{3,11},{4,20},{5,13},{6,22},{7,15},{8,24},{9,1... | collective-permute-start | bytes 393224 | tf_op jit(solution)/shard_map/ppermute | solution.py:240
  33.3 8.3 %copy-start = (f32[1,1,512,512]{3,2,1,0:T(8,128)S(1)}, f32[1,1,512,512]{3,2,1,0:T(8,128)}, u32[]{:S(2)}) copy-start(f32[1,1,512,512]{3,2,1,0:T(8,128)} %param.8) | copy-start | bytes 3145732
  33.6 7.9 %collective-permute-start.11 = (f32[2,80,128]{2,1,0:T(8,128)S(1)}, f32[2,80,128]{2,1,0:T(8,128)S(1)}, u32[]{:S(2)}, u32[]{:S(2)}) collective-permute-start(f32[2,80,128]{2,1,0:T(8,128)S(1)} %get-tuple-element.53), channel_id=1, source_target_pairs={{0,4},{1,5},{2,6},{3,7},{4,0},{5,1},{6,2},{7,3},{8,12},{9,13},{10,... | collective-permute-start | bytes 245768 | tf_op jit(solution)/shard_map/ppermute | solution.py:475
  36.2 5.8 %collective-permute-start.12 = (f32[1,80,128]{2,1,0:T(8,128)S(1)}, f32[1,80,128]{2,1,0:T(8,128)S(1)}, u32[]{:S(2)}, u32[]{:S(2)}) collective-permute-start(f32[1,80,128]{2,1,0:T(8,128)S(1)} %get-tuple-element.54), channel_id=1, source_target_pairs={{0,1},{1,0},{2,3},{3,2},{4,5},{5,4},{6,7},{7,6},{8,9},{9,8},{10,11... | collective-permute-start | bytes 122888 | tf_op jit(solution)/shard_map/ppermute | solution.py:475
  36.7 7.9 %collective-permute-start.15 = (f32[2,80,128]{2,1,0:T(8,128)S(1)}, f32[2,80,128]{2,1,0:T(8,128)S(1)}, u32[]{:S(2)}, u32[]{:S(2)}) collective-permute-start(f32[2,80,128]{2,1,0:T(8,128)S(1)} %get-tuple-element.60), channel_id=1, source_target_pairs={{0,5},{1,6},{2,7},{3,0},{4,1},{5,2},{6,3},{7,4},{8,13},{9,14},{10,... | collective-permute-start | bytes 245768 | tf_op jit(solution)/shard_map/ppermute | solution.py:475
  37.3 8.3 %collective-permute-start.16 = (f32[2,80,128]{2,1,0:T(8,128)S(1)}, f32[2,80,128]{2,1,0:T(8,128)S(1)}, u32[]{:S(2)}, u32[]{:S(2)}) collective-permute-start(f32[2,80,128]{2,1,0:T(8,128)S(1)} %get-tuple-element.61), channel_id=1, source_target_pairs={{0,3},{1,4},{2,5},{3,6},{4,7},{5,0},{6,1},{7,2},{8,11},{9,12},{10,... | collective-permute-start | bytes 245768 | tf_op jit(solution)/shard_map/ppermute | solution.py:475
  38.5 7.3 %collective-permute-start.17 = (f32[2,80,128]{2,1,0:T(8,128)S(1)}, f32[2,80,128]{2,1,0:T(8,128)S(1)}, u32[]{:S(2)}, u32[]{:S(2)}) collective-permute-start(f32[2,80,128]{2,1,0:T(8,128)S(1)} %get-tuple-element.62), channel_id=1, source_target_pairs={{0,6},{1,7},{2,0},{3,1},{4,2},{5,3},{6,4},{7,5},{8,14},{9,15},{10,... | collective-permute-start | bytes 245768 | tf_op jit(solution)/shard_map/ppermute | solution.py:475
  41.6 6.8 %collective-permute-start.14 = (f32[2,80,128]{2,1,0:T(8,128)S(1)}, f32[2,80,128]{2,1,0:T(8,128)S(1)}, u32[]{:S(2)}, u32[]{:S(2)}) collective-permute-start(f32[2,80,128]{2,1,0:T(8,128)S(1)} %get-tuple-element.58.refs_2_), channel_id=1, source_target_pairs={{0,2},{1,3},{2,4},{3,5},{4,6},{5,7},{6,0},{7,1},{8,10},{9,11},{10,... | collective-permute-start | bytes 245768 | tf_op jit(solution)/shard_map/ppermute | solution.py:475
  42.0 6.3 %collective-permute-start.13 = (f32[1,80,128]{2,1,0:T(8,128)S(1)}, f32[1,80,128]{2,1,0:T(8,128)S(1)}, u32[]{:S(2)}, u32[]{:S(2)}) collective-permute-start(f32[1,80,128]{2,1,0:T(8,128)S(1)} %shard_map.92), channel_id=1, source_target_pairs={{0,7},{1,2},{2,1},{3,4},{4,3},{5,6},{6,5},{7,0},{8,15},{9,10},{10,... | collective-permute-start | bytes 122888 | tf_op jit(solution)/shard_map/ppermute | solution.py:475

commit v10 on v6

--- a/solution.py
+++ b/solution.py
@@ -80,8 +80,9 @@
     for ahead, group in groups.items():
         messages.append(Message([(at, (at - ahead) % count) for at in range(count)], group))
     messages.sort(key=lambda message: -message.across)
-    first = messages[:1] + [m for m in messages[:0:-1] if m.odd_slots is not None]
-    return [first, [message for message in messages if message not in first]]
+    short = [message for message in messages[::-1] if message.odd_slots is not None]
+    long = [message for message in messages if message.odd_slots is None]
+    return [long[-1:] + short, long[-2:-1] + long[:-2]]
 
 
 def slots_of(messages):

time: 50.3 us -> 52.3 us (1.040); the launches traced: 49.6 us -> 52.2 us
  waiting for transfers between devices: 11.9 us -> 20.4 us
  starting transfers between devices: 28.3 us -> 22.5 us
    ppermute x14, waiting for transfers between devices: 6.31 us -> 14.1 us  [send(): return lax.ppermute(value, 'tile', message.pairs)]
    ppermute x14, starting transfers between devices: 21 us -> 16.3 us  [send(): return lax.ppermute(value, 'tile', message.pairs)]
    ppermute x2, starting transfers between devices: 4.21 us -> 3.13 us  [mix(): lax.ppermute(send, axes, pairs)]
    ppermute x2, waiting for transfers between devices: 2.05 us -> 2.79 us  [mix(): lax.ppermute(part, axes, pairs)]
  transfers between devices with their start and end apart: 18 -> 18, of which waited for: 7 -> 9; matrix products, arithmetic and copies ran while one was open for 0% -> 0% of each run, Pallas kernels for 8% -> 7%
where the time goes in v10:
time: 52.3 us; the launch traced here: 52.2 us
  starting transfers between devices  22.5 us (43%)
  waiting for transfers between devices  20.4 us (39%)
  Pallas kernels  9.13 us (17%)
    ppermute x14, starting transfers between devices, send(): return lax.ppermute(value, 'tile', message.pairs)  16.3 us
    ppermute x14, waiting for transfers between devices, send(): return lax.ppermute(value, 'tile', message.pairs)  14.1 us
    ppermute x2, waiting for transfers between devices, mix(): lax.ppermute(send, axes, pairs)  3.51 us
    ppermute x2, starting transfers between devices, mix(): lax.ppermute(send, axes, pairs)  3.13 us
    pallas_call x2, Pallas kernels, rows(): call(functools.partial(row_kernel, messages, halves, final), pltpu.HBM((s...  3.1 us
    ppermute x2, starting transfers between devices, mix(): lax.ppermute(part, axes, pairs)  3.08 us
    ppermute x2, waiting for transfers between devices, mix(): lax.ppermute(part, axes, pairs)  2.79 us
    pallas_call x1, Pallas kernels, prepare(): call(functools.partial(prepare_kernel, halves), [struct(size, width), str...  2.21 us
  transfers between devices with their start and end apart: 18, of which 9 were waited for; matrix products, arithmetic and copies ran while one was open for 0% of the time, Pallas kernels for 7%

profile of v10, /device:TPU:0, one launch (start us, length us, event | category | flops | bytes accessed | tf_op | source)
XLA Modules:
  0.0 52.2 jit_solution(5248748455505036870)
XLA Ops:
  0.0 1.8 %shard_map.82 = (f32[2,80,128]{2,1,0:T(8,128)S(1)}, f32[1,80,128]{2,1,0:T(8,128)S(1)}, f32[1,80,128]{2,1,0:T(8,128)S(1)}, bf16[640,512]{1,0:T(8,128)(2,1)S(1)}, ...) custom-call(f32[512,128]{1,0:T(8,128)} %bitcast.21, f32[12,80,512]{2,1,0:T(8,128)} %bitcast.19), custom_call_target="tpu_custom_call" | custom-call | flops 167772160 | bytes 1966080 | tf_op jit(solution)/shard_map/pallas_call | solution.py:162
  2.4 2.6 %collective-permute-start = (f32[2,80,128]{2,1,0:T(8,128)S(1)}, f32[2,80,128]{2,1,0:T(8,128)S(1)}, u32[]{:S(2)}, u32[]{:S(2)}) collective-permute-start(f32[2,80,128]{2,1,0:T(8,128)S(1)} %get-tuple-element.34), channel_id=1, source_target_pairs={{0,2},{1,3},{2,4},{3,5},{4,6},{5,7},{6,0},{7,1},{8,10},{9,11},{10,... | collective-permute-start | bytes 245768 | tf_op jit(solution)/shard_map/ppermute | solution.py:475
  5.6 2.7 %collective-permute-start.4 = (f32[2,80,128]{2,1,0:T(8,128)S(1)}, f32[2,80,128]{2,1,0:T(8,128)S(1)}, u32[]{:S(2)}, u32[]{:S(2)}) collective-permute-start(f32[2,80,128]{2,1,0:T(8,128)S(1)} %get-tuple-element.41), channel_id=1, source_target_pairs={{0,4},{1,5},{2,6},{3,7},{4,0},{5,1},{6,2},{7,3},{8,12},{9,13},{10,... | collective-permute-start | bytes 245768 | tf_op jit(solution)/shard_map/ppermute | solution.py:475
  8.3 1.7 %collective-permute-start.6 = (f32[2,80,128]{2,1,0:T(8,128)S(1)}, f32[2,80,128]{2,1,0:T(8,128)S(1)}, u32[]{:S(2)}, u32[]{:S(2)}) collective-permute-start(f32[2,80,128]{2,1,0:T(8,128)S(1)} %get-tuple-element.43), channel_id=1, source_target_pairs={{0,3},{1,4},{2,5},{3,6},{4,7},{5,0},{6,1},{7,2},{8,11},{9,12},{10,... | collective-permute-start | bytes 245768 | tf_op jit(solution)/shard_map/ppermute | solution.py:475
  10.0 3.1 %collective-permute-start.3 = (f32[2,80,128]{2,1,0:T(8,128)S(1)}, f32[2,80,128]{2,1,0:T(8,128)S(1)}, u32[]{:S(2)}, u32[]{:S(2)}) collective-permute-start(f32[2,80,128]{2,1,0:T(8,128)S(1)} %get-tuple-element.39.refs_2_), channel_id=1, source_target_pairs={{0,6},{1,7},{2,0},{3,1},{4,2},{5,3},{6,4},{7,5},{8,14},{9,15},{10,... | collective-permute-start | bytes 245768 | tf_op jit(solution)/shard_map/ppermute | solution.py:475
  13.2 2.2 %shard_map.84 = (f32[512,128]{1,0:T(8,128)S(1)}, bf16[1024,640]{1,0:T(8,128)(2,1)S(1)}, f32[8,256,128]{2,1,0:T(8,128)S(1)}) custom-call(f32[512,512]{1,0:T(8,128)} %bitcast.11, f32[512,128]{1,0:T(8,128)} %bitcast.22, f32[640,512]{1,0:T(8,128)} %bitcast.20, f32[16,64]{1,0:T(8,128)S(1)} %bitcast.13, s32[1,512]{1,0:T(1,128)S(1)} %bitcast.14), custom_call_target="tpu_custom_call" | custom-call | flops 268435456 | bytes 4194304 | tf_op jit(solution)/shard_map/pallas_call | solution.py:386
  16.2 3.5 %collective-permute-done.6.refs_6_ = f32[2,80,128]{2,1,0:T(8,128)S(1)} collective-permute-done((f32[2,80,128]{2,1,0:T(8,128)S(1)}, f32[2,80,128]{2,1,0:T(8,128)S(1)}, u32[]{:S(2)}, u32[]{:S(2)}) %collective-permute-start.6) | collective-permute-done | bytes 81952 | tf_op jit(solution)/shard_map/ppermute | solution.py:475
  19.7 1.1 %collective-permute-done.2.refs_2_ = f32[1,80,128]{2,1,0:T(8,128)S(1)} collective-permute-done((f32[1,80,128]{2,1,0:T(8,128)S(1)}, f32[1,80,128]{2,1,0:T(8,128)S(1)}, u32[]{:S(2)}, u32[]{:S(2)}) %collective-permute-start.2) | collective-permute-done | bytes 40992 | tf_op jit(solution)/shard_map/ppermute | solution.py:475
  20.8 1.2 %shard_map.86 = (f32[256,128]{1,0:T(8,128)S(1)}, f32[256,128]{1,0:T(8,128)S(1)}) custom-call(s32[1,8]{1,0:T(1,128)S(1)} %bitcast.15, s32[1,8]{1,0:T(1,128)S(1)} %bitcast.17, f32[2,80,128]{2,1,0:T(8,128)S(1)} %collective-permute-done.refs_0_, f32[1,80,128]{2,1,0:T(8,128)S(1)} %collective-permute-done.1.refs_1_, ...), custom_call_target="tpu_custom_call" | custom-call | flops 335544320 | bytes 1638400 | tf_op jit(solution)/shard_map/pallas_call | solution.py:463
  22.0 1.6 %collective-permute-start.7 = (f32[256,128]{1,0:T(8,128)S(1)}, f32[256,128]{1,0:T(8,128)S(1)}, u32[]{:S(2)}, u32[]{:S(2)}) collective-permute-start(f32[256,128]{1,0:T(8,128)S(1)} %get-tuple-element.45.own_ref), channel_id=1, source_target_pairs={{0,8},{1,17},{2,10},{3,19},{4,12},{5,21},{6,14},{7,23},{8,0},{9,25... | collective-permute-start | bytes 393224 | tf_op jit(solution)/shard_map/ppermute | solution.py:234
  23.6 1.5 %collective-permute-start.9 = (f32[256,128]{1,0:T(8,128)S(1)}, f32[256,128]{1,0:T(8,128)S(1)}, u32[]{:S(2)}, u32[]{:S(2)}) collective-permute-start(f32[256,128]{1,0:T(8,128)S(1)} %get-tuple-element.49.own_ref), channel_id=1, source_target_pairs={{0,16},{1,9},{2,18},{3,11},{4,20},{5,13},{6,22},{7,15},{8,24},{9,1... | collective-permute-start | bytes 393224 | tf_op jit(solution)/shard_map/ppermute | solution.py:234
  25.1 2.8 %collective-permute-done.7.got_ref = f32[256,128]{1,0:T(8,128)S(1)} collective-permute-done((f32[256,128]{1,0:T(8,128)S(1)}, f32[256,128]{1,0:T(8,128)S(1)}, u32[]{:S(2)}, u32[]{:S(2)}) %collective-permute-start.7) | collective-permute-done | bytes 131104 | tf_op jit(solution)/shard_map/ppermute | solution.py:234
  27.9 1.6 %collective-permute-start.8 = (f32[256,128]{1,0:T(8,128)S(1)}, f32[256,128]{1,0:T(8,128)S(1)}, u32[]{:S(2)}, u32[]{:S(2)}) collective-permute-start(f32[256,128]{1,0:T(8,128)S(1)} %get-tuple-element.48), channel_id=1, source_target_pairs={{0,16},{1,9},{2,18},{3,11},{4,20},{5,13},{6,22},{7,15},{8,24},{9,1... | collective-permute-start | bytes 393224 | tf_op jit(solution)/shard_map/ppermute | solution.py:240
  29.6 1.5 %collective-permute-start.10 = (f32[256,128]{1,0:T(8,128)S(1)}, f32[256,128]{1,0:T(8,128)S(1)}, u32[]{:S(2)}, u32[]{:S(2)}) collective-permute-start(f32[256,128]{1,0:T(8,128)S(1)} %get-tuple-element.51), channel_id=1, source_target_pairs={{0,8},{1,17},{2,10},{3,19},{4,12},{5,21},{6,14},{7,23},{8,0},{9,25... | collective-permute-start | bytes 393224 | tf_op jit(solution)/shard_map/ppermute | solution.py:240
  31.1 1.8 %collective-permute-done.8.refs_1_ = f32[256,128]{1,0:T(8,128)S(1)} collective-permute-done((f32[256,128]{1,0:T(8,128)S(1)}, f32[256,128]{1,0:T(8,128)S(1)}, u32[]{:S(2)}, u32[]{:S(2)}) %collective-permute-start.8) | collective-permute-done | bytes 131104 | tf_op jit(solution)/shard_map/ppermute | solution.py:240
  32.9 1.7 %collective-permute-done.10.refs_3_ = f32[256,128]{1,0:T(8,128)S(1)} collective-permute-done((f32[256,128]{1,0:T(8,128)S(1)}, f32[256,128]{1,0:T(8,128)S(1)}, u32[]{:S(2)}, u32[]{:S(2)}) %collective-permute-start.10) | collective-permute-done | bytes 131104 | tf_op jit(solution)/shard_map/ppermute | solution.py:240
  35.7 1.7 %collective-permute-start.15 = (f32[2,80,128]{2,1,0:T(8,128)S(1)}, f32[2,80,128]{2,1,0:T(8,128)S(1)}, u32[]{:S(2)}, u32[]{:S(2)}) collective-permute-start(f32[2,80,128]{2,1,0:T(8,128)S(1)} %get-tuple-element.60), channel_id=1, source_target_pairs={{0,4},{1,5},{2,6},{3,7},{4,0},{5,1},{6,2},{7,3},{8,12},{9,13},{10,... | collective-permute-start | bytes 245768 | tf_op jit(solution)/shard_map/ppermute | solution.py:475
  37.3 1.1 %collective-permute-start.16 = (f32[2,80,128]{2,1,0:T(8,128)S(1)}, f32[2,80,128]{2,1,0:T(8,128)S(1)}, u32[]{:S(2)}, u32[]{:S(2)}) collective-permute-start(f32[2,80,128]{2,1,0:T(8,128)S(1)} %get-tuple-element.61), channel_id=1, source_target_pairs={{0,5},{1,6},{2,7},{3,0},{4,1},{5,2},{6,3},{7,4},{8,13},{9,14},{10,... | collective-permute-start | bytes 245768 | tf_op jit(solution)/shard_map/ppermute | solution.py:475
  38.5 1.4 %collective-permute-start.17 = (f32[2,80,128]{2,1,0:T(8,128)S(1)}, f32[2,80,128]{2,1,0:T(8,128)S(1)}, u32[]{:S(2)}, u32[]{:S(2)}) collective-permute-start(f32[2,80,128]{2,1,0:T(8,128)S(1)} %get-tuple-element.62), channel_id=1, source_target_pairs={{0,3},{1,4},{2,5},{3,6},{4,7},{5,0},{6,1},{7,2},{8,11},{9,12},{10,... | collective-permute-start | bytes 245768 | tf_op jit(solution)/shard_map/ppermute | solution.py:475
  39.8 2.1 %collective-permute-done.11.refs_1_.refs_0_ = f32[2,80,128]{2,1,0:T(8,128)S(1)} collective-permute-done((f32[2,80,128]{2,1,0:T(8,128)S(1)}, f32[2,80,128]{2,1,0:T(8,128)S(1)}, u32[]{:S(2)}, u32[]{:S(2)}) %collective-permute-start.11) | collective-permute-done | bytes 81952 | tf_op jit(solution)/shard_map/ppermute | solution.py:475
  42.0 1.1 %collective-permute-start.14 = (f32[2,80,128]{2,1,0:T(8,128)S(1)}, f32[2,80,128]{2,1,0:T(8,128)S(1)}, u32[]{:S(2)}, u32[]{:S(2)}) collective-permute-start(f32[2,80,128]{2,1,0:T(8,128)S(1)} %get-tuple-element.58.refs_2_), channel_id=1, source_target_pairs={{0,6},{1,7},{2,0},{3,1},{4,2},{5,3},{6,4},{7,5},{8,14},{9,15},{10,... | collective-permute-start | bytes 245768 | tf_op jit(solution)/shard_map/ppermute | solution.py:475
  43.6 3.3 %collective-permute-done.15.refs_4_ = f32[2,80,128]{2,1,0:T(8,128)S(1)} collective-permute-done((f32[2,80,128]{2,1,0:T(8,128)S(1)}, f32[2,80,128]{2,1,0:T(8,128)S(1)}, u32[]{:S(2)}, u32[]{:S(2)}) %collective-permute-start.15) | collective-permute-done | bytes 81952 | tf_op jit(solution)/shard_map/ppermute | solution.py:475
  46.9 3.3 %collective-permute-done.17.refs_6_ = f32[2,80,128]{2,1,0:T(8,128)S(1)} collective-permute-done((f32[2,80,128]{2,1,0:T(8,128)S(1)}, f32[2,80,128]{2,1,0:T(8,128)S(1)}, u32[]{:S(2)}, u32[]{:S(2)}) %collective-permute-start.17) | collective-permute-done | bytes 81952 | tf_op jit(solution)/shard_map/ppermute | solution.py:475
  50.3 1.9 %shard_map.93 = f32[512,128]{1,0:T(8,128)} custom-call(s32[1,8]{1,0:T(1,128)S(1)} %bitcast.16, s32[1,8]{1,0:T(1,128)S(1)} %bitcast.18, f32[2,80,128]{2,1,0:T(8,128)S(1)} %collective-permute-done.11.refs_1_.refs_0_, f32[1,80,128]{2,1,0:T(8,128)S(1)} %collective-permute-done.12.refs_1_, f32[1,80,128]{2,1,0:T(8,128)S(1)} %collective-permute-done.13.refs_2_, ...), custom_call_target="tpu_custom_call" | custom-call | flops 335544320 | bytes 1638400 | tf_op jit(solution)/shard_map/pallas_call | solution.py:463
  (34 shorter events, 3.6 us)
Async XLA Ops:
  1.8 11.3 %copy-start.1 = (f32[64,4,4]{0,2,1:T(4,128)S(1)}, f32[64,4,4]{0,2,1:T(4,128)}, u32[]{:S(2)}) copy-start(f32[64,4,4]{0,2,1:T(4,128)} %param.13) | copy-start | bytes 12292
  1.8 11.3 %copy-start.2 = (s32[512]{0:T(512)S(1)}, s32[512]{0:T(512)}, u32[]{:S(2)}) copy-start(s32[512]{0:T(512)} %param.14) | copy-start | bytes 6148
  1.8 8.2 %collective-permute-start.1 = (f32[1,80,128]{2,1,0:T(8,128)S(1)}, f32[1,80,128]{2,1,0:T(8,128)S(1)}, u32[]{:S(2)}, u32[]{:S(2)}) collective-permute-start(f32[1,80,128]{2,1,0:T(8,128)S(1)} %get-tuple-element.35), channel_id=1, source_target_pairs={{0,1},{1,0},{2,3},{3,2},{4,5},{5,4},{6,7},{7,6},{8,9},{9,8},{10,11... | collective-permute-start | bytes 122888 | tf_op jit(solution)/shard_map/ppermute | solution.py:475
  2.4 13.0 %collective-permute-start = (f32[2,80,128]{2,1,0:T(8,128)S(1)}, f32[2,80,128]{2,1,0:T(8,128)S(1)}, u32[]{:S(2)}, u32[]{:S(2)}) collective-permute-start(f32[2,80,128]{2,1,0:T(8,128)S(1)} %get-tuple-element.34), channel_id=1, source_target_pairs={{0,2},{1,3},{2,4},{3,5},{4,6},{5,7},{6,0},{7,1},{8,10},{9,11},{10,... | collective-permute-start | bytes 245768 | tf_op jit(solution)/shard_map/ppermute | solution.py:475
  5.6 10.6 %collective-permute-start.4 = (f32[2,80,128]{2,1,0:T(8,128)S(1)}, f32[2,80,128]{2,1,0:T(8,128)S(1)}, u32[]{:S(2)}, u32[]{:S(2)}) collective-permute-start(f32[2,80,128]{2,1,0:T(8,128)S(1)} %get-tuple-element.41), channel_id=1, source_target_pairs={{0,4},{1,5},{2,6},{3,7},{4,0},{5,1},{6,2},{7,3},{8,12},{9,13},{10,... | collective-permute-start | bytes 245768 | tf_op jit(solution)/shard_map/ppermute | solution.py:475
  8.3 7.9 %collective-permute-start.5 = (f32[2,80,128]{2,1,0:T(8,128)S(1)}, f32[2,80,128]{2,1,0:T(8,128)S(1)}, u32[]{:S(2)}, u32[]{:S(2)}) collective-permute-start(f32[2,80,128]{2,1,0:T(8,128)S(1)} %get-tuple-element.42), channel_id=1, source_target_pairs={{0,5},{1,6},{2,7},{3,0},{4,1},{5,2},{6,3},{7,4},{8,13},{9,14},{10,... | collective-permute-start | bytes 245768 | tf_op jit(solution)/shard_map/ppermute | solution.py:475
  8.3 11.5 %collective-permute-start.6 = (f32[2,80,128]{2,1,0:T(8,128)S(1)}, f32[2,80,128]{2,1,0:T(8,128)S(1)}, u32[]{:S(2)}, u32[]{:S(2)}) collective-permute-start(f32[2,80,128]{2,1,0:T(8,128)S(1)} %get-tuple-element.43), channel_id=1, source_target_pairs={{0,3},{1,4},{2,5},{3,6},{4,7},{5,0},{6,1},{7,2},{8,11},{9,12},{10,... | collective-permute-start | bytes 245768 | tf_op jit(solution)/shard_map/ppermute | solution.py:475
  10.0 9.7 %collective-permute-start.3 = (f32[2,80,128]{2,1,0:T(8,128)S(1)}, f32[2,80,128]{2,1,0:T(8,128)S(1)}, u32[]{:S(2)}, u32[]{:S(2)}) collective-permute-start(f32[2,80,128]{2,1,0:T(8,128)S(1)} %get-tuple-element.39.refs_2_), channel_id=1, source_target_pairs={{0,6},{1,7},{2,0},{3,1},{4,2},{5,3},{6,4},{7,5},{8,14},{9,15},{10,... | collective-permute-start | bytes 245768 | tf_op jit(solution)/shard_map/ppermute | solution.py:475
  13.2 7.7 %copy-start.3 = (s32[1,1,8]{2,1,0:T(1,128)S(1)}, s32[1,1,8]{2,1,0:T(1,128)}, u32[]{:S(2)}) copy-start(s32[1,1,8]{2,1,0:T(1,128)} %param.11) | copy-start | bytes 100
  13.2 7.7 %copy-start.4 = (s32[1,1,8]{2,1,0:T(1,128)S(1)}, s32[1,1,8]{2,1,0:T(1,128)}, u32[]{:S(2)}) copy-start(s32[1,1,8]{2,1,0:T(1,128)} %param.12) | copy-start | bytes 100
  15.4 5.4 %collective-permute-start.2 = (f32[1,80,128]{2,1,0:T(8,128)S(1)}, f32[1,80,128]{2,1,0:T(8,128)S(1)}, u32[]{:S(2)}, u32[]{:S(2)}) collective-permute-start(f32[1,80,128]{2,1,0:T(8,128)S(1)} %shard_map.85), channel_id=1, source_target_pairs={{0,7},{1,2},{2,1},{3,4},{4,3},{5,6},{6,5},{7,0},{8,15},{9,10},{10,... | collective-permute-start | bytes 122888 | tf_op jit(solution)/shard_map/ppermute | solution.py:475
  22.0 5.8 %collective-permute-start.7 = (f32[256,128]{1,0:T(8,128)S(1)}, f32[256,128]{1,0:T(8,128)S(1)}, u32[]{:S(2)}, u32[]{:S(2)}) collective-permute-start(f32[256,128]{1,0:T(8,128)S(1)} %get-tuple-element.45.own_ref), channel_id=1, source_target_pairs={{0,8},{1,17},{2,10},{3,19},{4,12},{5,21},{6,14},{7,23},{8,0},{9,25... | collective-permute-start | bytes 393224 | tf_op jit(solution)/shard_map/ppermute | solution.py:234
  23.6 6.0 %collective-permute-start.9 = (f32[256,128]{1,0:T(8,128)S(1)}, f32[256,128]{1,0:T(8,128)S(1)}, u32[]{:S(2)}, u32[]{:S(2)}) collective-permute-start(f32[256,128]{1,0:T(8,128)S(1)} %get-tuple-element.49.own_ref), channel_id=1, source_target_pairs={{0,16},{1,9},{2,18},{3,11},{4,20},{5,13},{6,22},{7,15},{8,24},{9,1... | collective-permute-start | bytes 393224 | tf_op jit(solution)/shard_map/ppermute | solution.py:234
  27.9 5.0 %collective-permute-start.8 = (f32[256,128]{1,0:T(8,128)S(1)}, f32[256,128]{1,0:T(8,128)S(1)}, u32[]{:S(2)}, u32[]{:S(2)}) collective-permute-start(f32[256,128]{1,0:T(8,128)S(1)} %get-tuple-element.48), channel_id=1, source_target_pairs={{0,16},{1,9},{2,18},{3,11},{4,20},{5,13},{6,22},{7,15},{8,24},{9,1... | collective-permute-start | bytes 393224 | tf_op jit(solution)/shard_map/ppermute | solution.py:240
  29.6 5.0 %collective-permute-start.10 = (f32[256,128]{1,0:T(8,128)S(1)}, f32[256,128]{1,0:T(8,128)S(1)}, u32[]{:S(2)}, u32[]{:S(2)}) collective-permute-start(f32[256,128]{1,0:T(8,128)S(1)} %get-tuple-element.51), channel_id=1, source_target_pairs={{0,8},{1,17},{2,10},{3,19},{4,12},{5,21},{6,14},{7,23},{8,0},{9,25... | collective-permute-start | bytes 393224 | tf_op jit(solution)/shard_map/ppermute | solution.py:240
  34.6 8.4 %copy-start = (f32[1,1,512,512]{3,2,1,0:T(8,128)S(1)}, f32[1,1,512,512]{3,2,1,0:T(8,128)}, u32[]{:S(2)}) copy-start(f32[1,1,512,512]{3,2,1,0:T(8,128)} %param.8) | copy-start | bytes 3145732
  35.0 7.0 %collective-permute-start.11 = (f32[2,80,128]{2,1,0:T(8,128)S(1)}, f32[2,80,128]{2,1,0:T(8,128)S(1)}, u32[]{:S(2)}, u32[]{:S(2)}) collective-permute-start(f32[2,80,128]{2,1,0:T(8,128)S(1)} %get-tuple-element.53), channel_id=1, source_target_pairs={{0,2},{1,3},{2,4},{3,5},{4,6},{5,7},{6,0},{7,1},{8,10},{9,11},{10,... | collective-permute-start | bytes 245768 | tf_op jit(solution)/shard_map/ppermute | solution.py:475
  35.1 8.5 %collective-permute-start.12 = (f32[1,80,128]{2,1,0:T(8,128)S(1)}, f32[1,80,128]{2,1,0:T(8,128)S(1)}, u32[]{:S(2)}, u32[]{:S(2)}) collective-permute-start(f32[1,80,128]{2,1,0:T(8,128)S(1)} %get-tuple-element.54), channel_id=1, source_target_pairs={{0,1},{1,0},{2,3},{3,2},{4,5},{5,4},{6,7},{7,6},{8,9},{9,8},{10,11... | collective-permute-start | bytes 122888 | tf_op jit(solution)/shard_map/ppermute | solution.py:475
  35.7 11.3 %collective-permute-start.15 = (f32[2,80,128]{2,1,0:T(8,128)S(1)}, f32[2,80,128]{2,1,0:T(8,128)S(1)}, u32[]{:S(2)}, u32[]{:S(2)}) collective-permute-start(f32[2,80,128]{2,1,0:T(8,128)S(1)} %get-tuple-element.60), channel_id=1, source_target_pairs={{0,4},{1,5},{2,6},{3,7},{4,0},{5,1},{6,2},{7,3},{8,12},{9,13},{10,... | collective-permute-start | bytes 245768 | tf_op jit(solution)/shard_map/ppermute | solution.py:475
  37.3 9.6 %collective-permute-start.16 = (f32[2,80,128]{2,1,0:T(8,128)S(1)}, f32[2,80,128]{2,1,0:T(8,128)S(1)}, u32[]{:S(2)}, u32[]{:S(2)}) collective-permute-start(f32[2,80,128]{2,1,0:T(8,128)S(1)} %get-tuple-element.61), channel_id=1, source_target_pairs={{0,5},{1,6},{2,7},{3,0},{4,1},{5,2},{6,3},{7,4},{8,13},{9,14},{10,... | collective-permute-start | bytes 245768 | tf_op jit(solution)/shard_map/ppermute | solution.py:475
  38.5 11.8 %collective-permute-start.17 = (f32[2,80,128]{2,1,0:T(8,128)S(1)}, f32[2,80,128]{2,1,0:T(8,128)S(1)}, u32[]{:S(2)}, u32[]{:S(2)}) collective-permute-start(f32[2,80,128]{2,1,0:T(8,128)S(1)} %get-tuple-element.62), channel_id=1, source_target_pairs={{0,3},{1,4},{2,5},{3,6},{4,7},{5,0},{6,1},{7,2},{8,11},{9,12},{10,... | collective-permute-start | bytes 245768 | tf_op jit(solution)/shard_map/ppermute | solution.py:475
  42.0 8.3 %collective-permute-start.14 = (f32[2,80,128]{2,1,0:T(8,128)S(1)}, f32[2,80,128]{2,1,0:T(8,128)S(1)}, u32[]{:S(2)}, u32[]{:S(2)}) collective-permute-start(f32[2,80,128]{2,1,0:T(8,128)S(1)} %get-tuple-element.58.refs_2_), channel_id=1, source_target_pairs={{0,6},{1,7},{2,0},{3,1},{4,2},{5,3},{6,4},{7,5},{8,14},{9,15},{10,... | collective-permute-start | bytes 245768 | tf_op jit(solution)/shard_map/ppermute | solution.py:475
  43.6 6.7 %collective-permute-start.13 = (f32[1,80,128]{2,1,0:T(8,128)S(1)}, f32[1,80,128]{2,1,0:T(8,128)S(1)}, u32[]{:S(2)}, u32[]{:S(2)}) collective-permute-start(f32[1,80,128]{2,1,0:T(8,128)S(1)} %shard_map.92), channel_id=1, source_target_pairs={{0,7},{1,2},{2,1},{3,4},{4,3},{5,6},{6,5},{7,0},{8,15},{9,10},{10,... | collective-permute-start | bytes 122888 | tf_op jit(solution)/shard_map/ppermute | solution.py:475

commit v11 on v8

--- a/solution.py
+++ b/solution.py
@@ -124,43 +124,37 @@
             out[w] = value
 
 
-def split_rows(right, split_ref):
-    count, rank, size = right.shape
-    rows = count * rank
-    hi, lo = split(right[...].reshape(rows, size))
-    split_ref[:rows] = hi
-    split_ref[rows:] = lo
-
-
-def first_coeff_kernel(messages, others, cols_ref, right_ref, *refs):
+def split_rows(right, slots, split_ref):
+    rank = right.shape[1]
+    rows = len(slots) * rank
+    for at, slot in enumerate(slots):
+        hi, lo = split(right[slot])
+        split_ref[at * rank : (at + 1) * rank] = hi
+        split_ref[rows + at * rank : rows + (at + 1) * rank] = lo
+
+
+def first_coeff_kernel(messages, cols_ref, right_ref, *refs):
     outs, refs = refs[: len(messages)], refs[len(messages) :]
-    split_ref, both_ref, rest_ref, cols, right, cols_sem, sems, rest_sems = refs
+    split_ref, both_ref, cols, right, cols_sem, sems = refs
     cols_copy = pltpu.make_async_copy(cols_ref, cols, cols_sem)
     cols_copy.start()
     copies = copy_runs(slots_of(messages), right_ref, right, sems)
-    rest = copy_runs(slots_of(others), right_ref, rest_ref, rest_sems)
     cols_copy.wait()
     both_ref[...] = side_by_side(cols[...])
     for copy in copies:
         copy.wait()
-    split_rows(right, split_ref)
+    split_rows(right, range(right.shape[0]), split_ref)
     store_coefficients(split_ref, both_ref[...], messages, right.shape[1], outs)
-    for copy in rest:
-        copy.wait()
-
-
-def first_coefficients(cols, right_tile, messages, others):
+
+
+def first_coefficients(cols, right_tile, messages):
     _, rank, size = right_tile.shape
     width = cols.shape[1]
-    count, rest = len(slots_of(messages)), len(slots_of(others))
+    count = len(slots_of(messages))
     outs = [struct(message.width, rank, width) for message in messages]
-    outs += [
-        struct(2 * count * rank, size, dtype=bf16),
-        struct(size, 2 * width, dtype=bf16),
-        struct(rest, rank, size),
-    ]
+    outs += [struct(2 * count * rank, size, dtype=bf16), struct(size, 2 * width, dtype=bf16)]
     got = call(
-        functools.partial(first_coeff_kernel, messages, others),
+        functools.partial(first_coeff_kernel, messages),
         outs,
         [in_vmem] * len(outs),
         [in_hbm, in_hbm],
@@ -169,22 +163,22 @@
             pltpu.VMEM((count, rank, size), f32),
             pltpu.SemaphoreType.DMA,
             pltpu.SemaphoreType.DMA((count,)),
-            pltpu.SemaphoreType.DMA((rest,)),
         ],
         flops=8 * count * rank * size * width,
-        moved=4 * (count + rest) * rank * size,
+        moved=4 * count * rank * size,
     )(to_hbm(cols), to_hbm(right_tile))
-    return got[:-3], got[-3], got[-2], got[-1]
+    return got[:-2], got[-2], got[-1]
 
 
 def rest_coeff_kernel(messages, both_ref, right_ref, *refs):
     outs, split_ref = refs[:-1], refs[-1]
-    split_rows(right_ref, split_ref)
+    split_rows(right_ref, slots_of(messages), split_ref)
     store_coefficients(split_ref, both_ref[...], messages, right_ref.shape[1], outs)
 
 
-def rest_coefficients(both, right, messages):
-    count, rank, size = right.shape
+def rest_coefficients(both, right_tile, messages):
+    _, rank, size = right_tile.shape
+    count = len(slots_of(messages))
     width = both.shape[1] // 2
     outs = [struct(message.width, rank, width) for message in messages]
     outs.append(struct(2 * count * rank, size, dtype=bf16))
@@ -195,7 +189,7 @@
         [in_vmem] * 2,
         flops=8 * count * rank * size * width,
         moved=8 * count * rank * size,
-    )(both, right)
+    )(both, right_tile)
     return got[:-1], got[-1]
 
 
@@ -508,8 +502,8 @@
 
     one, two = message_sets_of(lax.axis_size("tile"), slots)
     messages = one + two
-    coeffs, split_one, both, rest = first_coefficients(cols, right_tile, one, two)
-    more, split_two = rest_coefficients(both, rest, two)
+    coeffs, split_one, both = first_coefficients(cols, right_tile, one)
+    more, split_two = rest_coefficients(both, right_tile, two)
     diag_part, left_split, weights = prepare(diag_tile, cols, left_rows, table, index, halves)
     gots = send_all(one, two, coeffs, more, -1, diag_part)
     first = rows(offsets, ranks, gots, messages, left_split, diag_part, slots, halves, False)

time: 50.4 us -> 50.2 us (level)
  no operation moved by 1% of the time
where the time goes in v11:
time: 50.2 us; the launch traced here: 50 us
  starting transfers between devices  29.5 us (59%)
  waiting for transfers between devices  11.3 us (23%)
  Pallas kernels  9.04 us (18%)
    ppermute x14, starting transfers between devices, send(): return lax.ppermute(value, 'tile', message.pairs)  23.6 us
    ppermute x14, waiting for transfers between devices, send(): return lax.ppermute(value, 'tile', message.pairs)  5.54 us
    ppermute x2, waiting for transfers between devices, mix(): lax.ppermute(send, axes, pairs)  3.47 us
    pallas_call x2, Pallas kernels, rows(): call(functools.partial(row_kernel, messages, halves, final), pltpu.HBM((s...  3.1 us
    ppermute x2, starting transfers between devices, mix(): lax.ppermute(part, axes, pairs)  3.06 us
    ppermute x2, starting transfers between devices, mix(): lax.ppermute(send, axes, pairs)  2.84 us
    ppermute x2, waiting for transfers between devices, mix(): lax.ppermute(part, axes, pairs)  2.26 us
    pallas_call x1, Pallas kernels, prepare(): call(functools.partial(prepare_kernel, halves), [struct(size, width), str...  2.21 us
  transfers between devices with their start and end apart: 18, of which 8 were waited for; matrix products, arithmetic and copies ran while one was open for 0% of the time, Pallas kernels for 8%

profile of v11, /device:TPU:0, one launch (start us, length us, event | category | flops | bytes accessed | tf_op | source)
XLA Modules:
  0.0 50.0 jit_solution(4684604130503977815)
XLA Ops:
  0.0 1.7 %shard_map.82 = (f32[2,80,128]{2,1,0:T(8,128)S(1)}, f32[1,80,128]{2,1,0:T(8,128)S(1)}, f32[1,80,128]{2,1,0:T(8,128)S(1)}, bf16[640,512]{1,0:T(8,128)(2,1)S(1)}, bf16[512,256]{1,0:T(8,128)(2,1)S(1)}) custom-call(f32[512,128]{1,0:T(8,128)} %bitcast.22, f32[12,80,512]{2,1,0:T(8,128)} %bitcast.11), custom_call_target="tpu_custom_call" | custom-call | flops 167772160 | bytes 655360 | tf_op jit(solution)/shard_map/pallas_call | solution.py:156
  2.3 3.7 %collective-permute-start = (f32[2,80,128]{2,1,0:T(8,128)S(1)}, f32[2,80,128]{2,1,0:T(8,128)S(1)}, u32[]{:S(2)}, u32[]{:S(2)}) collective-permute-start(f32[2,80,128]{2,1,0:T(8,128)S(1)} %get-tuple-element.33), channel_id=1, source_target_pairs={{0,4},{1,5},{2,6},{3,7},{4,0},{5,1},{6,2},{7,3},{8,12},{9,13},{10,... | collective-permute-start | bytes 245768 | tf_op jit(solution)/shard_map/ppermute | solution.py:469
  5.9 0.6 %shard_map.83 = (f32[2,80,128]{2,1,0:T(8,128)S(1)}, f32[2,80,128]{2,1,0:T(8,128)S(1)}, f32[2,80,128]{2,1,0:T(8,128)S(1)}, f32[2,80,128]{2,1,0:T(8,128)S(1)}, bf16[1280,512]{1,0:T(8,128)(2,1)S(1)}) custom-call(bf16[512,256]{1,0:T(8,128)(2,1)S(1)} %get-tuple-element.36.both_ref, f32[12,80,512]{2,1,0:T(8,128)S(1)} %bitcast.12), custom_call_target="tpu_custom_call" | custom-call | flops 335544320 | bytes 2621440 | tf_op jit(solution)/shard_map/pallas_call | solution.py:185
  6.6 1.7 %collective-permute-start.5 = (f32[2,80,128]{2,1,0:T(8,128)S(1)}, f32[2,80,128]{2,1,0:T(8,128)S(1)}, u32[]{:S(2)}, u32[]{:S(2)}) collective-permute-start(f32[2,80,128]{2,1,0:T(8,128)S(1)} %get-tuple-element.40), channel_id=1, source_target_pairs={{0,3},{1,4},{2,5},{3,6},{4,7},{5,0},{6,1},{7,2},{8,11},{9,12},{10,... | collective-permute-start | bytes 245768 | tf_op jit(solution)/shard_map/ppermute | solution.py:469
  8.3 3.1 %collective-permute-start.6 = (f32[2,80,128]{2,1,0:T(8,128)S(1)}, f32[2,80,128]{2,1,0:T(8,128)S(1)}, u32[]{:S(2)}, u32[]{:S(2)}) collective-permute-start(f32[2,80,128]{2,1,0:T(8,128)S(1)} %get-tuple-element.41), channel_id=1, source_target_pairs={{0,6},{1,7},{2,0},{3,1},{4,2},{5,3},{6,4},{7,5},{8,14},{9,15},{10,... | collective-permute-start | bytes 245768 | tf_op jit(solution)/shard_map/ppermute | solution.py:469
  11.5 2.2 %shard_map.84 = (f32[512,128]{1,0:T(8,128)S(1)}, bf16[1024,640]{1,0:T(8,128)(2,1)S(1)}, f32[8,256,128]{2,1,0:T(8,128)S(1)}) custom-call(f32[512,512]{1,0:T(8,128)} %bitcast.13, f32[512,128]{1,0:T(8,128)} %bitcast.23, f32[640,512]{1,0:T(8,128)} %bitcast.21, f32[16,64]{1,0:T(8,128)S(1)} %bitcast.15, s32[1,512]{1,0:T(1,128)S(1)} %bitcast.16), custom_call_target="tpu_custom_call" | custom-call | flops 268435456 | bytes 4194304 | tf_op jit(solution)/shard_map/pallas_call | solution.py:380
  13.8 4.6 %collective-permute-start.2 = (f32[1,80,128]{2,1,0:T(8,128)S(1)}, f32[1,80,128]{2,1,0:T(8,128)S(1)}, u32[]{:S(2)}, u32[]{:S(2)}) collective-permute-start(f32[1,80,128]{2,1,0:T(8,128)S(1)} %shard_map.85), channel_id=1, source_target_pairs={{0,7},{1,2},{2,1},{3,4},{4,3},{5,6},{6,5},{7,0},{8,15},{9,10},{10,... | collective-permute-start | bytes 122888 | tf_op jit(solution)/shard_map/ppermute | solution.py:469
  18.5 1.6 %collective-permute-done.2.refs_2_ = f32[1,80,128]{2,1,0:T(8,128)S(1)} collective-permute-done((f32[1,80,128]{2,1,0:T(8,128)S(1)}, f32[1,80,128]{2,1,0:T(8,128)S(1)}, u32[]{:S(2)}, u32[]{:S(2)}) %collective-permute-start.2) | collective-permute-done | bytes 40992 | tf_op jit(solution)/shard_map/ppermute | solution.py:469
  20.1 1.2 %shard_map.86 = (f32[256,128]{1,0:T(8,128)S(1)}, f32[256,128]{1,0:T(8,128)S(1)}) custom-call(s32[1,8]{1,0:T(1,128)S(1)} %bitcast.17, s32[1,8]{1,0:T(1,128)S(1)} %bitcast.19, f32[2,80,128]{2,1,0:T(8,128)S(1)} %collective-permute-done.refs_0_, f32[1,80,128]{2,1,0:T(8,128)S(1)} %collective-permute-done.1.refs_1_, ...), custom_call_target="tpu_custom_call" | custom-call | flops 335544320 | bytes 1638400 | tf_op jit(solution)/shard_map/pallas_call | solution.py:457
  21.3 1.5 %collective-permute-start.7 = (f32[256,128]{1,0:T(8,128)S(1)}, f32[256,128]{1,0:T(8,128)S(1)}, u32[]{:S(2)}, u32[]{:S(2)}) collective-permute-start(f32[256,128]{1,0:T(8,128)S(1)} %get-tuple-element.43.own_ref), channel_id=1, source_target_pairs={{0,8},{1,17},{2,10},{3,19},{4,12},{5,21},{6,14},{7,23},{8,0},{9,25... | collective-permute-start | bytes 393224 | tf_op jit(solution)/shard_map/ppermute | solution.py:228
  22.9 1.5 %collective-permute-start.9 = (f32[256,128]{1,0:T(8,128)S(1)}, f32[256,128]{1,0:T(8,128)S(1)}, u32[]{:S(2)}, u32[]{:S(2)}) collective-permute-start(f32[256,128]{1,0:T(8,128)S(1)} %get-tuple-element.47.own_ref), channel_id=1, source_target_pairs={{0,16},{1,9},{2,18},{3,11},{4,20},{5,13},{6,22},{7,15},{8,24},{9,1... | collective-permute-start | bytes 393224 | tf_op jit(solution)/shard_map/ppermute | solution.py:228
  24.4 2.3 %collective-permute-done.7.got_ref = f32[256,128]{1,0:T(8,128)S(1)} collective-permute-done((f32[256,128]{1,0:T(8,128)S(1)}, f32[256,128]{1,0:T(8,128)S(1)}, u32[]{:S(2)}, u32[]{:S(2)}) %collective-permute-start.7) | collective-permute-done | bytes 131104 | tf_op jit(solution)/shard_map/ppermute | solution.py:228
  26.7 1.3 %collective-permute-start.8 = (f32[256,128]{1,0:T(8,128)S(1)}, f32[256,128]{1,0:T(8,128)S(1)}, u32[]{:S(2)}, u32[]{:S(2)}) collective-permute-start(f32[256,128]{1,0:T(8,128)S(1)} %get-tuple-element.46), channel_id=1, source_target_pairs={{0,16},{1,9},{2,18},{3,11},{4,20},{5,13},{6,22},{7,15},{8,24},{9,1... | collective-permute-start | bytes 393224 | tf_op jit(solution)/shard_map/ppermute | solution.py:234
  28.0 1.6 %collective-permute-start.10 = (f32[256,128]{1,0:T(8,128)S(1)}, f32[256,128]{1,0:T(8,128)S(1)}, u32[]{:S(2)}, u32[]{:S(2)}) collective-permute-start(f32[256,128]{1,0:T(8,128)S(1)} %get-tuple-element.49), channel_id=1, source_target_pairs={{0,8},{1,17},{2,10},{3,19},{4,12},{5,21},{6,14},{7,23},{8,0},{9,25... | collective-permute-start | bytes 393224 | tf_op jit(solution)/shard_map/ppermute | solution.py:234
  29.6 2.1 %collective-permute-done.8.refs_1_ = f32[256,128]{1,0:T(8,128)S(1)} collective-permute-done((f32[256,128]{1,0:T(8,128)S(1)}, f32[256,128]{1,0:T(8,128)S(1)}, u32[]{:S(2)}, u32[]{:S(2)}) %collective-permute-start.8) | collective-permute-done | bytes 131104 | tf_op jit(solution)/shard_map/ppermute | solution.py:234
  31.7 1.3 %collective-permute-done.10.refs_3_ = f32[256,128]{1,0:T(8,128)S(1)} collective-permute-done((f32[256,128]{1,0:T(8,128)S(1)}, f32[256,128]{1,0:T(8,128)S(1)}, u32[]{:S(2)}, u32[]{:S(2)}) %collective-permute-start.10) | collective-permute-done | bytes 131104 | tf_op jit(solution)/shard_map/ppermute | solution.py:234
  33.4 2.6 %collective-permute-start.11 = (f32[2,80,128]{2,1,0:T(8,128)S(1)}, f32[2,80,128]{2,1,0:T(8,128)S(1)}, u32[]{:S(2)}, u32[]{:S(2)}) collective-permute-start(f32[2,80,128]{2,1,0:T(8,128)S(1)} %get-tuple-element.51), channel_id=1, source_target_pairs={{0,4},{1,5},{2,6},{3,7},{4,0},{5,1},{6,2},{7,3},{8,12},{9,13},{10,... | collective-permute-start | bytes 245768 | tf_op jit(solution)/shard_map/ppermute | solution.py:469
  36.5 0.6 %collective-permute-start.15 = (f32[2,80,128]{2,1,0:T(8,128)S(1)}, f32[2,80,128]{2,1,0:T(8,128)S(1)}, u32[]{:S(2)}, u32[]{:S(2)}) collective-permute-start(f32[2,80,128]{2,1,0:T(8,128)S(1)} %get-tuple-element.58), channel_id=1, source_target_pairs={{0,5},{1,6},{2,7},{3,0},{4,1},{5,2},{6,3},{7,4},{8,13},{9,14},{10,... | collective-permute-start | bytes 245768 | tf_op jit(solution)/shard_map/ppermute | solution.py:469
  37.1 1.2 %collective-permute-start.16 = (f32[2,80,128]{2,1,0:T(8,128)S(1)}, f32[2,80,128]{2,1,0:T(8,128)S(1)}, u32[]{:S(2)}, u32[]{:S(2)}) collective-permute-start(f32[2,80,128]{2,1,0:T(8,128)S(1)} %get-tuple-element.59), channel_id=1, source_target_pairs={{0,3},{1,4},{2,5},{3,6},{4,7},{5,0},{6,1},{7,2},{8,11},{9,12},{10,... | collective-permute-start | bytes 245768 | tf_op jit(solution)/shard_map/ppermute | solution.py:469
  38.3 3.0 %collective-permute-start.17 = (f32[2,80,128]{2,1,0:T(8,128)S(1)}, f32[2,80,128]{2,1,0:T(8,128)S(1)}, u32[]{:S(2)}, u32[]{:S(2)}) collective-permute-start(f32[2,80,128]{2,1,0:T(8,128)S(1)} %get-tuple-element.60), channel_id=1, source_target_pairs={{0,6},{1,7},{2,0},{3,1},{4,2},{5,3},{6,4},{7,5},{8,14},{9,15},{10,... | collective-permute-start | bytes 245768 | tf_op jit(solution)/shard_map/ppermute | solution.py:469
  41.8 2.5 %collective-permute-start.13 = (f32[1,80,128]{2,1,0:T(8,128)S(1)}, f32[1,80,128]{2,1,0:T(8,128)S(1)}, u32[]{:S(2)}, u32[]{:S(2)}) collective-permute-start(f32[1,80,128]{2,1,0:T(8,128)S(1)} %shard_map.92), channel_id=1, source_target_pairs={{0,7},{1,2},{2,1},{3,4},{4,3},{5,6},{6,5},{7,0},{8,15},{9,10},{10,... | collective-permute-start | bytes 122888 | tf_op jit(solution)/shard_map/ppermute | solution.py:469
  44.4 1.1 %collective-permute-done.16.refs_5_ = f32[2,80,128]{2,1,0:T(8,128)S(1)} collective-permute-done((f32[2,80,128]{2,1,0:T(8,128)S(1)}, f32[2,80,128]{2,1,0:T(8,128)S(1)}, u32[]{:S(2)}, u32[]{:S(2)}) %collective-permute-start.16) | collective-permute-done | bytes 81952 | tf_op jit(solution)/shard_map/ppermute | solution.py:469
  45.8 2.3 %collective-permute-done.14.refs_3_ = f32[2,80,128]{2,1,0:T(8,128)S(1)} collective-permute-done((f32[2,80,128]{2,1,0:T(8,128)S(1)}, f32[2,80,128]{2,1,0:T(8,128)S(1)}, u32[]{:S(2)}, u32[]{:S(2)}) %collective-permute-start.14) | collective-permute-done | bytes 81952 | tf_op jit(solution)/shard_map/ppermute | solution.py:469
  48.1 1.9 %shard_map.93 = f32[512,128]{1,0:T(8,128)} custom-call(s32[1,8]{1,0:T(1,128)S(1)} %bitcast.18, s32[1,8]{1,0:T(1,128)S(1)} %bitcast.20, f32[2,80,128]{2,1,0:T(8,128)S(1)} %collective-permute-done.11.refs_1_.refs_0_, f32[1,80,128]{2,1,0:T(8,128)S(1)} %collective-permute-done.12.refs_1_, f32[1,80,128]{2,1,0:T(8,128)S(1)} %collective-permute-done.13.refs_2_, ...), custom_call_target="tpu_custom_call" | custom-call | flops 335544320 | bytes 1638400 | tf_op jit(solution)/shard_map/pallas_call | solution.py:457
  (36 shorter events, 2.7 us)
Async XLA Ops:
  0.0 5.9 %copy-start = (f32[1,1,12,80,512]{4,3,2,1,0:T(8,128)S(1)}, f32[1,1,12,80,512]{4,3,2,1,0:T(8,128)}, u32[]{:S(2)}) copy-start(f32[1,1,12,80,512]{4,3,2,1,0:T(8,128)} %param.10) | copy-start | bytes 5898244
  1.7 9.7 %copy-start.2 = (f32[64,4,4]{0,2,1:T(4,128)S(1)}, f32[64,4,4]{0,2,1:T(4,128)}, u32[]{:S(2)}) copy-start(f32[64,4,4]{0,2,1:T(4,128)} %param.13) | copy-start | bytes 12292
  1.7 9.7 %copy-start.3 = (s32[512]{0:T(512)S(1)}, s32[512]{0:T(512)}, u32[]{:S(2)}) copy-start(s32[512]{0:T(512)} %param.14) | copy-start | bytes 6148
  1.8 9.7 %collective-permute-start.1 = (f32[1,80,128]{2,1,0:T(8,128)S(1)}, f32[1,80,128]{2,1,0:T(8,128)S(1)}, u32[]{:S(2)}, u32[]{:S(2)}) collective-permute-start(f32[1,80,128]{2,1,0:T(8,128)S(1)} %get-tuple-element.34), channel_id=1, source_target_pairs={{0,1},{1,0},{2,3},{3,2},{4,5},{5,4},{6,7},{7,6},{8,9},{9,8},{10,11... | collective-permute-start | bytes 122888 | tf_op jit(solution)/shard_map/ppermute | solution.py:469
  2.3 11.5 %collective-permute-start = (f32[2,80,128]{2,1,0:T(8,128)S(1)}, f32[2,80,128]{2,1,0:T(8,128)S(1)}, u32[]{:S(2)}, u32[]{:S(2)}) collective-permute-start(f32[2,80,128]{2,1,0:T(8,128)S(1)} %get-tuple-element.33), channel_id=1, source_target_pairs={{0,4},{1,5},{2,6},{3,7},{4,0},{5,1},{6,2},{7,3},{8,12},{9,13},{10,... | collective-permute-start | bytes 245768 | tf_op jit(solution)/shard_map/ppermute | solution.py:469
  6.5 11.8 %collective-permute-start.4 = (f32[2,80,128]{2,1,0:T(8,128)S(1)}, f32[2,80,128]{2,1,0:T(8,128)S(1)}, u32[]{:S(2)}, u32[]{:S(2)}) collective-permute-start(f32[2,80,128]{2,1,0:T(8,128)S(1)} %get-tuple-element.39), channel_id=1, source_target_pairs={{0,5},{1,6},{2,7},{3,0},{4,1},{5,2},{6,3},{7,4},{8,13},{9,14},{10,... | collective-permute-start | bytes 245768 | tf_op jit(solution)/shard_map/ppermute | solution.py:469
  6.6 11.9 %collective-permute-start.5 = (f32[2,80,128]{2,1,0:T(8,128)S(1)}, f32[2,80,128]{2,1,0:T(8,128)S(1)}, u32[]{:S(2)}, u32[]{:S(2)}) collective-permute-start(f32[2,80,128]{2,1,0:T(8,128)S(1)} %get-tuple-element.40), channel_id=1, source_target_pairs={{0,3},{1,4},{2,5},{3,6},{4,7},{5,0},{6,1},{7,2},{8,11},{9,12},{10,... | collective-permute-start | bytes 245768 | tf_op jit(solution)/shard_map/ppermute | solution.py:469
  8.3 10.2 %collective-permute-start.6 = (f32[2,80,128]{2,1,0:T(8,128)S(1)}, f32[2,80,128]{2,1,0:T(8,128)S(1)}, u32[]{:S(2)}, u32[]{:S(2)}) collective-permute-start(f32[2,80,128]{2,1,0:T(8,128)S(1)} %get-tuple-element.41), channel_id=1, source_target_pairs={{0,6},{1,7},{2,0},{3,1},{4,2},{5,3},{6,4},{7,5},{8,14},{9,15},{10,... | collective-permute-start | bytes 245768 | tf_op jit(solution)/shard_map/ppermute | solution.py:469
  11.5 7.1 %collective-permute-start.3 = (f32[2,80,128]{2,1,0:T(8,128)S(1)}, f32[2,80,128]{2,1,0:T(8,128)S(1)}, u32[]{:S(2)}, u32[]{:S(2)}) collective-permute-start(f32[2,80,128]{2,1,0:T(8,128)S(1)} %get-tuple-element.37.refs_2_), channel_id=1, source_target_pairs={{0,2},{1,3},{2,4},{3,5},{4,6},{5,7},{6,0},{7,1},{8,10},{9,11},{10,... | collective-permute-start | bytes 245768 | tf_op jit(solution)/shard_map/ppermute | solution.py:469
  11.5 8.6 %copy-start.4 = (s32[1,1,8]{2,1,0:T(1,128)S(1)}, s32[1,1,8]{2,1,0:T(1,128)}, u32[]{:S(2)}) copy-start(s32[1,1,8]{2,1,0:T(1,128)} %param.11) | copy-start | bytes 100
  11.5 8.6 %copy-start.5 = (s32[1,1,8]{2,1,0:T(1,128)S(1)}, s32[1,1,8]{2,1,0:T(1,128)}, u32[]{:S(2)}) copy-start(s32[1,1,8]{2,1,0:T(1,128)} %param.12) | copy-start | bytes 100
  13.8 6.4 %collective-permute-start.2 = (f32[1,80,128]{2,1,0:T(8,128)S(1)}, f32[1,80,128]{2,1,0:T(8,128)S(1)}, u32[]{:S(2)}, u32[]{:S(2)}) collective-permute-start(f32[1,80,128]{2,1,0:T(8,128)S(1)} %shard_map.85), channel_id=1, source_target_pairs={{0,7},{1,2},{2,1},{3,4},{4,3},{5,6},{6,5},{7,0},{8,15},{9,10},{10,... | collective-permute-start | bytes 122888 | tf_op jit(solution)/shard_map/ppermute | solution.py:469
  21.3 5.3 %collective-permute-start.7 = (f32[256,128]{1,0:T(8,128)S(1)}, f32[256,128]{1,0:T(8,128)S(1)}, u32[]{:S(2)}, u32[]{:S(2)}) collective-permute-start(f32[256,128]{1,0:T(8,128)S(1)} %get-tuple-element.43.own_ref), channel_id=1, source_target_pairs={{0,8},{1,17},{2,10},{3,19},{4,12},{5,21},{6,14},{7,23},{8,0},{9,25... | collective-permute-start | bytes 393224 | tf_op jit(solution)/shard_map/ppermute | solution.py:228
  22.9 5.1 %collective-permute-start.9 = (f32[256,128]{1,0:T(8,128)S(1)}, f32[256,128]{1,0:T(8,128)S(1)}, u32[]{:S(2)}, u32[]{:S(2)}) collective-permute-start(f32[256,128]{1,0:T(8,128)S(1)} %get-tuple-element.47.own_ref), channel_id=1, source_target_pairs={{0,16},{1,9},{2,18},{3,11},{4,20},{5,13},{6,22},{7,15},{8,24},{9,1... | collective-permute-start | bytes 393224 | tf_op jit(solution)/shard_map/ppermute | solution.py:228
  26.7 5.0 %collective-permute-start.8 = (f32[256,128]{1,0:T(8,128)S(1)}, f32[256,128]{1,0:T(8,128)S(1)}, u32[]{:S(2)}, u32[]{:S(2)}) collective-permute-start(f32[256,128]{1,0:T(8,128)S(1)} %get-tuple-element.46), channel_id=1, source_target_pairs={{0,16},{1,9},{2,18},{3,11},{4,20},{5,13},{6,22},{7,15},{8,24},{9,1... | collective-permute-start | bytes 393224 | tf_op jit(solution)/shard_map/ppermute | solution.py:234
  28.0 5.0 %collective-permute-start.10 = (f32[256,128]{1,0:T(8,128)S(1)}, f32[256,128]{1,0:T(8,128)S(1)}, u32[]{:S(2)}, u32[]{:S(2)}) collective-permute-start(f32[256,128]{1,0:T(8,128)S(1)} %get-tuple-element.49), channel_id=1, source_target_pairs={{0,8},{1,17},{2,10},{3,19},{4,12},{5,21},{6,14},{7,23},{8,0},{9,25... | collective-permute-start | bytes 393224 | tf_op jit(solution)/shard_map/ppermute | solution.py:234
  33.1 8.3 %copy-start.1 = (f32[1,1,512,512]{3,2,1,0:T(8,128)S(1)}, f32[1,1,512,512]{3,2,1,0:T(8,128)}, u32[]{:S(2)}) copy-start(f32[1,1,512,512]{3,2,1,0:T(8,128)} %param.8) | copy-start | bytes 3145732
  33.4 7.9 %collective-permute-start.11 = (f32[2,80,128]{2,1,0:T(8,128)S(1)}, f32[2,80,128]{2,1,0:T(8,128)S(1)}, u32[]{:S(2)}, u32[]{:S(2)}) collective-permute-start(f32[2,80,128]{2,1,0:T(8,128)S(1)} %get-tuple-element.51), channel_id=1, source_target_pairs={{0,4},{1,5},{2,6},{3,7},{4,0},{5,1},{6,2},{7,3},{8,12},{9,13},{10,... | collective-permute-start | bytes 245768 | tf_op jit(solution)/shard_map/ppermute | solution.py:469
  36.0 5.8 %collective-permute-start.12 = (f32[1,80,128]{2,1,0:T(8,128)S(1)}, f32[1,80,128]{2,1,0:T(8,128)S(1)}, u32[]{:S(2)}, u32[]{:S(2)}) collective-permute-start(f32[1,80,128]{2,1,0:T(8,128)S(1)} %get-tuple-element.52), channel_id=1, source_target_pairs={{0,1},{1,0},{2,3},{3,2},{4,5},{5,4},{6,7},{7,6},{8,9},{9,8},{10,11... | collective-permute-start | bytes 122888 | tf_op jit(solution)/shard_map/ppermute | solution.py:469
  36.5 7.8 %collective-permute-start.15 = (f32[2,80,128]{2,1,0:T(8,128)S(1)}, f32[2,80,128]{2,1,0:T(8,128)S(1)}, u32[]{:S(2)}, u32[]{:S(2)}) collective-permute-start(f32[2,80,128]{2,1,0:T(8,128)S(1)} %get-tuple-element.58), channel_id=1, source_target_pairs={{0,5},{1,6},{2,7},{3,0},{4,1},{5,2},{6,3},{7,4},{8,13},{9,14},{10,... | collective-permute-start | bytes 245768 | tf_op jit(solution)/shard_map/ppermute | solution.py:469
  37.1 8.3 %collective-permute-start.16 = (f32[2,80,128]{2,1,0:T(8,128)S(1)}, f32[2,80,128]{2,1,0:T(8,128)S(1)}, u32[]{:S(2)}, u32[]{:S(2)}) collective-permute-start(f32[2,80,128]{2,1,0:T(8,128)S(1)} %get-tuple-element.59), channel_id=1, source_target_pairs={{0,3},{1,4},{2,5},{3,6},{4,7},{5,0},{6,1},{7,2},{8,11},{9,12},{10,... | collective-permute-start | bytes 245768 | tf_op jit(solution)/shard_map/ppermute | solution.py:469
  38.3 7.5 %collective-permute-start.17 = (f32[2,80,128]{2,1,0:T(8,128)S(1)}, f32[2,80,128]{2,1,0:T(8,128)S(1)}, u32[]{:S(2)}, u32[]{:S(2)}) collective-permute-start(f32[2,80,128]{2,1,0:T(8,128)S(1)} %get-tuple-element.60), channel_id=1, source_target_pairs={{0,6},{1,7},{2,0},{3,1},{4,2},{5,3},{6,4},{7,5},{8,14},{9,15},{10,... | collective-permute-start | bytes 245768 | tf_op jit(solution)/shard_map/ppermute | solution.py:469
  41.3 6.8 %collective-permute-start.14 = (f32[2,80,128]{2,1,0:T(8,128)S(1)}, f32[2,80,128]{2,1,0:T(8,128)S(1)}, u32[]{:S(2)}, u32[]{:S(2)}) collective-permute-start(f32[2,80,128]{2,1,0:T(8,128)S(1)} %get-tuple-element.56.refs_2_), channel_id=1, source_target_pairs={{0,2},{1,3},{2,4},{3,5},{4,6},{5,7},{6,0},{7,1},{8,10},{9,11},{10,... | collective-permute-start | bytes 245768 | tf_op jit(solution)/shard_map/ppermute | solution.py:469
  41.8 6.3 %collective-permute-start.13 = (f32[1,80,128]{2,1,0:T(8,128)S(1)}, f32[1,80,128]{2,1,0:T(8,128)S(1)}, u32[]{:S(2)}, u32[]{:S(2)}) collective-permute-start(f32[1,80,128]{2,1,0:T(8,128)S(1)} %shard_map.92), channel_id=1, source_target_pairs={{0,7},{1,2},{2,1},{3,4},{4,3},{5,6},{6,5},{7,0},{8,15},{9,10},{10,... | collective-permute-start | bytes 122888 | tf_op jit(solution)/shard_map/ppermute | solution.py:469
